TPU v7x, 32 devices: a whole 2x2x4 slice. The times are simulated.
32 devices in a mesh: fsdp: 8 (over y, x, core), ctx: 4 (over z).
Axes of the slice: x: 2, y: 2, z: 4, core: 2. Of those that a mesh axis runs over, the one named last changes fastest.
Arguments:
- tokens: bfloat16 [16384, 1024], P(('fsdp', 'ctx')), may hold values from -6 to 6
- value_first: bfloat16 [16384, 1024], P(('fsdp', 'ctx')), may hold values from -6 to 6
- lengths: int32 [8, 4], P('fsdp'), may hold values from 64 to 1792, as said below
- w_query: float32 [1024, 1024], P('fsdp', 'ctx'), may hold values from -0.1875 to 0.1875
- w_key: float32 [1024, 1024], P('fsdp', 'ctx'), may hold values from -0.1875 to 0.1875
- w_value: float32 [1024, 1024], P('fsdp', 'ctx'), may hold values from -0.1875 to 0.1875
- w_out: float32 [1024, 1024], P('fsdp', 'ctx'), may hold values from -0.75 to 0.75
- w_gate: float32 [1024, 2816], P('fsdp', 'ctx'), may hold values from -0.1875 to 0.1875
- w_up: float32 [1024, 2816], P('fsdp', 'ctx'), may hold values from -0.1875 to 0.1875
- w_down: float32 [2816, 1024], P('fsdp', 'ctx'), may hold values from -0.109375 to 0.109375
- gain_attn: float32 [1024], P('fsdp'), may hold values from 0.5 to 1.5
- gain_ffn: float32 [1024], P('fsdp'), may hold values from 0.5 to 1.5
- out_grad: bfloat16 [16384, 1024], P(('fsdp', 'ctx')), may hold values from -6 to 6
- value_grad: float32 [16384, 1024], P(('fsdp', 'ctx')), may hold values from -6 to 6
Outputs:
- output: bfloat16 [16384, 1024], P(('fsdp', 'ctx'))
- input_grad: float32 [16384, 1024], P(('fsdp', 'ctx'))
- value_first_grad: float32 [16384, 1024], P(('fsdp', 'ctx'))
- grad_query: float32 [1024, 1024], P('fsdp', 'ctx')
- grad_key: float32 [1024, 1024], P('fsdp', 'ctx')
- grad_value: float32 [1024, 1024], P('fsdp', 'ctx')
- grad_out: float32 [1024, 1024], P('fsdp', 'ctx')
- grad_gate: float32 [1024, 2816], P('fsdp', 'ctx')
- grad_up: float32 [1024, 2816], P('fsdp', 'ctx')
- grad_down: float32 [2816, 1024], P('fsdp', 'ctx')
- grad_gain_attn: float32 [1024], P('fsdp')
- grad_gain_ffn: float32 [1024], P('fsdp')
Inputs may be any that keep to these rules, and one draw needn't show every extreme that they name: `lengths`: row f sums to 2048; exactly one entry of each row is 1792, the others are short.
All inputs are finite; a program needn't handle non-finite values.
Results may differ from a plain program's by a relative error of at most 0.022.
Values may be sent and summed in bfloat16 or wider, within the bound.
A program may use at most 256 MiB of HBM per device.

v0:
```python
import math

import jax
import jax.numpy as jnp
from jax import lax
from jax.sharding import PartitionSpec as P

HEAD = 64
TOK_DEV = 512


EPSILON = 1e-05
THETA = 10000.0
NEGATIVE = -1e30


def normalize(vector, gain_vector):
    return (
        vector
        * lax.rsqrt(jnp.mean(vector * vector, axis=-1, keepdims=True) + EPSILON)
        * gain_vector
    )


def rotary(positions):
    half_size = HEAD // 2
    frequency = jnp.exp(jnp.arange(half_size).astype(jnp.float32) * (-2.0 * math.log(THETA) / HEAD))
    angles = positions.astype(jnp.float32)[:, None] * frequency[None, :]
    return (jnp.cos(angles), jnp.sin(angles))


def rotate(vector, cosine_table, sine_table):
    half_size = vector.shape[-1] // 2
    first_half = vector[..., :half_size]
    second_half = vector[..., half_size:]
    cosine_part = cosine_table[:, None, :]
    sine_part = sine_table[:, None, :]
    return jnp.concatenate(
        [
            first_half * cosine_part - second_half * sine_part,
            first_half * sine_part + second_half * cosine_part,
        ],
        axis=-1,
    )


def documents(length_row, places):
    doc_ends = jnp.cumsum(length_row)
    doc_starts = doc_ends - length_row
    owner_ids = jnp.sum((places[:, None] >= doc_ends[None, :]).astype(jnp.int32), axis=1)
    chosen = owner_ids[:, None] == jnp.arange(length_row.shape[0], dtype=jnp.int32)[None, :]
    first_place = jnp.sum(jnp.where(chosen, doc_starts[None, :], 0), axis=1)
    return (owner_ids, places - first_place)


def product(left, right):
    return jnp.dot(left, right, preferred_element_type=jnp.float32)


def contract_last(left, right):
    return lax.dot_general(
        left, right, (((1,), (1,)), ((), ())), preferred_element_type=jnp.float32
    )


def contract_first(left, right):
    return lax.dot_general(
        left, right, (((0,), (0,)), ((), ())), preferred_element_type=jnp.float32
    )


def over_blocks(carried, portion, visit):
    row_count = portion[0].shape[0]
    block_rows = TOK_DEV

    def advance(state_now, number):
        first_row = number * block_rows
        key_block = lax.dynamic_slice_in_dim(portion[0], first_row, block_rows, 0)
        value_block = lax.dynamic_slice_in_dim(portion[1], first_row, block_rows, 0)
        return (visit(state_now, key_block, value_block, first_row), None)

    carried, unused = lax.scan(
        advance, carried, jnp.arange(row_count // block_rows, dtype=jnp.int32)
    )
    return carried


def per_device(
    tokens,
    value_first,
    lengths,
    w_query,
    w_key,
    w_value,
    w_out,
    w_gate,
    w_up,
    w_down,
    gain_attn,
    gain_ffn,
    out_grad,
    value_grad,
):
    halves = (
        w_query.astype(jnp.bfloat16),
        w_key.astype(jnp.bfloat16),
        w_value.astype(jnp.bfloat16),
        w_out.astype(jnp.bfloat16),
        w_gate.astype(jnp.bfloat16),
        w_up.astype(jnp.bfloat16),
        w_down.astype(jnp.bfloat16),
        gain_attn.astype(jnp.bfloat16),
        gain_ffn.astype(jnp.bfloat16),
    )
    rows_part = (
        lax.all_gather(halves[0], "fsdp", axis=0, tiled=True),
        lax.all_gather(halves[1], "fsdp", axis=0, tiled=True),
        lax.all_gather(halves[2], "fsdp", axis=0, tiled=True),
        lax.all_gather(halves[3], "fsdp", axis=0, tiled=True),
        lax.all_gather(halves[4], "fsdp", axis=0, tiled=True),
        lax.all_gather(halves[5], "fsdp", axis=0, tiled=True),
        lax.all_gather(halves[6], "fsdp", axis=0, tiled=True),
        lax.all_gather(halves[7], "fsdp", axis=0, tiled=True),
        lax.all_gather(halves[8], "fsdp", axis=0, tiled=True),
    )
    weights = (
        lax.all_gather(rows_part[0], "ctx", axis=1, tiled=True),
        lax.all_gather(rows_part[1], "ctx", axis=1, tiled=True),
        lax.all_gather(rows_part[2], "ctx", axis=1, tiled=True),
        lax.all_gather(rows_part[3], "ctx", axis=1, tiled=True),
        lax.all_gather(rows_part[4], "ctx", axis=1, tiled=True),
        lax.all_gather(rows_part[5], "ctx", axis=1, tiled=True),
        lax.all_gather(rows_part[6], "ctx", axis=1, tiled=True),
    )
    gain_one = rows_part[7].astype(jnp.float32)
    gain_two = rows_part[8].astype(jnp.float32)
    token_count = tokens.shape[0]
    model_width = tokens.shape[1]
    head_count = model_width // HEAD
    ctx_count = lax.axis_size("ctx")
    my_first = lax.axis_index("ctx") * token_count
    my_last = my_first + token_count - 1
    length_row = lengths[0]
    my_places = my_first + jnp.arange(token_count, dtype=jnp.int32)
    my_owner, my_positions = documents(length_row, my_places)
    cosine_table, sine_table = rotary(my_positions)
    scale_factor = 1.0 / math.sqrt(HEAD)
    anchor = jnp.zeros((), jnp.int32)
    inputs = tokens.astype(jnp.float32)
    hidden_one = normalize(inputs, gain_one).astype(jnp.bfloat16)
    raw_query = product(hidden_one, weights[0])
    raw_key = product(hidden_one, weights[1])
    raw_value = product(hidden_one, weights[2])
    queries = rotate(
        raw_query.reshape(token_count, head_count, HEAD), cosine_table, sine_table
    ).astype(jnp.bfloat16)
    key_flat = (
        rotate(raw_key.reshape(token_count, head_count, HEAD), cosine_table, sine_table)
        .reshape(token_count, model_width)
        .astype(jnp.bfloat16)
    )
    mixed_flat = (0.5 * raw_value + 0.5 * value_first.astype(jnp.float32)).astype(jnp.bfloat16)

    def block_mask(offset, block_rows):
        places = offset + jnp.arange(block_rows, dtype=jnp.int32)
        owner_ids, unused = documents(length_row, places)
        return (owner_ids[None, :] == my_owner[:, None]) & (places[None, :] <= my_places[:, None])

    def forward_visit(state_now, key_block, value_block, offset):
        block_rows = key_block.shape[0]
        key_heads = key_block.reshape(block_rows, head_count, HEAD)
        value_heads = value_block.reshape(block_rows, head_count, HEAD)

        def forward_compute(current):
            running_max, running_total, running_sum = current
            scores = (
                jnp.einsum("qhd,khd->hqk", queries, key_heads, preferred_element_type=jnp.float32)
                * scale_factor
            )
            scores = jnp.where(block_mask(offset, block_rows)[None, :, :], scores, -jnp.inf)
            new_max = jnp.maximum(running_max, jnp.max(scores, axis=-1))
            shrink = jnp.exp(running_max - new_max)
            exponent_terms = jnp.exp(scores - new_max[..., None])
            new_total = running_total * shrink + jnp.sum(exponent_terms, axis=-1)
            new_sum = running_sum * shrink[..., None] + jnp.einsum(
                "hqk,khd->hqd",
                exponent_terms.astype(jnp.bfloat16),
                value_heads,
                preferred_element_type=jnp.float32,
            )
            return (new_max, new_total, new_sum)

        return lax.cond(offset <= my_last, forward_compute, lambda current: current, state_now)

    start_state = (
        jnp.full((head_count, token_count), NEGATIVE, jnp.float32),
        jnp.zeros((head_count, token_count), jnp.float32),
        jnp.zeros((head_count, token_count, HEAD), jnp.float32),
    )
    final_max, final_total, final_sum = over_blocks(
        start_state,
        (
            lax.all_gather(key_flat, "ctx", axis=0, tiled=True),
            lax.all_gather(mixed_flat, "ctx", axis=0, tiled=True),
        ),
        forward_visit,
    )
    attended = final_sum / final_total[..., None]
    log_total = final_max + jnp.log(final_total)
    attended_low = (
        jnp.transpose(attended, (1, 0, 2)).reshape(token_count, model_width).astype(jnp.bfloat16)
    )
    middle = inputs + product(attended_low, weights[3])
    hidden_two = normalize(middle, gain_two).astype(jnp.bfloat16)
    gate_rows = product(hidden_two, weights[4])
    up_rows = product(hidden_two, weights[5])
    sigmoid_gate = jax.nn.sigmoid(gate_rows)
    silu_gate = gate_rows * sigmoid_gate
    activation = (silu_gate * up_rows).astype(jnp.bfloat16)
    output = (middle + product(activation, weights[6])).astype(jnp.bfloat16)
    rows_again = (
        lax.all_gather(halves[0], "fsdp", axis=0, tiled=True),
        lax.all_gather(halves[1], "fsdp", axis=0, tiled=True),
        lax.all_gather(halves[2], "fsdp", axis=0, tiled=True),
        lax.all_gather(halves[3], "fsdp", axis=0, tiled=True),
        lax.all_gather(halves[4], "fsdp", axis=0, tiled=True),
        lax.all_gather(halves[5], "fsdp", axis=0, tiled=True),
        lax.all_gather(halves[6], "fsdp", axis=0, tiled=True),
        lax.all_gather(halves[7], "fsdp", axis=0, tiled=True),
        lax.all_gather(halves[8], "fsdp", axis=0, tiled=True),
    )
    back_weights = (
        lax.all_gather(rows_again[0], "ctx", axis=1, tiled=True),
        lax.all_gather(rows_again[1], "ctx", axis=1, tiled=True),
        lax.all_gather(rows_again[2], "ctx", axis=1, tiled=True),
        lax.all_gather(rows_again[3], "ctx", axis=1, tiled=True),
        lax.all_gather(rows_again[4], "ctx", axis=1, tiled=True),
        lax.all_gather(rows_again[5], "ctx", axis=1, tiled=True),
        lax.all_gather(rows_again[6], "ctx", axis=1, tiled=True),
    )
    back_gain_one = rows_again[7].astype(jnp.float32)
    back_gain_two = rows_again[8].astype(jnp.float32)
    grad_wdown = contract_first(activation, out_grad)
    grad_activation = (
        contract_last(out_grad, back_weights[6]).astype(jnp.bfloat16).astype(jnp.float32)
    )
    silu_slope = sigmoid_gate * (1.0 + gate_rows * (1.0 - sigmoid_gate))
    grad_gate_rows = (grad_activation * up_rows * silu_slope).astype(jnp.bfloat16)
    grad_up_rows = (grad_activation * silu_gate).astype(jnp.bfloat16)
    grad_wgate = contract_first(hidden_two, grad_gate_rows)
    grad_wup = contract_first(hidden_two, grad_up_rows)
    grad_hidden_two = contract_last(grad_gate_rows, back_weights[4]) + contract_last(
        grad_up_rows, back_weights[5]
    )
    unused, pull_two = jax.vjp(normalize, middle, back_gain_two)
    grad_middle_norm, grad_gain_two = pull_two(grad_hidden_two)
    grad_middle = out_grad.astype(jnp.float32) + grad_middle_norm
    grad_branch = grad_middle.astype(jnp.bfloat16)
    grad_wout = contract_first(attended_low, grad_branch)
    grad_attended = contract_last(grad_branch, back_weights[3]).astype(jnp.bfloat16)
    grad_heads = jnp.transpose(grad_attended.reshape(token_count, head_count, HEAD), (1, 0, 2))
    row_dots = jnp.sum(grad_heads.astype(jnp.float32) * attended, axis=-1)

    def backward_visit(state_now, key_block, value_block, offset):
        block_rows = key_block.shape[0]
        key_heads = key_block.reshape(block_rows, head_count, HEAD)
        value_heads = value_block.reshape(block_rows, head_count, HEAD)

        def backward_compute(current):
            grad_queries = current[0]
            scores = (
                jnp.einsum("qhd,khd->hqk", queries, key_heads, preferred_element_type=jnp.float32)
                * scale_factor
            )
            allowed = block_mask(offset, block_rows)[None, :, :]
            probabilities = jnp.where(allowed, jnp.exp(scores - log_total[..., None]), 0.0)
            grad_probs = jnp.einsum(
                "hqd,khd->hqk", grad_heads, value_heads, preferred_element_type=jnp.float32
            )
            grad_scores = (probabilities * (grad_probs - row_dots[..., None])).astype(jnp.bfloat16)
            grad_queries = grad_queries + scale_factor * jnp.einsum(
                "hqk,khd->hqd", grad_scores, key_heads, preferred_element_type=jnp.float32
            )
            key_grads = current[1]
            block_keys = scale_factor * jnp.einsum(
                "hqk,qhd->khd", grad_scores, queries, preferred_element_type=jnp.float32
            )
            block_values = jnp.einsum(
                "hqk,hqd->khd",
                probabilities.astype(jnp.bfloat16),
                grad_heads,
                preferred_element_type=jnp.float32,
            )
            stacked = jnp.stack(
                [
                    block_keys.reshape(block_rows, model_width),
                    block_values.reshape(block_rows, model_width),
                ]
            )
            current_rows = lax.dynamic_slice(
                key_grads, (anchor, offset, anchor), (2, block_rows, model_width)
            )
            key_grads = lax.dynamic_update_slice(
                key_grads, current_rows + stacked, (anchor, offset, anchor)
            )
            return (grad_queries, key_grads)

        return lax.cond(offset <= my_last, backward_compute, lambda current: current, state_now)

    query_zeros = jnp.zeros((head_count, token_count, HEAD), jnp.float32)
    back_state = (query_zeros, jnp.zeros((2, ctx_count * token_count, model_width), jnp.float32))
    folded = over_blocks(
        back_state,
        (
            lax.all_gather(key_flat, "ctx", axis=0, tiled=True),
            lax.all_gather(mixed_flat, "ctx", axis=0, tiled=True),
        ),
        backward_visit,
    )
    grad_query_heads = folded[0]
    own_grads = lax.psum_scatter(
        folded[1].astype(jnp.bfloat16), "ctx", scatter_dimension=1, tiled=True
    ).astype(jnp.float32)
    grad_query_rows = (
        rotate(jnp.transpose(grad_query_heads, (1, 0, 2)), cosine_table, -sine_table)
        .reshape(token_count, model_width)
        .astype(jnp.bfloat16)
    )
    grad_key_rows = (
        rotate(own_grads[0].reshape(token_count, head_count, HEAD), cosine_table, -sine_table)
        .reshape(token_count, model_width)
        .astype(jnp.bfloat16)
    )
    grad_value_rows = (0.5 * own_grads[1]).astype(jnp.bfloat16)
    value_first_grad = value_grad + 0.5 * own_grads[1]
    grad_wquery = contract_first(hidden_one, grad_query_rows)
    grad_wkey = contract_first(hidden_one, grad_key_rows)
    grad_wvalue = contract_first(hidden_one, grad_value_rows)
    grad_hidden_one = (
        contract_last(grad_query_rows, back_weights[0])
        + contract_last(grad_key_rows, back_weights[1])
        + contract_last(grad_value_rows, back_weights[2])
    )
    unused_one, pull_one = jax.vjp(normalize, inputs, back_gain_one)
    grad_inputs_norm, grad_gain_one = pull_one(grad_hidden_one)
    input_grad = grad_middle + grad_inputs_norm
    local_grads = (grad_wquery, grad_wkey, grad_wvalue, grad_wout, grad_wgate, grad_wup, grad_wdown)
    summed_rows = (
        lax.psum_scatter(
            local_grads[0].astype(jnp.bfloat16), "fsdp", scatter_dimension=0, tiled=True
        ).astype(jnp.float32),
        lax.psum_scatter(
            local_grads[1].astype(jnp.bfloat16), "fsdp", scatter_dimension=0, tiled=True
        ).astype(jnp.float32),
        lax.psum_scatter(
            local_grads[2].astype(jnp.bfloat16), "fsdp", scatter_dimension=0, tiled=True
        ).astype(jnp.float32),
        lax.psum_scatter(
            local_grads[3].astype(jnp.bfloat16), "fsdp", scatter_dimension=0, tiled=True
        ).astype(jnp.float32),
        lax.psum_scatter(
            local_grads[4].astype(jnp.bfloat16), "fsdp", scatter_dimension=0, tiled=True
        ).astype(jnp.float32),
        lax.psum_scatter(
            local_grads[5].astype(jnp.bfloat16), "fsdp", scatter_dimension=0, tiled=True
        ).astype(jnp.float32),
        lax.psum_scatter(
            local_grads[6].astype(jnp.bfloat16), "fsdp", scatter_dimension=0, tiled=True
        ).astype(jnp.float32),
        lax.psum_scatter(
            grad_gain_one.astype(jnp.bfloat16), "fsdp", scatter_dimension=0, tiled=True
        ).astype(jnp.float32),
        lax.psum_scatter(
            grad_gain_two.astype(jnp.bfloat16), "fsdp", scatter_dimension=0, tiled=True
        ).astype(jnp.float32),
    )
    matrices = (
        lax.psum_scatter(
            summed_rows[0].astype(jnp.bfloat16), "ctx", scatter_dimension=1, tiled=True
        ).astype(jnp.float32),
        lax.psum_scatter(
            summed_rows[1].astype(jnp.bfloat16), "ctx", scatter_dimension=1, tiled=True
        ).astype(jnp.float32),
        lax.psum_scatter(
            summed_rows[2].astype(jnp.bfloat16), "ctx", scatter_dimension=1, tiled=True
        ).astype(jnp.float32),
        lax.psum_scatter(
            summed_rows[3].astype(jnp.bfloat16), "ctx", scatter_dimension=1, tiled=True
        ).astype(jnp.float32),
        lax.psum_scatter(
            summed_rows[4].astype(jnp.bfloat16), "ctx", scatter_dimension=1, tiled=True
        ).astype(jnp.float32),
        lax.psum_scatter(
            summed_rows[5].astype(jnp.bfloat16), "ctx", scatter_dimension=1, tiled=True
        ).astype(jnp.float32),
        lax.psum_scatter(
            summed_rows[6].astype(jnp.bfloat16), "ctx", scatter_dimension=1, tiled=True
        ).astype(jnp.float32),
    )
    gain_parts = lax.psum((summed_rows[7], summed_rows[8]), "ctx")
    return (
        output,
        input_grad,
        value_first_grad,
        matrices[0],
        matrices[1],
        matrices[2],
        matrices[3],
        matrices[4],
        matrices[5],
        matrices[6],
        gain_parts[0],
        gain_parts[1],
    )


def solution(mesh):
    return jax.shard_map(
        per_device,
        mesh=mesh,
        in_specs=(
            P(("fsdp", "ctx"), None),
            P(("fsdp", "ctx"), None),
            P("fsdp", None),
            P("fsdp", "ctx"),
            P("fsdp", "ctx"),
            P("fsdp", "ctx"),
            P("fsdp", "ctx"),
            P("fsdp", "ctx"),
            P("fsdp", "ctx"),
            P("fsdp", "ctx"),
            P("fsdp"),
            P("fsdp"),
            P(("fsdp", "ctx"), None),
            P(("fsdp", "ctx"), None),
        ),
        out_specs=(
            P(("fsdp", "ctx"), None),
            P(("fsdp", "ctx"), None),
            P(("fsdp", "ctx"), None),
            P("fsdp", "ctx"),
            P("fsdp", "ctx"),
            P("fsdp", "ctx"),
            P("fsdp", "ctx"),
            P("fsdp", "ctx"),
            P("fsdp", "ctx"),
            P("fsdp", "ctx"),
            P("fsdp"),
            P("fsdp"),
        ),
        check_vma=False,
    )
```

profile of v0, /device:TPU:0, one launch (start us, length us, event | category | flops | bytes accessed | tf_op | source)
XLA Modules:
  0.0 1556.2 jit_solution(15316788648211868541)
XLA Ops:
  8.2 12.5 all_gather.78
  21.8 10.7 all_gather.76
  32.6 10.1 all_gather.73
  45.1 8.6 all-gather
  54.1 13.4 all-gather.21.cloned.1.call-done
  67.4 3.9 multiply_convert_fusion.2
  72.7 40.8 %all-gather.19.cloned.1.call-done = bf16[1024,1024]{1,0:T(8,128)(2,1)} async-done(((bf16[1024,256]{1,0:T(8,128)(2,1)}), bf16[1024,1024]{1,0:T(8,128)(2,1)}) %all-gather.19.cloned.1.call-update) | async-done | bytes 2097168 | tf_op jit(solution)/shard_map/all_gather | solution.py:127
  116.5 43.1 %all-gather.15.cloned.1.call-done = bf16[1024,1024]{1,0:T(8,128)(2,1)} async-done(((bf16[1024,256]{1,0:T(8,128)(2,1)}), bf16[1024,1024]{1,0:T(8,128)(2,1)}) %all-gather.15.cloned.1.call-update) | async-done | bytes 2097168 | tf_op jit(solution)/shard_map/all_gather | solution.py:128
  165.4 11.4 all_gather.81
  176.8 9.5 all-gather.35.cloned.1.call-done
  186.4 27.6 %all-gather.27.cloned.1.call-done = bf16[1024,704]{0,1:T(8,128)(2,1)} async-done(((bf16[128,704]{0,1:T(8,128)(2,1)}), bf16[1024,704]{0,1:T(8,128)(2,1)}) %all-gather.27.cloned.1.call-update) | async-done | bytes 1441808 | tf_op jit(solution)/shard_map/all_gather | solution.py:120
  214.0 27.6 %all-gather.31.cloned.1.call-done = bf16[1024,704]{0,1:T(8,128)(2,1)} async-done(((bf16[128,704]{0,1:T(8,128)(2,1)}), bf16[1024,704]{0,1:T(8,128)(2,1)}) %all-gather.31.cloned.1.call-update) | async-done | bytes 1441808 | tf_op jit(solution)/shard_map/all_gather | solution.py:121
  241.7 9.2 all-gather.1
  251.0 73.5 %all-gather.23.cloned.1.call-done = bf16[2048,1024]{1,0:T(8,128)(2,1)} async-done(((bf16[512,1024]{1,0:T(8,128)(2,1)}), bf16[2048,1024]{1,0:T(8,128)(2,1)}) %all-gather.23.cloned.1.call-update) | async-done | bytes 4194320 | tf_op jit(solution)/shard_map/all_gather | solution.py:204
  324.6 6.5 copy.74
  331.1 74.9 %all-gather.17.cloned.1.call-done = bf16[2048,1024]{0,1:T(8,128)(2,1)} async-done(((bf16[512,1024]{0,1:T(8,128)(2,1)}), bf16[2048,1024]{0,1:T(8,128)(2,1)}) %all-gather.17.cloned.1.call-update) | async-done | bytes 4194320 | tf_op jit(solution)/shard_map/all_gather | solution.py:203
  407.6 35.5 %while.28 = (s32[]{:T(128)}, f32[16,512]{1,0:T(8,128)S(1)}, f32[16,512]{1,0:T(8,128)S(1)}, f32[16,512,64]{1,2,0:T(8,128)}, s32[4]{0:T(128)S(1)}, /*index=5*/s32[...) while((s32[]{:T(128)}, f32[16,512]{1,0:T(8,128)S(1)}, ...), condition=%wide.region_11.12_spmd.clone, body=%wide.region_4.11_spmd.clone.sunk | while | flops 1121737216 | bytes 63459744 | solution.py:82
  408.9 30.2 %conditional.6 = ((f32[16,512]{1,0:T(8,128)S(1)}, f32[16,512]{1,0:T(8,128)S(1)}, f32[16,512,64]{1,2,0:T(8,128)})) conditional(s32[]{:T(128)} %convert_element_type.378, (f32[16,512]{1,0:T(8,128)S(1)}, f32[16,512]{1,0:T(8,128)S(1)}, f32[16,512,64]{1,2,0:T(8,128)}) %tuple.116, (s32[]{:T(128)}, s32[4]{0:T(128)S(1)}, s32[512]{0:T(512)S(1)}, s32[]{:T(128)}, ...), branch_computations={%region_5.5_spmd, %region_6.10_spmd} | conditional | flops 1121737216 | bytes 63457408 | solution.py:193
  412.3 7.4 fusion.6
  419.6 9.2 fusion.5
  428.9 10.2 multiply_add_fusion
  446.0 6.4 all-gather.25.cloned.1.call-done
  452.4 3.5 multiply_reduce_fusion.3
  457.4 101.0 %all-gather.37.cloned.1.call-done = bf16[2816,1024]{1,0:T(8,128)(2,1)} async-done(((bf16[2816,256]{1,0:T(8,128)(2,1)}), bf16[2816,1024]{1,0:T(8,128)(2,1)}) %all-gather.37.cloned.1.call-update) | async-done | bytes 5767184 | tf_op jit(solution)/shard_map/all_gather | solution.py:133
  558.3 7.8 convolution_convert_fusion.3
  566.1 98.7 %all-gather.29.cloned.1.call-done = bf16[1024,2816]{0,1:T(8,128)(2,1)} async-done(((bf16[1024,704]{0,1:T(8,128)(2,1)}), bf16[1024,2816]{0,1:T(8,128)(2,1)}) %all-gather.29.cloned.1.call-update) | async-done | bytes 5767184 | tf_op jit(solution)/shard_map/all_gather | solution.py:131
  664.9 8.8 fusion.56
  673.7 97.7 %all-gather.33.cloned.1.call-done = bf16[1024,2816]{0,1:T(8,128)(2,1)} async-done(((bf16[1024,704]{0,1:T(8,128)(2,1)}), bf16[1024,2816]{0,1:T(8,128)(2,1)}) %all-gather.33.cloned.1.call-update) | async-done | bytes 5767184 | tf_op jit(solution)/shard_map/all_gather | solution.py:132
  771.3 10.9 fusion.22
  782.3 3.1 fusion.57
  787.0 4.0 multiply_reduce_fusion
  796.8 6.8 convolution_convert_fusion.1
  803.7 7.0 convolution_convert_fusion.2
  811.9 6.9 convolution_convert_fusion
  820.4 3.9 convolution_convert_fusion.8
  828.4 7.9 broadcast_in_dim.111
  836.4 72.6 %while.29 = (s32[]{:T(128)}, f32[16,512,64]{1,2,0:T(8,128)S(1)}, f32[2,2048,1024]{1,2,0:T(8,128)}, s32[4]{0:T(128)S(1)}, s32[]{:T(128)}, /*index=5*/s32[4]{0:T(1...) while((s32[]{:T(128)}, f32[16,512,64]{1,2,0:T(8,128)S(1)}, ...), condition=%wide.region_20.21_spmd.clone, body=%wide.region_15.20_spmd.clone.sunk | while | flops 2730760704 | bytes 159240800 | solution.py:82
  838.0 67.0 %conditional.7 = ((f32[16,512,64]{1,2,0:T(8,128)S(1)}, f32[2,2048,1024]{1,2,0:T(8,128)})) conditional(s32[]{:T(128)} %convert_element_type.379, (f32[16,512,64]{1,2,0:T(8,128)S(1)}, f32[2,2048,1024]{1,2,0:T(8,128)}) %tuple.119, (s32[]{:T(128)}, s32[4]{0:T(128)S(1)}, s32[512]{0:T(512)S(1)}, s32[]{:T(128)}, bf16[2048,1024]{0,1:T(8,128)(2,1)}, ...), branch_computations={%region_16.16_spmd, %region_17.19_spmd} | conditional | flops 2730760704 | bytes 159238432 | solution.py:308
  842.4 10.2 fusion.55
  852.6 10.8 fusion.16
  863.4 9.3 fusion.14
  878.2 5.8 maximum_add_fusion
  884.0 21.0 %dynamic_update_slice.5 = f32[2,2048,1024]{1,2,0:T(8,128)} dynamic-update-slice(f32[2,2048,1024]{1,2,0:T(8,128)} %get-tuple-element.383, f32[2,512,1024]{1,2,0:T(8,128)} %maximum_add_fusion, s32[]{:T(128)} %constant.102.clone, s32[]{:T(128)S(6)} %select_n.32, s32[]{:T(128)} %constant.102.clone) | dynamic-update-slice | bytes 8388612 | tf_op jit(solution)/shard_map/while/body/eval_jaxpr/cond/branch_1_fun/dynamic_update_slice | solution.py:303
  909.0 10.8 convert_element_type.266
  922.8 37.7 %reduce-scatter.38.cloned.1.call-done = bf16[128,2816]{1,0:T(8,128)(2,1)} async-done(((bf16[1024,2816]{1,0:T(8,128)(2,1)}), bf16[128,2816]{1,0:T(8,128)(2,1)}) %reduce-scatter.38.cloned.1.call-update) | async-done | bytes 720912 | tf_op jit(solution)/shard_map/reduce_scatter | solution.py:361
  962.9 60.4 %reduce-scatter.42.cloned.1.call-done = bf16[352,1024]{1,0:T(8,128)(2,1)} async-done(((bf16[2816,1024]{1,0:T(8,128)(2,1)}), bf16[352,1024]{1,0:T(8,128)(2,1)}) %reduce-scatter.42.cloned.1.call-update) | async-done | bytes 720912 | tf_op jit(solution)/shard_map/reduce_scatter | solution.py:367
  1023.4 234.6 %reduce-scatter.20.cloned.1.call-done = bf16[2,512,1024]{1,2,0:T(8,128)(2,1)} async-done(((bf16[2,2048,1024]{1,2,0:T(8,128)(2,1)}), bf16[2,512,1024]{1,2,0:T(8,128)(2,1)}) %reduce-scatter.20.cloned.1.call-update) | async-done | bytes 2097168 | tf_op jit(solution)/shard_map/reduce_scatter | solution.py:321
  1274.5 3.2 copy.77
  1279.0 7.7 add_convert_fusion
  1288.2 15.8 %reduce-scatter.48.cloned.1.call-done = bf16[704,128]{1,0:T(8,128)(2,1)} async-done(((bf16[2816,128]{1,0:T(8,128)(2,1)}), bf16[704,128]{1,0:T(8,128)(2,1)}) %reduce-scatter.48.cloned.1.call-update) | async-done | bytes 180240
  1305.9 22.1 %reduce-scatter.46.cloned.1.call-done = bf16[704,128]{1,0:T(8,128)(2,1)} async-done(((bf16[2816,128]{1,0:T(8,128)(2,1)}), bf16[704,128]{1,0:T(8,128)(2,1)}) %reduce-scatter.46.cloned.1.call-update) | async-done | bytes 180240
  1329.9 22.3 %reduce-scatter.44.cloned.1.call-done = bf16[352,256]{1,0:T(8,128)(2,1)} async-done(((bf16[352,1024]{1,0:T(8,128)(2,1)}), bf16[352,256]{1,0:T(8,128)(2,1)}) %reduce-scatter.44.cloned.1.call-update) | async-done | bytes 180240 | tf_op jit(solution)/shard_map/reduce_scatter | solution.py:396
  1353.9 4.4 fusion.59
  1360.9 35.2 %reduce-scatter.22.cloned.1.call-done = bf16[128,1024]{1,0:T(8,128)(2,1)} async-done(((bf16[1024,1024]{1,0:T(8,128)(2,1)}), bf16[128,1024]{1,0:T(8,128)(2,1)}) %reduce-scatter.22.cloned.1.call-update) | async-done | bytes 262160 | tf_op jit(solution)/shard_map/reduce_scatter | solution.py:349
  1396.2 6.6 fusion.28
  1402.8 37.9 %reduce-scatter.26.cloned.1.call-done = bf16[128,1024]{1,0:T(8,128)(2,1)} async-done(((bf16[1024,1024]{1,0:T(8,128)(2,1)}), bf16[128,1024]{1,0:T(8,128)(2,1)}) %reduce-scatter.26.cloned.1.call-update) | async-done | bytes 262160 | tf_op jit(solution)/shard_map/reduce_scatter | solution.py:352
  1440.7 3.4 fusion.34
  1447.2 12.7 all-reduce.3
  1460.1 12.2 all-reduce.2
  1472.2 13.2 reduce-scatter.30.cloned.1.call-done
  1485.5 3.4 fusion.30
  1488.9 18.5 %reduce-scatter.24.cloned.1.call-done = bf16[128,256]{1,0:T(8,128)(2,1)} async-done(((bf16[128,1024]{1,0:T(8,128)(2,1)}), bf16[128,256]{1,0:T(8,128)(2,1)}) %reduce-scatter.24.cloned.1.call-update) | async-done | bytes 65552 | tf_op jit(solution)/shard_map/reduce_scatter | solution.py:378
  1508.9 18.6 %reduce-scatter.28.cloned.1.call-done = bf16[128,256]{1,0:T(8,128)(2,1)} async-done(((bf16[128,1024]{1,0:T(8,128)(2,1)}), bf16[128,256]{1,0:T(8,128)(2,1)}) %reduce-scatter.28.cloned.1.call-update) | async-done | bytes 65552 | tf_op jit(solution)/shard_map/reduce_scatter | solution.py:381
  1529.0 18.6 %reduce-scatter.32.cloned.1.call-done = bf16[128,256]{1,0:T(8,128)(2,1)} async-done(((bf16[128,1024]{1,0:T(8,128)(2,1)}), bf16[128,256]{1,0:T(8,128)(2,1)}) %reduce-scatter.32.cloned.1.call-update) | async-done | bytes 65552 | tf_op jit(solution)/shard_map/reduce_scatter | solution.py:384
  (261 shorter events, 93.3 us)
Async XLA Ops:
  7.2 25.4 %copy-start.32 = (f32[128,256]{1,0:T(8,128)S(1)}, f32[128,256]{1,0:T(8,128)}, u32[]{:S(2)}) copy-start(f32[128,256]{1,0:T(8,128)} %param.26) | copy-start | bytes 393220
  7.2 35.6 %copy-start.28 = (f32[352,256]{1,0:T(8,128)S(1)}, f32[352,256]{1,0:T(8,128)}, u32[]{:S(2)}) copy-start(f32[352,256]{1,0:T(8,128)} %param.31) | copy-start | bytes 1081348
  7.2 60.2 %all-gather.21.cloned.1.call-start = ((), (), s32[]{:S(2)}) async-start(), calls=%async_computation.18 | async-start | bytes 2621440 | tf_op jit(solution)/shard_map/all_gather | solution.py:129
  8.2 35.3 %copy-start.29 = (f32[128,704]{0,1:T(8,128)S(1)}, f32[128,704]{0,1:T(8,128)}, u32[]{:S(2)}) copy-start(f32[128,704]{0,1:T(8,128)} %param.29) | copy-start | bytes 1081348
  20.7 23.6 %copy-start.30 = (f32[128,704]{0,1:T(8,128)S(1)}, f32[128,704]{0,1:T(8,128)}, u32[]{:S(2)}) copy-start(f32[128,704]{0,1:T(8,128)} %param.30) | copy-start | bytes 1081348
  20.7 92.7 %all-gather.19.cloned.1.call-start = ((), (), s32[]{:S(2)}) async-start(), calls=%async_computation.17 | async-start | bytes 2621440 | tf_op jit(solution)/shard_map/all_gather | solution.py:127
  32.5 12.6 copy-start.45
  32.5 21.3 %copy-start.8 = (bf16[512,1024]{1,0:T(8,128)(2,1)S(1)}, bf16[512,1024]{1,0:T(8,128)(2,1)}, u32[]{:S(2)}) copy-start(bf16[512,1024]{1,0:T(8,128)(2,1)} %param.22) | copy-start | bytes 3145732
  32.5 127.0 %all-gather.15.cloned.1.call-start = ((), (), s32[]{:S(2)}) async-start(), calls=%async_computation.15 | async-start | bytes 2621440 | tf_op jit(solution)/shard_map/all_gather | solution.py:128
  32.6 34.8 %copy-start.44 = (bf16[512,1024]{1,0:T(8,128)(2,1)S(1)}, bf16[512,1024]{1,0:T(8,128)(2,1)}, u32[]{:S(2)}) copy-start(bf16[512,1024]{1,0:T(8,128)(2,1)} %param.23) | copy-start | bytes 3145732
  42.7 143.6 %all-gather.35.cloned.1.call-start = ((), (), s32[]{:S(2)}) async-start(), calls=%async_computation.25 | async-start | bytes 1622016 | tf_op jit(solution)/shard_map/all_gather | solution.py:122
  43.5 170.5 %all-gather.27.cloned.1.call-start = ((), (), s32[]{:S(2)}) async-start(), calls=%async_computation.21 | async-start | bytes 1622016 | tf_op jit(solution)/shard_map/all_gather | solution.py:120
  44.3 197.4 %all-gather.31.cloned.1.call-start = ((), (), s32[]{:S(2)}) async-start(), calls=%async_computation.23 | async-start | bytes 1622016 | tf_op jit(solution)/shard_map/all_gather | solution.py:121
  45.0 279.5 %all-gather.23.cloned.1.call-start = ((), (), s32[]{:S(2)}) async-start(), calls=%async_computation.19 | async-start | bytes 5242880 | tf_op jit(solution)/shard_map/all_gather | solution.py:204
  53.8 105.8 %copy-start.34 = (f32[8,1,128]{2,1,0:T(1,128)}, f32[8,1,128]{2,1,0:T(1,128)S(1)}, u32[]{:S(2)}) copy-start(f32[8,1,128]{2,1,0:T(1,128)S(1)} %convert_element_type.288) | copy-start | bytes 12292
  54.0 17.3 %copy-start.36 = (f32[512]{0:T(512)}, f32[512]{0:T(512)S(1)}, u32[]{:S(2)}) copy-start(f32[512]{0:T(512)S(1)} %fusion.31) | copy-start | bytes 6148
  54.1 105.5 %copy-start.38 = (f32[512]{0:T(512)}, f32[512]{0:T(512)S(1)}, u32[]{:S(2)}) copy-start(f32[512]{0:T(512)S(1)} %fusion.42) | copy-start | bytes 6148
  67.4 4.0 copy-start.47
  71.3 334.7 %all-gather.17.cloned.1.call-start = ((), (), s32[]{:S(2)}) async-start(), calls=%async_computation.16 | async-start | bytes 5242880 | tf_op jit(solution)/shard_map/all_gather | solution.py:203
  72.7 89.8 %copy-start.26 = (f32[512,32]{0,1:T(8,128)}, f32[512,32]{0,1:T(8,128)S(1)}, u32[]{:S(2)}) copy-start(f32[512,32]{0,1:T(8,128)S(1)} %get-tuple-element.733) | copy-start | bytes 196612
  165.3 287.1 %all-gather.25.cloned.1.call-start = ((), (), s32[]{:S(2)}) async-start(), calls=%async_computation.20 | async-start | bytes 2621440 | tf_op jit(solution)/shard_map/all_gather | solution.py:130
  176.8 381.6 %all-gather.37.cloned.1.call-start = ((), (), s32[]{:S(2)}) async-start(), calls=%async_computation.26 | async-start | bytes 7208960 | tf_op jit(solution)/shard_map/all_gather | solution.py:133
  186.3 55.3 %copy-start.46 = (f32[128]{0:T(128)S(1)}, f32[128]{0:T(128)}, u32[]{:S(2)}) copy-start(f32[128]{0:T(128)} %param.33) | copy-start | bytes 1540
  186.3 64.6 %copy-start.17 = (bf16[512,16,32]{0,2,1:T(8,128)(2,1)S(1)}, bf16[512,16,32]{0,2,1:T(8,128)(2,1)}, u32[]{:S(2)}) copy-start(bf16[512,16,32]{0,2,1:T(8,128)(2,1)} %get-tuple-element.723) | copy-start | bytes 1572868
  186.4 64.6 %copy-start.18 = (bf16[512,16,32]{0,2,1:T(8,128)(2,1)S(1)}, bf16[512,16,32]{0,2,1:T(8,128)(2,1)}, u32[]{:S(2)}) copy-start(bf16[512,16,32]{0,2,1:T(8,128)(2,1)} %get-tuple-element.724) | copy-start | bytes 1572868
  186.4 478.5 %all-gather.29.cloned.1.call-start = ((), (), s32[]{:S(2)}) async-start(), calls=%async_computation.22 | async-start | bytes 7208960 | tf_op jit(solution)/shard_map/all_gather | solution.py:131
  214.0 557.3 %all-gather.33.cloned.1.call-start = ((), (), s32[]{:S(2)}) async-start(), calls=%async_computation.24 | async-start | bytes 7208960 | tf_op jit(solution)/shard_map/all_gather | solution.py:132
  241.6 678.3 %reduce-scatter.34.cloned.1.call-start = ((), (), s32[]{:S(2)}) async-start(), calls=%async_computation.34 | async-start | bytes 2359296 | tf_op jit(solution)/shard_map/reduce_scatter | solution.py:358
  455.9 335.1 %copy-start.5 = (f32[512,1024]{1,0:T(8,128)}, f32[512,1024]{1,0:T(8,128)S(1)}, u32[]{:S(2)}) copy-start(f32[512,1024]{1,0:T(8,128)S(1)} %get-tuple-element.735) | copy-start | bytes 6291460
  771.3 10.9 copy-start.41
  782.2 3.2 copy-start.49
  782.2 3.2 copy-start.50
  782.2 4.7 copy-start.42
  787.0 4.1 copy-start.20
  795.6 124.8 %reduce-scatter.40.cloned.1.call-start = ((), (), s32[]{:S(2)}) async-start(), calls=%async_computation.37 | async-start | bytes 6488064 | tf_op jit(solution)/shard_map/reduce_scatter | solution.py:364
  803.6 156.8 %reduce-scatter.38.cloned.1.call-start = ((), (), s32[]{:S(2)}) async-start(), calls=%async_computation.36 | async-start | bytes 6488064 | tf_op jit(solution)/shard_map/reduce_scatter | solution.py:361
  810.7 212.6 %reduce-scatter.42.cloned.1.call-start = ((), (), s32[]{:S(2)}) async-start(), calls=%async_computation.38 | async-start | bytes 6488064 | tf_op jit(solution)/shard_map/reduce_scatter | solution.py:367
  818.8 439.1 %reduce-scatter.20.cloned.1.call-start = ((), (), s32[]{:S(2)}) async-start(), calls=%async_computation.27 | async-start | bytes 10485760 | tf_op jit(solution)/shard_map/reduce_scatter | solution.py:321
  825.8 2.4 copy-start.15
  872.7 2.7 copy-start.1
  875.4 2.8 copy-start.4
  884.0 21.0 %copy-start.3 = (f32[16,512,64]{1,2,0:T(8,128)S(1)}, f32[16,512,64]{1,2,0:T(8,128)}, u32[]{:S(2)}) copy-start(f32[16,512,64]{1,2,0:T(8,128)} %copy-done.2) | copy-start | bytes 6291460 | tf_op jit(solution)/shard_map/while/body/eval_jaxpr/cond
  919.8 366.8 %reduce-scatter.36.cloned.1.call-start = ((), (), s32[]{:S(2)}) async-start(), calls=%async_computation.35 | async-start | bytes 327680 | tf_op jit(solution)/shard_map/reduce_scatter | solution.py:387
  920.4 383.6 %reduce-scatter.48.cloned.1.call-start = ((), (), s32[]{:S(2)}) async-start(), calls=%async_computation.41 | async-start | bytes 901120
  922.8 405.2 %reduce-scatter.46.cloned.1.call-start = ((), (), s32[]{:S(2)}) async-start(), calls=%async_computation.40 | async-start | bytes 901120
  962.8 389.4 %reduce-scatter.44.cloned.1.call-start = ((), (), s32[]{:S(2)}) async-start(), calls=%async_computation.39 | async-start | bytes 901120 | tf_op jit(solution)/shard_map/reduce_scatter | solution.py:396
  1023.3 236.2 %copy-start.27 = (f32[512,32]{0,1:T(8,128)S(1)}, f32[512,32]{0,1:T(8,128)}, u32[]{:S(2)}) copy-start(f32[512,32]{0,1:T(8,128)} %copy-done.26) | copy-start | bytes 196612
  1023.3 236.2 %copy-start.31 = (f32[512,32]{0,1:T(8,128)S(1)}, f32[512,32]{0,1:T(8,128)}, u32[]{:S(2)}) copy-start(f32[512,32]{0,1:T(8,128)} %get-tuple-element.731) | copy-start | bytes 196612
  1023.3 372.8 %reduce-scatter.22.cloned.1.call-start = ((), (), s32[]{:S(2)}) async-start(), calls=%async_computation.28 | async-start | bytes 2359296 | tf_op jit(solution)/shard_map/reduce_scatter | solution.py:349
  1260.4 4.2 copy-start.24
  1264.5 176.2 %reduce-scatter.26.cloned.1.call-start = ((), (), s32[]{:S(2)}) async-start(), calls=%async_computation.30 | async-start | bytes 2359296 | tf_op jit(solution)/shard_map/reduce_scatter | solution.py:352
  1267.4 218.0 %reduce-scatter.30.cloned.1.call-start = ((), (), s32[]{:S(2)}) async-start(), calls=%async_computation.32 | async-start | bytes 2359296 | tf_op jit(solution)/shard_map/reduce_scatter | solution.py:355
  1274.4 233.0 %reduce-scatter.24.cloned.1.call-start = ((), (), s32[]{:S(2)}) async-start(), calls=%async_computation.29 | async-start | bytes 327680 | tf_op jit(solution)/shard_map/reduce_scatter | solution.py:378
  1274.5 3.3 copy-start.48
  1274.5 4.5 copy-start.6
  1286.6 67.2 %copy-start.25 = (bf16[512,16,64]{0,2,1:T(8,128)(2,1)S(1)}, bf16[512,16,64]{0,2,1:T(8,128)(2,1)}, u32[]{:S(2)}) copy-start(bf16[512,16,64]{0,2,1:T(8,128)(2,1)} %copy-done.24) | copy-start | bytes 3145732
  1353.9 4.4 copy-start.23
  1353.9 4.4 copy-start.43
  1396.1 44.6 %copy-start.11 = (f32[512,1024]{0,1:T(8,128)S(1)}, f32[512,1024]{0,1:T(8,128)}, u32[]{:S(2)}) copy-start(f32[512,1024]{0,1:T(8,128)} %copy.77) | copy-start | bytes 6291460
  1396.1 131.4 %reduce-scatter.28.cloned.1.call-start = ((), (), s32[]{:S(2)}) async-start(), calls=%async_computation.31 | async-start | bytes 327680 | tf_op jit(solution)/shard_map/reduce_scatter | solution.py:381
  1440.7 106.9 %reduce-scatter.32.cloned.1.call-start = ((), (), s32[]{:S(2)}) async-start(), calls=%async_computation.33 | async-start | bytes 327680 | tf_op jit(solution)/shard_map/reduce_scatter | solution.py:384
  1444.2 3.0 copy-start.40
  1444.2 41.3 %copy-start.37 = (f32[512]{0:T(512)S(1)}, f32[512]{0:T(512)}, u32[]{:S(2)}) copy-start(f32[512]{0:T(512)} %copy-done.36) | copy-start | bytes 6148
  1444.2 41.3 %copy-start.14 = (f32[512,1024]{1,0:T(8,128)S(1)}, f32[512,1024]{1,0:T(8,128)}, u32[]{:S(2)}) copy-start(f32[512,1024]{1,0:T(8,128)} %copy-done.12) | copy-start | bytes 6291460
  (14 other events, 20.2 us)
Sparse Core Ops, SparseCore 0:
  20.9 46.5 all-gather.20
  69.0 44.4 all-gather.18
  115.1 44.4 all-gather.14
  161.9 24.4 all-gather.34
  188.6 25.2 all-gather.26
  216.3 25.2 all-gather.30
  243.8 80.7 all-gather.22
  326.7 79.2 all-gather.16
  407.6 44.7 all-gather.24
  453.8 104.4 all-gather.36
  559.9 104.8 all-gather.28
  666.3 104.9 all-gather.32
  795.8 39.5 reduce-scatter.33
  839.0 59.0 reduce-scatter.39
  901.4 59.0 reduce-scatter.37
  964.2 59.0 reduce-scatter.41
  1025.5 232.4 reduce-scatter.19
  1260.1 20.2 reduce-scatter.35
  1282.8 21.1 reduce-scatter.47
  1306.2 21.7 reduce-scatter.45
  1330.4 21.7 reduce-scatter.43
  1355.8 40.2 reduce-scatter.21
  1399.4 41.2 reduce-scatter.25
  1444.2 41.2 reduce-scatter.29
  1487.7 19.6 reduce-scatter.23
  1509.6 17.8 reduce-scatter.27
  1529.6 17.9 reduce-scatter.31
where the time goes:
time: 1570 us; the launch traced here: 1560 us
  waiting for transfers between devices  1150 us (73%)
  matrix products  157 us (10%)
  blocking collectives  87.4 us (6%)
  local copies, waits for them, and re-layouts  79.9 us (5%)
  other arithmetic  58.8 us (4%)
  between operations  16 us (1%)
    reduce_scatter x1, waiting for transfers between devices, per_device(): lax.psum_scatter(folded[1].astype(jnp.bfloat16), 'ctx', scatter_dimension...  235 us
    all_gather x1, waiting for transfers between devices, per_device(): lax.all_gather(rows_part[6], 'ctx', axis=1, tiled=True)  101 us
    all_gather x1, waiting for transfers between devices, per_device(): lax.all_gather(rows_part[4], 'ctx', axis=1, tiled=True)  98.7 us
    all_gather x1, waiting for transfers between devices, per_device(): lax.all_gather(rows_part[5], 'ctx', axis=1, tiled=True)  97.7 us
    all_gather x1, waiting for transfers between devices, per_device(): lax.all_gather(key_flat, 'ctx', axis=0, tiled=True)  74.9 us
    all_gather x1, waiting for transfers between devices, per_device(): lax.all_gather(mixed_flat, 'ctx', axis=0, tiled=True)  73.5 us
    reduce_scatter x1, waiting for transfers between devices, per_device(): lax.psum_scatter(local_grads[6].astype(jnp.bfloat16), 'fsdp', scatter_dim...  60.4 us
    all_gather x1, waiting for transfers between devices, per_device(): lax.all_gather(rows_part[1], 'ctx', axis=1, tiled=True)  43.1 us
  transfers between devices with their start and end apart: 27, of which 24 were waited for; matrix products, arithmetic and copies ran while one was open for 17% of the time, Pallas kernels for 0%

commit v1 on v0

v1 whole, which is shorter than its diff:
```python
import functools
import math

import jax
import jax.numpy as jnp
from jax import lax
from jax.experimental import pallas as pl
from jax.experimental.pallas import tpu as pltpu
from jax.sharding import PartitionSpec as P

HEAD = 64
EPSILON = 1e-05
THETA = 10000.0
NEGATIVE = -1e30
BLOCK = 256
VMEM_LIMIT = 58 * 1024 * 1024
MESH = pl.DeviceIdType.MESH
BF16 = jnp.bfloat16
F32 = jnp.float32


def nn(left, right):
    return lax.dot_general(left, right, (((1,), (0,)), ((), ())), preferred_element_type=F32)


def nt(left, right):
    return lax.dot_general(left, right, (((1,), (1,)), ((), ())), preferred_element_type=F32)


def tn(left, right):
    return lax.dot_general(left, right, (((0,), (0,)), ((), ())), preferred_element_type=F32)


def widen(table, width):
    return jnp.concatenate([table] * (width // table.shape[1]), axis=1)


def half_swap(rows):
    width = rows.shape[1]
    lane = lax.broadcasted_iota(jnp.int32, rows.shape, 1)
    low = lax.rem(lane, HEAD) < HEAD // 2
    return jnp.where(
        low,
        pltpu.roll(rows, width - HEAD // 2, 1),
        pltpu.roll(rows, HEAD // 2, 1),
    )


def head_lanes(shape, head):
    lane = lax.broadcasted_iota(jnp.int32, shape, 1)
    return (lane >= head * HEAD) & (lane < (head + 1) * HEAD)


def forward_kernel(
    x, vf, wqkv, gain, cos_t, sin_t, start,
    h1, q, k, vm, kt, out, att, lse,
    vt, acc, mx, tot,
):
    group = x.shape[0]
    cols = vf.shape[1]
    heads = cols // HEAD
    blocks = group // BLOCK

    def project(b, carry):
        rows = pl.ds(pl.multiple_of(b * BLOCK, BLOCK), BLOCK)
        xv = x[rows, :].astype(F32)
        rstd = lax.rsqrt(jnp.mean(xv * xv, axis=1, keepdims=True) + EPSILON)
        hv = (xv * rstd * gain[...]).astype(BF16)
        h1[rows, :] = hv
        raw = nn(hv, wqkv[...])
        cos_v = widen(cos_t[rows, :], cols)
        sin_v = widen(sin_t[rows, :], cols)
        rq = raw[:, :cols]
        rk = raw[:, cols : 2 * cols]
        rv = raw[:, 2 * cols :]
        qv = (rq * cos_v + half_swap(rq) * sin_v).astype(BF16)
        q[rows, :] = (qv.astype(F32) * (1.0 / math.sqrt(HEAD))).astype(BF16)
        kv = (rk * cos_v + half_swap(rk) * sin_v).astype(BF16)
        k[rows, :] = kv
        kt[:, rows] = kv.T
        mixed = (0.5 * rv + 0.5 * vf[rows, :].astype(F32)).astype(BF16)
        vm[rows, :] = mixed
        vt[:, rows] = mixed.T
        return carry

    lax.fori_loop(0, blocks, project, 0)

    def queries(b, carry):
        rows = pl.ds(pl.multiple_of(b * BLOCK, BLOCK), BLOCK)
        acc[...] = jnp.zeros_like(acc)
        mx[...] = jnp.full_like(mx, NEGATIVE)
        tot[...] = jnp.zeros_like(tot)
        qv = q[rows, :]
        first = start[0:1, rows]

        def keys(kb, inner):
            krows = pl.ds(pl.multiple_of(kb * BLOCK, BLOCK), BLOCK)
            kv = k[krows, :]
            key_pos = kb * BLOCK + lax.broadcasted_iota(jnp.int32, (BLOCK, BLOCK), 0)
            query_pos = b * BLOCK + lax.broadcasted_iota(jnp.int32, (BLOCK, BLOCK), 1)
            allowed = (key_pos <= query_pos) & (key_pos >= first)
            for head in range(heads):
                band = slice(head * HEAD, (head + 1) * HEAD)
                qm = jnp.where(head_lanes(qv.shape, head), qv, jnp.zeros_like(qv))
                s = jnp.where(allowed, nt(kv, qm), NEGATIVE)
                old = mx[head : head + 1, :]
                new = jnp.maximum(old, jnp.max(s, axis=0, keepdims=True))
                p = jnp.exp(s - new)
                shrink = jnp.exp(old - new)
                mx[head : head + 1, :] = new
                tot[head : head + 1, :] = tot[head : head + 1, :] * shrink + jnp.sum(
                    p, axis=0, keepdims=True
                )
                acc[band, :] = acc[band, :] * shrink + nn(vt[band, krows], p.astype(BF16))
            return inner

        lax.fori_loop(0, b + 1, keys, 0)
        for head in range(heads):
            band = slice(head * HEAD, (head + 1) * HEAD)
            acc[band, :] = acc[band, :] / tot[head : head + 1, :]
        ov = acc[...].T
        att[rows, :] = ov
        out[rows, :] = ov.astype(BF16)
        lse[:, rows] = mx[...] + jnp.log(tot[...])
        return carry

    lax.fori_loop(0, blocks, queries, 0)


def forward_attention(x, vf, wqkv, gain, cos_t, sin_t, start):
    group, depth = x.shape
    cols = vf.shape[1]
    shapes = (
        jax.ShapeDtypeStruct((group, depth), BF16),
        jax.ShapeDtypeStruct((group, cols), BF16),
        jax.ShapeDtypeStruct((group, cols), BF16),
        jax.ShapeDtypeStruct((group, cols), BF16),
        jax.ShapeDtypeStruct((cols, group), BF16),
        jax.ShapeDtypeStruct((group, cols), BF16),
        jax.ShapeDtypeStruct((group, cols), F32),
        jax.ShapeDtypeStruct((8, group), F32),
    )
    vmem = pl.BlockSpec(memory_space=pltpu.VMEM)
    return pl.pallas_call(
        forward_kernel,
        out_shape=shapes,
        in_specs=[vmem] * 7,
        out_specs=[vmem] * 8,
        scratch_shapes=[
            pltpu.VMEM((cols, group), BF16),
            pltpu.VMEM((cols, BLOCK), F32),
            pltpu.VMEM((8, BLOCK), F32),
            pltpu.VMEM((8, BLOCK), F32),
        ],
        compiler_params=pltpu.CompilerParams(vmem_limit_bytes=VMEM_LIMIT),
        name="attention_forward",
    )(x, vf, wqkv, gain, cos_t, sin_t, start)


def backward_kernel(
    x, h1, q, k, vm, kt, att, lse, do, wqkv, gain, cos_t, sin_t, start,
    part, dvm, gw, dg,
    dqt, dkv, dvv, rows_t, d3,
):
    group, depth = x.shape
    cols = vm.shape[1]
    heads = cols // HEAD
    blocks = group // BLOCK
    dqt[...] = jnp.zeros_like(dqt)

    def dots(b, carry):
        rows = pl.ds(pl.multiple_of(b * BLOCK, BLOCK), BLOCK)
        prod = do[rows, :].astype(F32) * att[rows, :]
        high = prod.astype(BF16)
        low = (prod - high.astype(F32)).astype(BF16)
        head_row = lax.broadcasted_iota(jnp.int32, (8, cols), 0)
        lane = lax.broadcasted_iota(jnp.int32, (8, cols), 1)
        pick = (lane // HEAD == head_row).astype(F32).astype(BF16)
        rows_t[:, rows] = nt(pick, high) + nt(pick, low)
        return carry

    lax.fori_loop(0, blocks, dots, 0)

    def keys(kb, carry):
        krows = pl.ds(pl.multiple_of(kb * BLOCK, BLOCK), BLOCK)
        kv = k[krows, :]
        vv = vm[krows, :]
        dkv[...] = jnp.zeros_like(dkv)
        dvv[...] = jnp.zeros_like(dvv)

        def queries(b, inner):
            rows = pl.ds(pl.multiple_of(b * BLOCK, BLOCK), BLOCK)
            qv = q[rows, :]
            dov = do[rows, :]
            first = start[0:1, rows]
            key_pos = kb * BLOCK + lax.broadcasted_iota(jnp.int32, (BLOCK, BLOCK), 0)
            query_pos = b * BLOCK + lax.broadcasted_iota(jnp.int32, (BLOCK, BLOCK), 1)
            allowed = (key_pos <= query_pos) & (key_pos >= first)
            dk_sum = jnp.zeros((BLOCK, cols), F32)
            dv_sum = jnp.zeros((BLOCK, cols), F32)
            for head in range(heads):
                band = slice(head * HEAD, (head + 1) * HEAD)
                lanes = head_lanes(qv.shape, head)
                qm = jnp.where(lanes, qv, jnp.zeros_like(qv))
                dom = jnp.where(lanes, dov, jnp.zeros_like(dov))
                s = jnp.where(allowed, nt(kv, qm), NEGATIVE)
                p = jnp.exp(s - lse[head : head + 1, rows])
                ds = (p * (nt(vv, dom) - rows_t[head : head + 1, rows])).astype(BF16)
                dv_sum = dv_sum + nn(p.astype(BF16), dom)
                dk_sum = dk_sum + nn(ds, qm)
                dqt[band, rows] = dqt[band, rows] + nn(kt[band, krows], ds)
            dkv[...] = dkv[...] + dk_sum
            dvv[...] = dvv[...] + dv_sum
            return inner

        lax.fori_loop(kb, blocks, queries, 0)
        cos_v = widen(cos_t[krows, :], cols)
        sin_v = widen(sin_t[krows, :], cols)
        dk = dkv[...]
        d3[krows, cols : 2 * cols] = (dk * cos_v - half_swap(dk) * sin_v).astype(BF16)
        dv = dvv[...]
        dvm[krows, :] = dv.astype(BF16)
        d3[krows, 2 * cols :] = (0.5 * dv).astype(BF16)
        return carry

    lax.fori_loop(0, blocks, keys, 0)
    dg[...] = jnp.zeros_like(dg)

    def finish(b, carry):
        rows = pl.ds(pl.multiple_of(b * BLOCK, BLOCK), BLOCK)
        cos_v = widen(cos_t[rows, :], cols)
        sin_v = widen(sin_t[rows, :], cols)
        dq = dqt[:, rows].T * (1.0 / math.sqrt(HEAD))
        d3[rows, :cols] = (dq * cos_v - half_swap(dq) * sin_v).astype(BF16)
        dh = nt(d3[rows, :], wqkv[...])
        xv = x[rows, :].astype(F32)
        rstd = lax.rsqrt(jnp.mean(xv * xv, axis=1, keepdims=True) + EPSILON)
        xhat = xv * rstd
        u = dh * gain[...]
        part[rows, :] = (rstd * (u - xhat * jnp.mean(u * xhat, axis=1, keepdims=True))).astype(BF16)
        dg[0:1, :] = dg[0:1, :] + jnp.sum(dh * xhat, axis=0, keepdims=True)
        return carry

    lax.fori_loop(0, blocks, finish, 0)

    def weight(b, carry):
        at = pl.ds(pl.multiple_of(b * BLOCK, BLOCK), BLOCK)
        gw[at, :] = tn(h1[:, at], d3[...]).astype(BF16)
        return carry

    lax.fori_loop(0, depth // BLOCK, weight, 0)


def backward_attention(x, h1, q, k, vm, kt, att, lse, do, wqkv, gain, cos_t, sin_t, start):
    group, depth = x.shape
    cols = vm.shape[1]
    shapes = (
        jax.ShapeDtypeStruct((group, depth), BF16),
        jax.ShapeDtypeStruct((group, cols), BF16),
        jax.ShapeDtypeStruct((depth, 3 * cols), BF16),
        jax.ShapeDtypeStruct((8, depth), F32),
    )
    vmem = pl.BlockSpec(memory_space=pltpu.VMEM)
    return pl.pallas_call(
        backward_kernel,
        out_shape=shapes,
        in_specs=[vmem] * 14,
        out_specs=[vmem] * 4,
        scratch_shapes=[
            pltpu.VMEM((cols, group), F32),
            pltpu.VMEM((BLOCK, cols), F32),
            pltpu.VMEM((BLOCK, cols), F32),
            pltpu.VMEM((8, group), F32),
            pltpu.VMEM((group, 3 * cols), BF16),
        ],
        compiler_params=pltpu.CompilerParams(vmem_limit_bytes=VMEM_LIMIT),
        name="attention_backward",
    )(x, h1, q, k, vm, kt, att, lse, do, wqkv, gain, cos_t, sin_t, start)


def feed_kernel(
    o, x, dy, wo, gain, gu, wd,
    out, dx2, do, gwo, ggu, gwd, dg,
    x2, h2, h2t, total, dh2, act, dgu,
):
    step = pl.program_id(0)
    tokens, depth = x.shape
    chunk = wd.shape[0]
    blocks = tokens // BLOCK

    @pl.when(step == 0)
    def _():
        def rows_of(b, carry):
            rows = pl.ds(pl.multiple_of(b * BLOCK, BLOCK), BLOCK)
            mid = x[rows, :].astype(F32) + nn(o[rows, :], wo[...])
            x2[rows, :] = mid
            rstd = lax.rsqrt(jnp.mean(mid * mid, axis=1, keepdims=True) + EPSILON)
            hv = (mid * rstd * gain[...]).astype(BF16)
            h2[rows, :] = hv
            h2t[:, rows] = hv.T
            total[rows, :] = mid
            dh2[rows, :] = jnp.zeros((BLOCK, depth), F32)
            return carry

        lax.fori_loop(0, blocks, rows_of, 0)

    def rows_of(b, carry):
        rows = pl.ds(pl.multiple_of(b * BLOCK, BLOCK), BLOCK)
        both = nn(h2[rows, :], gu[0])
        gate = both[:, :chunk]
        up = both[:, chunk:]
        da = nt(dy[rows, :], wd[...]).astype(BF16).astype(F32)
        sig = 1.0 / (1.0 + jnp.exp(-gate))
        silu = gate * sig
        av = (silu * up).astype(BF16)
        act[rows, :] = av
        dgate = (da * up * (sig * (1.0 + gate * (1.0 - sig)))).astype(BF16)
        dup = (da * silu).astype(BF16)
        dv = jnp.concatenate([dgate, dup], axis=1)
        dgu[rows, :] = dv
        total[rows, :] = total[rows, :] + nn(av, wd[...])
        dh2[rows, :] = dh2[rows, :] + nt(dv, gu[0])
        return carry

    lax.fori_loop(0, blocks, rows_of, 0)

    gwd[...] = tn(act[...], dy[...]).astype(BF16)

    def weight(b, carry):
        rows = pl.ds(pl.multiple_of(b * BLOCK, BLOCK), BLOCK)
        ggu[0, rows, :] = nn(h2t[rows, :], dgu[...]).astype(BF16)
        return carry

    lax.fori_loop(0, depth // BLOCK, weight, 0)

    @pl.when(step == pl.num_programs(0) - 1)
    def _():
        dg[...] = jnp.zeros_like(dg)

        def rows_of(b, carry):
            rows = pl.ds(pl.multiple_of(b * BLOCK, BLOCK), BLOCK)
            out[rows, :] = total[rows, :].astype(BF16)
            mid = x2[rows, :]
            rstd = lax.rsqrt(jnp.mean(mid * mid, axis=1, keepdims=True) + EPSILON)
            xhat = mid * rstd
            dh = dh2[rows, :]
            u = dh * gain[...]
            dm = dy[rows, :].astype(F32) + rstd * (
                u - xhat * jnp.mean(u * xhat, axis=1, keepdims=True)
            )
            dx2[rows, :] = dm
            dg[0:1, :] = dg[0:1, :] + jnp.sum(dh * xhat, axis=0, keepdims=True)
            db = dm.astype(BF16)
            h2[rows, :] = db
            do[rows, :] = nt(db, wo[...]).astype(BF16)
            return carry

        lax.fori_loop(0, blocks, rows_of, 0)

        def weight_out(b, carry):
            at = pl.ds(pl.multiple_of(b * BLOCK, BLOCK), BLOCK)
            gwo[at, :] = tn(o[:, at], h2[...]).astype(BF16)
            return carry

        lax.fori_loop(0, depth // BLOCK, weight_out, 0)


def feed_forward(o, x, dy, wo, gain, gu, wd):
    tokens, depth = x.shape
    steps, _, width = gu.shape
    chunk = width // 2
    whole = lambda shape: pl.BlockSpec(shape, lambda i: (0,) * len(shape))
    shapes = (
        jax.ShapeDtypeStruct((tokens, depth), BF16),
        jax.ShapeDtypeStruct((tokens, depth), F32),
        jax.ShapeDtypeStruct((tokens, depth), BF16),
        jax.ShapeDtypeStruct((depth, depth), BF16),
        jax.ShapeDtypeStruct(gu.shape, BF16),
        jax.ShapeDtypeStruct(wd.shape, BF16),
        jax.ShapeDtypeStruct((8, depth), F32),
    )
    return pl.pallas_call(
        feed_kernel,
        grid=(steps,),
        out_shape=shapes,
        in_specs=[
            whole((tokens, depth)),
            whole((tokens, depth)),
            whole((tokens, depth)),
            whole((depth, depth)),
            whole((1, depth)),
            pl.BlockSpec((1, depth, width), lambda i: (i, 0, 0)),
            pl.BlockSpec((chunk, depth), lambda i: (i, 0)),
        ],
        out_specs=[
            whole((tokens, depth)),
            whole((tokens, depth)),
            whole((tokens, depth)),
            whole((depth, depth)),
            pl.BlockSpec((1, depth, width), lambda i: (i, 0, 0)),
            pl.BlockSpec((chunk, depth), lambda i: (i, 0)),
            whole((8, depth)),
        ],
        scratch_shapes=[
            pltpu.VMEM((tokens, depth), F32),
            pltpu.VMEM((tokens, depth), BF16),
            pltpu.VMEM((depth, tokens), BF16),
            pltpu.VMEM((tokens, depth), F32),
            pltpu.VMEM((tokens, depth), F32),
            pltpu.VMEM((tokens, chunk), BF16),
            pltpu.VMEM((tokens, width), BF16),
        ],
        compiler_params=pltpu.CompilerParams(
            vmem_limit_bytes=VMEM_LIMIT, dimension_semantics=("arbitrary",)
        ),
        name="feed_forward",
    )(o, x, dy, wo, gain, gu, wd)


class Plan:
    def __init__(self, fsdp, ctx):
        self.fsdp, self.ctx = fsdp, ctx
        self.lines = fsdp // 2
        self.across = math.isqrt(self.lines)
        self.along = self.lines // self.across
        self.half = ctx // 2
        self.f = lax.axis_index("fsdp")
        self.c = lax.axis_index("ctx")
        self.core = lax.rem(self.f, 2)
        self.line = self.f // 2
        self.a = self.line // self.along
        self.b = lax.rem(self.line, self.along)
        self.home = self.c // self.half
        self.started = []

    def barrier(self):
        sem = pltpu.get_barrier_semaphore()
        count = 0
        for step in range(1, self.fsdp):
            dev = (lax.rem(self.f + step, self.fsdp), self.c)
            pl.semaphore_signal(sem, inc=1, device_id=dev, device_id_type=MESH)
            count += 1
        for step in range(1, self.ctx):
            for core in range(2):
                dev = (self.line * 2 + core, lax.rem(self.c + step, self.ctx))
                pl.semaphore_signal(sem, inc=1, device_id=dev, device_id_type=MESH)
                count += 1
        pl.semaphore_wait(sem, count)

    def when(self, cond, act):
        if cond is True:
            act()
        else:
            pl.when(cond)(act)

    def send(self, src, dst, send_sem, recv_sem, dev, cond=True):
        def copy():
            return pltpu.make_async_remote_copy(
                src_ref=src, dst_ref=dst, send_sem=send_sem, recv_sem=recv_sem,
                device_id=dev, device_id_type=MESH,
            )

        self.when(cond, lambda: copy().start())
        self.started.append((cond, lambda: copy().wait_send()))

    def keep(self, src, dst, sem, cond=True):
        self.when(cond, lambda: pltpu.make_async_copy(src, dst, sem).start())

    def arrive(self, dst, sem, cond=True):
        self.when(cond, lambda: pltpu.make_async_copy(dst, dst, sem).wait())

    def drain(self):
        for cond, act in self.started:
            self.when(cond, act)
        self.started = []


def both(*conds):
    out = True
    for cond in conds:
        if cond is not True:
            out = cond if out is True else jnp.logical_and(out, cond)
    return out


def gather_kernel(
    fsdp, ctx,
    x, vf, wqkv, wo, gu, wd, gains,
    xs, vs, wq, wqh, wos, gus, wds, gs,
    x_sem, x_out, v_sem, v_out, q_sem, q_out, h_sem, g_sem, g_out, w_sem, w_z, w_p, w_s,
):
    plan = Plan(fsdp, ctx)
    f, c, core, line, home, half = plan.f, plan.c, plan.core, plan.line, plan.home, plan.half
    a, b, across, along, lines = plan.a, plan.b, plan.across, plan.along, plan.lines
    cols = vs.shape[2]
    owner = core == home
    sibling = (line * 2 + 1 - core, c)
    plan.barrier()

    def spread_x(j, below, above, cond):
        src, dst = xs.at[j], xs.at[j]
        if below:
            plan.send(src, dst, x_out.at[0, j], x_sem.at[j], (f, c - 1), both(cond, c > home * half))
        if above:
            plan.send(
                src, dst, x_out.at[1, j], x_sem.at[j], (f, c + 1),
                both(cond, c < home * half + half - 1),
            )
        plan.send(src, dst, x_out.at[2, j], x_sem.at[j], sibling, cond)

    away = jnp.logical_not(owner)
    entry = jnp.where(core == 0, half - 1, half)
    plan.send(x, xs.at[c], x_out.at[0, c], x_sem.at[c], (f, entry), away)
    plan.send(x, xs.at[c], x_out.at[0, c], x_sem.at[c], (f, c - 1), both(owner, c > home * half))
    plan.send(
        x, xs.at[c], x_out.at[1, c], x_sem.at[c], (f, c + 1),
        both(owner, c < home * half + half - 1),
    )
    plan.send(x, xs.at[c], x_out.at[2, c], x_sem.at[c], sibling, owner)
    plan.keep(x, xs.at[c], x_sem.at[c], owner)

    across_ctx = lax.rem(c + half, ctx)
    plan.send(wqkv, wqh, h_sem.at[0], h_sem.at[1], (f, across_ctx))

    def items(row, j):
        return (
            wos.at[row, :, pl.ds(pl.multiple_of(j * wo.shape[1], wo.shape[1]), wo.shape[1])],
            gus.at[j, row],
            wds.at[row, :, pl.ds(pl.multiple_of(j * wd.shape[1], wd.shape[1]), wd.shape[1])],
        )

    def spread_w(srcs, j, cond, up, down):
        dsts = items(f, j)
        for i in range(3):
            if up:
                plan.send(
                    srcs[i], dsts[i], w_z.at[i, 0, j], w_sem.at[i, f, j], (f, c + 1),
                    both(cond, c < ctx - 1),
                )
            if down:
                plan.send(
                    srcs[i], dsts[i], w_z.at[i, 1, j], w_sem.at[i, f, j], (f, c - 1),
                    both(cond, c > 0),
                )
        for i in range(3):
            for step in range(1, across):
                dev = ((lax.rem(a + step, across) * along + b) * 2 + core, c)
                plan.send(
                    srcs[i], dsts[i], w_p.at[i, step - 1, line, j], w_sem.at[i, f, j], dev, cond
                )
            for step in range(1, along):
                dev = ((a * along + lax.rem(b + step, along)) * 2 + core, c)
                plan.send(
                    srcs[i], dsts[i], w_p.at[i, across + step - 2, line, j], w_sem.at[i, f, j],
                    dev, cond,
                )
            plan.send(srcs[i], dsts[i], w_s.at[i, line, j], w_sem.at[i, f, j], sibling, cond)

    for step in range(1, fsdp):
        dev = (lax.rem(f + step, fsdp), c)
        plan.send(gains, gs.at[f], g_out.at[step - 1], g_sem.at[f], dev)
    plan.keep(gains, gs.at[f], g_sem.at[f])

    own = (wo, gu, wd)
    spread_w(own, c, True, True, True)
    for src, dst, i in zip(own, items(f, c), range(3)):
        plan.keep(src, dst, w_sem.at[i, f, c])

    for at in range(lines):
        dev = (at * 2, c)
        plan.send(wqkv, wq.at[f], q_out.at[0, at], q_sem.at[f], dev, jnp.logical_not(f == at * 2))
    plan.keep(wqkv, wq.at[f], q_sem.at[f], core == 0)

    for i in range(half):
        for k in range(2):
            to = core * half + i
            rank = lax.rem(to + k * half, ctx)
            src = vf.at[:, pl.ds(pl.multiple_of(rank * cols, cols), cols)]
            mine = both(owner, c == to, core == k)
            plan.send(
                src, vs.at[c], v_out.at[i, k], v_sem.at[c], (line * 2 + k, to),
                jnp.logical_not(mine),
            )
            plan.keep(src, vs.at[c], v_sem.at[c], mine)

    pltpu.make_async_copy(wqh, wqh, h_sem.at[1]).wait()
    for at in range(lines):
        dev = (at * 2 + 1, c)
        plan.send(
            wqh, wq.at[f], q_out.at[1, at], q_sem.at[f], dev, jnp.logical_not(f == at * 2 + 1)
        )
    plan.keep(wqh, wq.at[f], q_sem.at[f], core == 1)

    for dist in range(1, ctx):
        for side in range(2):
            j = c - dist if side == 0 else c + dist
            there = j >= 0 if side == 0 else j < ctx
            at = jnp.clip(j, 0, ctx - 1)
            cond = both(owner, there)
            plan.arrive(xs.at[at], x_sem.at[at], cond)
            spread_x(at, side == 1, side == 0, cond)
        for side in range(2):
            j = c - dist if side == 0 else c + dist
            there = j >= 0 if side == 0 else j < ctx
            at = jnp.clip(j, 0, ctx - 1)
            dsts = items(f, at)
            for i in range(3):
                plan.arrive(dsts[i], w_sem.at[i, f, at], there)
            spread_w(dsts, at, there, side == 0, side == 1)

    for dist in range(ctx):
        for side in range(2 if dist else 1):
            j = c - dist if side == 0 else c + dist
            there = j >= 0 if side == 0 else j < ctx
            at = jnp.clip(j, 0, ctx - 1)
            first = at < half
            for step in range(1, across):
                from_line = lax.rem(a + across - step, across) * along + b
                row = from_line * 2 + core
                dsts = items(row, at)
                for i in range(3):
                    plan.arrive(dsts[i], w_sem.at[i, row, at], there)
                for i in range(3):
                    for hop in range(1, along):
                        dev = ((a * along + lax.rem(b + hop, along)) * 2 + core, c)
                        plan.send(
                            dsts[i], dsts[i], w_p.at[i, across + hop - 2, from_line, at],
                            w_sem.at[i, row, at], dev, both(there, first),
                        )
                    plan.send(
                        dsts[i], dsts[i], w_s.at[i, from_line, at], w_sem.at[i, row, at], sibling,
                        there,
                    )
            for step in range(1, along):
                from_line = a * along + lax.rem(b + along - step, along)
                row = from_line * 2 + core
                dsts = items(row, at)
                for i in range(3):
                    plan.arrive(dsts[i], w_sem.at[i, row, at], there)
                for i in range(3):
                    for hop in range(1, across):
                        dev = ((lax.rem(a + hop, across) * along + b) * 2 + core, c)
                        plan.send(
                            dsts[i], dsts[i], w_p.at[i, hop - 1, from_line, at],
                            w_sem.at[i, row, at], dev, both(there, jnp.logical_not(first)),
                        )
                    plan.send(
                        dsts[i], dsts[i], w_s.at[i, from_line, at], w_sem.at[i, row, at], sibling,
                        there,
                    )
    for dist in range(ctx):
        for side in range(2 if dist else 1):
            j = c - dist if side == 0 else c + dist
            there = j >= 0 if side == 0 else j < ctx
            at = jnp.clip(j, 0, ctx - 1)
            for step in range(1, across):
                for hop in range(1, along):
                    from_line = lax.rem(a + step, across) * along + lax.rem(b + hop, along)
                    row = from_line * 2 + core
                    dsts = items(row, at)
                    for i in range(3):
                        plan.arrive(dsts[i], w_sem.at[i, row, at], there)
                        plan.send(
                            dsts[i], dsts[i], w_s.at[i, from_line, at], w_sem.at[i, row, at],
                            sibling, there,
                        )

    for i in range(3):
        plan.arrive(items(f, c)[i], w_sem.at[i, f, c])

    def far(at, carry):
        row = at * 2 + 1 - core
        for j in range(ctx):
            dsts = items(row, j)
            for i in range(3):
                plan.arrive(dsts[i], w_sem.at[i, row, j])
        return carry

    lax.fori_loop(0, lines, far, 0)
    for j in range(ctx):
        plan.arrive(xs.at[j], x_sem.at[j], both(jnp.logical_or(away, c == j)))
        plan.arrive(vs.at[j], v_sem.at[j])
    for row in range(fsdp):
        plan.arrive(wq.at[row], q_sem.at[row])
        plan.arrive(gs.at[row], g_sem.at[row])
    plan.drain()


def gather(mesh, x, vf, wqkv, wo, gu, wd, gains):
    fsdp, ctx = mesh.shape["fsdp"], mesh.shape["ctx"]
    tokens, depth = x.shape
    cols = depth // ctx
    lines = fsdp // 2
    across = math.isqrt(lines)
    peers = max(across - 1 + lines // across - 1, 1)
    anywhere = pl.BlockSpec(memory_space=pl.ANY)
    dma = pltpu.SemaphoreType.DMA
    return pl.pallas_call(
        functools.partial(gather_kernel, fsdp, ctx),
        out_shape=(
            jax.ShapeDtypeStruct((ctx, tokens, depth), BF16),
            jax.ShapeDtypeStruct((ctx, tokens, cols), BF16),
            jax.ShapeDtypeStruct((fsdp,) + wqkv.shape, BF16),
            jax.ShapeDtypeStruct(wqkv.shape, BF16),
            jax.ShapeDtypeStruct((fsdp, wo.shape[0], depth), BF16),
            jax.ShapeDtypeStruct((ctx, fsdp) + gu.shape, BF16),
            jax.ShapeDtypeStruct((fsdp, wd.shape[0], depth), BF16),
            jax.ShapeDtypeStruct((fsdp,) + gains.shape, F32),
        ),
        in_specs=[anywhere] * 7,
        out_specs=[anywhere] * 8,
        scratch_shapes=[
            dma((ctx,)), dma((3, ctx)), dma((ctx,)), dma((ctx // 2, 2)),
            dma((fsdp,)), dma((2, lines)), dma((2,)), dma((fsdp,)), dma((fsdp,)),
            dma((3, fsdp, ctx)), dma((3, 2, ctx)), dma((3, peers, lines, ctx)), dma((3, lines, ctx)),
        ],
        compiler_params=pltpu.CompilerParams(collective_id=0, has_side_effects=True),
        name="gather_all",
    )(x, vf, wqkv, wo, gu, wd, gains)


def trade_kernel(fsdp, ctx, inward, src_ref, dst_ref, recv, sent):
    plan = Plan(fsdp, ctx)
    f, c, core, line, home, half = plan.f, plan.c, plan.core, plan.line, plan.home, plan.half
    cols = (src_ref if inward else dst_ref).shape[2]
    plan.barrier()

    def band(rank):
        return pl.ds(pl.multiple_of(rank * cols, cols), cols)

    if inward:
        rank = lax.rem(c + core * half, ctx)
        for step in range(ctx):
            j = lax.rem(c + step, ctx)
            src, dst = src_ref.at[j], dst_ref.at[:, band(rank)]
            dev = (line * 2 + home, j)
            mine = both(core == home) if step == 0 else False
            if step == 0:
                plan.keep(src, dst, recv.at[rank], mine)
                plan.send(src, dst, sent.at[j], recv.at[rank], dev, jnp.logical_not(mine))
            else:
                plan.send(src, dst, sent.at[j], recv.at[rank], dev)
        for rank in range(ctx):
            plan.arrive(dst_ref.at[:, band(rank)], recv.at[rank])
    else:
        for i in range(half):
            for k in range(2):
                to = core * half + i
                src = src_ref.at[:, band(lax.rem(to + k * half, ctx))]
                mine = both(core == home, c == to, core == k)
                plan.send(
                    src, dst_ref.at[c], sent.at[i * 2 + k], recv.at[c], (line * 2 + k, to),
                    jnp.logical_not(mine),
                )
                plan.keep(src, dst_ref.at[c], recv.at[c], mine)
        for j in range(ctx):
            plan.arrive(dst_ref.at[j], recv.at[j])
    plan.drain()


def trade(mesh, array, inward, ident):
    fsdp, ctx = mesh.shape["fsdp"], mesh.shape["ctx"]
    if inward:
        shape = (array.shape[1], array.shape[2] * ctx)
    else:
        shape = (ctx, array.shape[0], array.shape[1] // ctx)
    anywhere = pl.BlockSpec(memory_space=pl.ANY)
    return pl.pallas_call(
        functools.partial(trade_kernel, fsdp, ctx, inward),
        out_shape=jax.ShapeDtypeStruct(shape, BF16),
        in_specs=[anywhere],
        out_specs=anywhere,
        scratch_shapes=[pltpu.SemaphoreType.DMA((ctx,)), pltpu.SemaphoreType.DMA((ctx,))],
        compiler_params=pltpu.CompilerParams(collective_id=ident, has_side_effects=True),
        name="trade_in" if inward else "trade_out",
    )(array)


def fold_kernel(
    fsdp, ctx,
    part, dvm, out, vout,
    other, chain, summed,
    recv, sent, line_recv, line_sent, last, last_sent, v_recv, v_sent,
):
    plan = Plan(fsdp, ctx)
    f, c, core, line, home, half = plan.f, plan.c, plan.core, plan.line, plan.home, plan.half
    sibling = (line * 2 + 1 - core, c)
    low, high = home * half, home * half + half - 1
    plan.barrier()
    pairs = [jnp.where(home == 0, ctx - 2 - 2 * i, 2 * i) for i in range(half)]
    for i, base in enumerate(pairs):
        give = base + 1 - core
        plan.send(part.at[give], other.at[i], sent.at[i], recv.at[i], sibling)
    cols = dvm.shape[2]
    rank = lax.rem(c + core * half, ctx)
    for step in range(ctx):
        j = lax.rem(c + step, ctx)
        src = dvm.at[j]
        dst = vout.at[:, pl.ds(pl.multiple_of(rank * cols, cols), cols)]
        mine = core == home
        if step == 0:
            plan.keep(src, dst, v_recv.at[rank], mine)
        plan.send(
            src, dst, v_sent.at[step], v_recv.at[rank], (line * 2 + home, j),
            jnp.logical_not(mine) if step == 0 else True,
        )
    for i, base in enumerate(pairs):
        j = base + core
        plan.arrive(other.at[i], recv.at[i])
        def add(src, slot, i=i, j=j):
            def body(t, carry):
                at = pl.ds(pl.multiple_of(t * 128, 128), 128)
                summed[i, at, :] = (
                    part[j, at, :].astype(F32) + src[slot, at, :].astype(F32)
                ).astype(BF16)
                return carry

            lax.fori_loop(0, part.shape[1] // 128, body, 0)

        def more(slot, i=i):
            def body(t, carry):
                at = pl.ds(pl.multiple_of(t * 128, 128), 128)
                summed[i, at, :] = (
                    summed[i, at, :].astype(F32) + chain[slot, i, at, :].astype(F32)
                ).astype(BF16)
                return carry

            lax.fori_loop(0, part.shape[1] // 128, body, 0)

        add(other, i)
        top = jnp.minimum(j, high)
        bottom = jnp.maximum(j, low)
        from_below = both(c > low, c <= top)
        from_above = both(c < high, c >= bottom)

        @pl.when(from_below)
        def _(i=i):
            plan.arrive(chain.at[0, i], line_recv.at[0, i])
            more(0)

        @pl.when(from_above)
        def _(i=i):
            plan.arrive(chain.at[1, i], line_recv.at[1, i])
            more(1)

        plan.send(summed.at[i], chain.at[0, i], line_sent.at[0, i], line_recv.at[0, i], (f, c + 1), c < top)
        plan.send(summed.at[i], chain.at[1, i], line_sent.at[1, i], line_recv.at[1, i], (f, c - 1), c > bottom)
        end = jnp.clip(j, low, high)
        mine = both(c == end, j == c, core == home)
        plan.send(
            summed.at[i], out, last_sent.at[i], last.at[0], (line * 2 + home, j),
            both(c == end, jnp.logical_not(mine)),
        )
        plan.keep(summed.at[i], out, last.at[0], mine)
    plan.arrive(out, last.at[0])
    for at in range(ctx):
        plan.arrive(vout.at[:, pl.ds(at * cols, cols)], v_recv.at[at])
    plan.drain()


def fold(mesh, part, dvm, ident):
    fsdp, ctx = mesh.shape["fsdp"], mesh.shape["ctx"]
    _, tokens, depth = part.shape
    half = ctx // 2
    dma = pltpu.SemaphoreType.DMA
    return pl.pallas_call(
        functools.partial(fold_kernel, fsdp, ctx),
        out_shape=(
            jax.ShapeDtypeStruct((tokens, depth), BF16),
            jax.ShapeDtypeStruct((tokens, depth), BF16),
        ),
        in_specs=[
            pl.BlockSpec(memory_space=pltpu.VMEM),
            pl.BlockSpec(memory_space=pl.ANY),
        ],
        out_specs=(
            pl.BlockSpec(memory_space=pltpu.VMEM),
            pl.BlockSpec(memory_space=pl.ANY),
        ),
        scratch_shapes=[
            pltpu.VMEM((half, tokens, depth), BF16),
            pltpu.VMEM((2, half, tokens, depth), BF16),
            pltpu.VMEM((half, tokens, depth), BF16),
            dma((half,)), dma((half,)), dma((2, half)), dma((2, half)), dma((1,)), dma((half,)),
            dma((ctx,)), dma((ctx,)),
        ],
        compiler_params=pltpu.CompilerParams(
            collective_id=ident, has_side_effects=True, vmem_limit_bytes=VMEM_LIMIT
        ),
        name="fold_tokens",
    )(part, dvm)


def documents(length_row, places):
    doc_ends = jnp.cumsum(length_row)
    doc_starts = doc_ends - length_row
    owner_ids = jnp.sum((places[:, None] >= doc_ends[None, :]).astype(jnp.int32), axis=1)
    chosen = owner_ids[:, None] == jnp.arange(length_row.shape[0], dtype=jnp.int32)[None, :]
    first_place = jnp.sum(jnp.where(chosen, doc_starts[None, :], 0), axis=1)
    return first_place


def tables(length_row, group):
    places = jnp.arange(group, dtype=jnp.int32)
    first = documents(length_row, places)
    half = HEAD // 2
    frequency = jnp.exp(jnp.arange(half).astype(F32) * (-2.0 * math.log(THETA) / HEAD))
    angles = (places - first).astype(F32)[:, None] * frequency[None, :]
    cos, sin = jnp.cos(angles), jnp.sin(angles)
    return (
        jnp.concatenate([cos] * 4, axis=1),
        jnp.concatenate([-sin, sin] * 2, axis=1),
        first[None, :],
    )


def pick(array, index, axis):
    return lax.dynamic_index_in_dim(array, index, axis, keepdims=False)


def add_low(*parts):
    total = parts[0].astype(F32)
    for part in parts[1:]:
        total = total + part.astype(F32)
    return total


def sum_over(array, axis_name, axis, position, size, perm):
    parts = [pick(array, position, axis)]
    for hop in range(1, size):
        out = pick(array, lax.rem(position + hop, size), axis)
        parts.append(lax.ppermute(out, axis_name, perm(hop)))
    return add_low(*parts)


def reduce_shards(mesh, grads):
    fsdp, ctx = mesh.shape["fsdp"], mesh.shape["ctx"]
    lines = fsdp // 2
    across = math.isqrt(lines)
    along = lines // across
    f, c = lax.axis_index("fsdp"), lax.axis_index("ctx")
    core, line = lax.rem(f, 2), f // 2
    a, b = line // along, lax.rem(line, along)

    def number(aa, bb, kk):
        return (aa * along + bb) * 2 + kk

    def over_core(hop):
        return [(i, i ^ 1) for i in range(fsdp)]

    def over_along(hop):
        return [
            (number(aa, bb, kk), number(aa, (bb + hop) % along, kk))
            for aa in range(across) for bb in range(along) for kk in range(2)
        ]

    def over_across(hop):
        return [
            (number(aa, bb, kk), number((aa + hop) % across, bb, kk))
            for aa in range(across) for bb in range(along) for kk in range(2)
        ]

    def over_ctx(hop):
        return [(i, (i + hop) % ctx) for i in range(ctx)]

    out = []
    for grad in grads:
        near = sum_over(grad, "fsdp", 2, core, 2, over_core).astype(BF16)
        half = ctx // 2
        low = sum_over(near[:, :, :half], "fsdp", 1, b, along, over_along).astype(BF16)
        low = sum_over(low, "fsdp", 0, a, across, over_across).astype(BF16)
        high = sum_over(near[:, :, half:], "fsdp", 0, a, across, over_across).astype(BF16)
        high = sum_over(high, "fsdp", 0, b, along, over_along).astype(BF16)
        out.append(
            sum_over(jnp.concatenate([low, high], axis=0), "ctx", 0, c, ctx, over_ctx)
        )
    return out


def reduce_heads(mesh, grad):
    fsdp, ctx = mesh.shape["fsdp"], mesh.shape["ctx"]
    lines = fsdp // 2
    f, c = lax.axis_index("fsdp"), lax.axis_index("ctx")
    core, line = lax.rem(f, 2), f // 2

    def over_lines(hop):
        return [
            (at * 2 + k, ((at + hop) % lines) * 2 + k) for at in range(lines) for k in range(2)
        ]

    summed = sum_over(grad, "fsdp", 0, line, lines, over_lines).astype(BF16)
    half = ctx // 2
    pairs = []
    for at in range(lines):
        for z in range(ctx):
            far = (z + half) % ctx
            pairs.append(((at * 2) * ctx + z, (at * 2 + 1) * ctx + z))
            pairs.append(((at * 2 + 1) * ctx + z, (at * 2) * ctx + far))
    other = lax.ppermute(pick(summed, 1 - core, 0), ("fsdp", "ctx"), pairs)
    mine = pick(summed, core, 0)
    return other, mine, half


def reduce_heads_final(mesh, grad):
    fsdp, ctx = mesh.shape["fsdp"], mesh.shape["ctx"]
    lines, half = fsdp // 2, ctx // 2
    other, mine, _ = reduce_heads(mesh, grad)
    core = lax.rem(lax.axis_index("fsdp"), 2)
    pairs = [((at * 2 + 1) * ctx + z, (at * 2 + 1) * ctx + (z + half) % ctx)
             for at in range(lines) for z in range(ctx)]
    moved = lax.ppermute(mine, ("fsdp", "ctx"), pairs)
    return other.astype(F32) + jnp.where(core == 0, mine, moved).astype(F32)


def layer(
    mesh, tokens, value_first, lengths, w_query, w_key, w_value, w_out, w_gate, w_up, w_down,
    gain_attn, gain_ffn, out_grad, value_grad,
):
    fsdp, ctx = mesh.shape["fsdp"], mesh.shape["ctx"]
    lines = fsdp // 2
    across = math.isqrt(lines)
    along = lines // across
    count, depth = tokens.shape
    group = count * ctx
    cols = depth // ctx
    rows = depth // fsdp
    f, c = lax.axis_index("fsdp"), lax.axis_index("ctx")
    core = lax.rem(f, 2)
    home = c // (ctx // 2)

    wqkv = jnp.concatenate([w_query, w_key, w_value], axis=1).astype(BF16)
    gu = jnp.concatenate([w_gate, w_up], axis=1).astype(BF16)
    gains = jnp.stack([gain_attn, gain_ffn]).astype(BF16).astype(F32)
    gains = lax.dynamic_update_slice(
        jnp.zeros((8, depth), F32), gains, (jnp.int32(0), (f * rows).astype(jnp.int32))
    )
    other_lengths = lax.ppermute(lengths, "fsdp", [(i, i ^ 1) for i in range(fsdp)])
    length_row = jnp.where(core == home, lengths, other_lengths)[0]
    cos_t, sin_t, first = tables(length_row, group)

    xs, vs, wq, _, wos, gus, wds, gs = gather(
        mesh, tokens, value_first, wqkv, w_out.astype(BF16), gu, w_down.astype(BF16), gains
    )
    gain_full = jnp.sum(gs, axis=0)
    gain_one, gain_two = gain_full[0:1], gain_full[1:2]
    xg = xs.reshape(group, depth)
    wq = wq.reshape(depth, 3 * cols)
    h1, q, k, vm, kt, out, att, lse = forward_attention(
        xg, vs.reshape(group, cols), wq, gain_one, cos_t, sin_t, first
    )
    attended = trade(mesh, out.reshape(ctx, count, cols), True, 1)
    result, dx2, d_out, g_wo, g_gu, g_wd, dg_two = feed_forward(
        attended, tokens, out_grad, wos.reshape(depth, depth), gain_two,
        gus.reshape(ctx, depth, gu.shape[1]), wds.reshape(-1, depth),
    )
    do = trade(mesh, d_out, False, 2).reshape(group, cols)
    part, dvm, g_qkv, dg_one = backward_attention(
        xg, h1, q, k, vm, kt, att, lse, do, wq, gain_one, cos_t, sin_t, first
    )
    folded, dvm_own = fold(
        mesh, part.reshape(ctx, count, depth), dvm.reshape(ctx, count, cols), 3
    )
    ff = w_gate.shape[1]
    rows_d = w_down.shape[0]
    g_wo, g_gu, g_wd = reduce_shards(
        mesh,
        (
            g_wo.reshape(across, along, 2, rows, ctx, cols).transpose(0, 1, 2, 4, 3, 5),
            g_gu.reshape(ctx, across, along, 2, rows, 2 * ff).transpose(1, 2, 3, 0, 4, 5),
            g_wd.reshape(across, along, 2, rows_d, ctx, cols).transpose(0, 1, 2, 4, 3, 5),
        ),
    )
    g_qkv = reduce_heads_final(mesh, g_qkv.reshape(lines, 2, rows, 3 * cols))
    gain_grads = jnp.stack([dg_one[0], dg_two[0]])
    gain_grads = lax.psum(
        lax.psum_scatter(gain_grads, "fsdp", scatter_dimension=1, tiled=True), "ctx"
    )
    return (
        result,
        dx2 + folded.astype(F32),
        value_grad + 0.5 * dvm_own.astype(F32),
        g_qkv[:, :cols],
        g_qkv[:, cols : 2 * cols],
        g_qkv[:, 2 * cols :],
        g_wo,
        g_gu[:, :ff],
        g_gu[:, ff:],
        g_wd,
        gain_grads[0],
        gain_grads[1],
    )


def solution(mesh):
    rows = P(("fsdp", "ctx"), None)
    shard = P("fsdp", "ctx")
    return jax.shard_map(
        functools.partial(layer, mesh),
        mesh=mesh,
        in_specs=(rows, rows, P("fsdp", None)) + (shard,) * 7 + (P("fsdp"),) * 2 + (rows, rows),
        out_specs=(rows, rows, rows) + (shard,) * 7 + (P("fsdp"),) * 2,
        check_vma=False,
    )
```

time: 1570 us -> 723 us (0.46)
  waiting for transfers between devices: 1150 us -> 116 us
  Pallas kernels: 0 us -> 440 us
  matrix products: 157 us -> 0 us
  blocking collectives: 87.4 us -> 8.37 us
  starting transfers between devices: 1.1 us -> 31.4 us
  other arithmetic: 58.8 us -> 35 us
  local copies, waits for them, and re-layouts: 79.9 us -> 63.8 us
    all_gather x12 -> x0, waiting for transfers between devices: 614 us -> none  [the longest x1 101 us: per_device(): lax.all_gather(rows_part[6], 'ctx', axis=1, tiled=True)]
    reduce_scatter x13 -> x0, waiting for transfers between devices: 497 us -> none  [the longest x1 235 us: per_device(): lax.psum_scatter(folded[1].astype(jnp.bfloat16), 'ctx', scatter_dimension...]
    pallas_call x0 -> x7, Pallas kernels: none -> 440 us  [the longest x1 140 us: gather(): pl.pallas_call(functools.partial(gather_kernel, fsdp, ctx), out_shape=(ja...]
    dot_general x28 -> x0, matrix products: 157 us -> none  [the longest x7 40.7 us: product(): return jnp.dot(left, right, preferred_element_type=jnp.float32)]
    ppermute x0 -> x30, waiting for transfers between devices: none -> 116 us  [the longest x27 107 us: sum_over(): parts.append(lax.ppermute(out, axis_name, perm(hop)))]
    all_gather x6 -> x0, blocking collectives: 62.6 us -> none  [the longest x1 12.5 us: per_device(): lax.all_gather(halves[2], 'fsdp', axis=0, tiled=True)]
    unnamed x29 -> x2, waiting for transfers between devices: 38.7 us -> 0.02 us
    ppermute x0 -> x30, starting transfers between devices: none -> 31.4 us  [the longest x27 29.7 us: sum_over(): parts.append(lax.ppermute(out, axis_name, perm(hop)))]
  transfers between devices with their start and end apart: 27 -> 31, of which waited for: 24 -> 13; matrix products, arithmetic and copies ran while one was open for 17% -> 10% of each run, Pallas kernels for 0% -> 44%
where the time goes in v1:
time: 723 us; the launch traced here: 709 us
  Pallas kernels  440 us (61%)
  waiting for transfers between devices  116 us (16%)
  local copies, waits for them, and re-layouts  63.8 us (9%)
  other arithmetic  35 us (5%)
  starting transfers between devices  31.4 us (4%)
  between operations  15.1 us (2%)
  blocking collectives  8.37 us (1%)
    pallas_call x1, Pallas kernels, gather(): pl.pallas_call(functools.partial(gather_kernel, fsdp, ctx), out_shape=(ja...  140 us
    ppermute x27, waiting for transfers between devices, sum_over(): parts.append(lax.ppermute(out, axis_name, perm(hop)))  107 us
    pallas_call x1, Pallas kernels, fold(): pl.pallas_call(functools.partial(fold_kernel, fsdp, ctx), out_shape=(jax....  78.7 us
    pallas_call x1, Pallas kernels, backward_attention(): pl.pallas_call(backward_kernel, out_shape=shapes, in_specs=[vmem] * 14, o...  69.6 us
    pallas_call x1, Pallas kernels, forward_attention(): pl.pallas_call(forward_kernel, out_shape=shapes, in_specs=[vmem] * 7, out...  56.9 us
    pallas_call x1, Pallas kernels, feed_forward(): pl.pallas_call(feed_kernel, grid=(steps,), out_shape=shapes, in_specs=[wh...  49 us
    pallas_call x2, Pallas kernels, trade(): pl.pallas_call(functools.partial(trade_kernel, fsdp, ctx, inward), out_sh...  46.1 us
    ppermute x27, starting transfers between devices, sum_over(): parts.append(lax.ppermute(out, axis_name, perm(hop)))  29.7 us
  transfers between devices with their start and end apart: 31, of which 13 were waited for; matrix products, arithmetic and copies ran while one was open for 10% of the time, Pallas kernels for 44%

profile of v1, /device:TPU:0, one launch (start us, length us, event | category | flops | bytes accessed | tf_op | source)
XLA Modules:
  0.0 709.4 jit_solution(769463900695150191)
XLA Ops:
  7.8 1.0 convert.48
  9.0 1.0 convert.49
  10.1 0.9 convert.45
  12.5 0.9 pad_maximum_fusion.2.gu
  14.6 139.5 %gather_all.1 = (bf16[4,512,1024]{2,1,0:T(8,128)(2,1)}, bf16[4,512,256]{2,1,0:T(8,128)(2,1)}, bf16[8,128,768]{2,1,0:T(8,128)(2,1)}, bf16[128,768]{1,0:T(8,128)(2...) custom-call(bf16[512,1024]{1,0:T(8,128)(2,1)} %x.3, ...), custom_call_target="tpu_custom_call" | custom-call | tf_op jit(solution)/shard_map/gather_all/pallas_call | solution.py:698
  154.2 1.0 reduce_sum.27
  156.2 3.7 fusion.28
  159.9 3.0 pad_maximum_fusion
  162.9 56.9 %attention_forward.1 = (bf16[2048,1024]{1,0:T(8,128)(2,1)}, bf16[2048,256]{1,0:T(8,128)(2,1)}, bf16[2048,256]{1,0:T(8,128)(2,1)}, bf16[2048,256]{1,0:T(8,128)(2,...) custom-call(bf16[2048,1024]{1,0:T(8,128)(2,1)} %bitcast.171, ...), custom_call_target="tpu_custom_call" | custom-call | tf_op jit(solution)/shard_map/attention_forward/pallas_call | solution.py:144
  219.8 21.8 %trade_in.1.o = bf16[512,1024]{1,0:T(8,128)(2,1)} custom-call(bf16[4,512,256]{2,1,0:T(8,128)(2,1)} %bitcast.188), custom_call_target="tpu_custom_call" | custom-call | tf_op jit(solution)/shard_map/trade_in/pallas_call | solution.py:768
  241.7 49.0 %feed_forward.1 = (bf16[512,1024]{1,0:T(8,128)(2,1)}, f32[512,1024]{1,0:T(8,128)}, bf16[512,1024]{1,0:T(8,128)(2,1)}, bf16[1024,1024]{1,0:T(8,128)(2,1)}, bf16[4...) custom-call(bf16[512,1024]{1,0:T(8,128)(2,1)} %trade_in.1.o, bf16[512,1024]{1,0:T(8,128)(2,1)} %x.3, ...), custom_call_target="tpu_custom_call" | custom-call | tf_op jit(solution)/shard_map/feed_forward/pallas_call | solution.py:382
  290.6 10.1 %constant_dynamic-slice_fusion.2 = (bf16[4,2,2,1,128,1408]{5,4,3,2,1,0:T(8,128)(2,1)}, bf16[4,2,2,1,128,1408]{5,4,3,2,1,0:T(8,128)(2,1)}) fusion(bf16[4,2,2,2,128,1408]{5,4,3,2,1,0:T(8,128)(2,1)} %bitcast.174, s32[]{:T(128)S(6)} %select_n.144, s32[]{:T(128)S(6)} %select_n.142), kind=kLoop, calls=%fused_computation.126 | loop fusion | bytes 23068680 | tf_op jit(solution)/shard_map/dynamic-slice.3
  300.7 8.3 %copy.64 = bf16[4,2,2,1,128,1408]{4,5,0,2,1,3:T(8,128)(2,1)} copy(bf16[4,2,2,1,128,1408]{5,4,3,2,1,0:T(8,128)(2,1)} %get-tuple-element.68) | data formatting | bytes 11534336
  309.0 1.4 collective-permute-start.14
  310.4 24.3 %trade_out.1 = bf16[4,512,256]{2,1,0:T(8,128)(2,1)} custom-call(bf16[512,1024]{1,0:T(8,128)(2,1)} %get-tuple-element.57.src_ref), custom_call_target="tpu_custom_call" | custom-call | tf_op jit(solution)/shard_map/trade_out/pallas_call | solution.py:768
  334.7 69.6 %attention_backward.1 = (bf16[2048,1024]{1,0:T(8,128)(2,1)}, bf16[2048,256]{1,0:T(8,128)(2,1)}, bf16[1024,768]{1,0:T(8,128)(2,1)}, f32[8,1024]{1,0:T(8,128)}) custom-call(bf16[2048,1024]{1,0:T(8,128)(2,1)} %bitcast.172, bf16[2048,1024]{1,0:T(8,128)(2,1)} %get-tuple-element.50.h1, bf16[2048,256]{1,0:T(8,128)(2,1)} %get-tuple-element.51.q, ...), custom_call_target="tpu_custom_call" | custom-call | tf_op jit(solution)/shard_map/attention_backward/pallas_call | solution.py:264
  405.8 1.0 copy.59
  406.9 3.5 reshape.141
  410.5 1.7 constant_dynamic-slice_fusion.5
  412.2 1.2 copy.72
  413.4 2.6 collective-permute-start.6
  416.0 0.9 dynamic-slice_bitcast_fusion.8
  417.0 1.5 collective-permute-start.1
  419.0 1.4 collective-permute-start.3
  420.4 78.7 %fold_tokens.1 = (bf16[512,1024]{1,0:T(8,128)(2,1)}, bf16[512,1024]{1,0:T(8,128)(2,1)}) custom-call(bf16[4,512,1024]{2,1,0:T(8,128)(2,1)} %bitcast.179, bf16[4,512,256]{2,1,0:T(8,128)(2,1)} %bitcast.186), custom_call_target="tpu_custom_call" | custom-call | tf_op jit(solution)/shard_map/fold_tokens/pallas_call | solution.py:866
  499.2 3.1 convert_add_fusion.2
  502.4 1.6 multiply_add_fusion
  504.0 10.5 %reshape.143 = bf16[2,2,2,352,4,256]{5,4,3,2,1,0:T(4,128)(2,1)} reshape(bf16[2816,1024]{1,0:T(8,128)(2,1)} %get-tuple-element.65) | data formatting | bytes 11534336 | tf_op jit(solution)/shard_map/reshape | solution.py:1070
  514.5 4.7 constant_dynamic-slice_fusion.1
  519.2 2.0 copy.71
  521.2 8.3 %copy.63 = bf16[4,2,2,1,128,1408]{4,5,0,2,1,3:T(8,128)(2,1)} copy(bf16[4,2,2,1,128,1408]{5,4,3,2,1,0:T(8,128)(2,1)} %get-tuple-element.69) | data formatting | bytes 11534336
  529.5 0.9 copy.60
  530.4 8.4 %psum.7 = f32[2,128]{1,0:T(2,128)S(1)} all-reduce(f32[2,128]{1,0:T(2,128)S(1)} %copy.60), channel_id=1, replica_groups=mesh['fsdp'=8,'ctx'=4] {'ctx'}, use_global_device_ids=true, to_apply=%region_5.6 | all-reduce | flops 256 | bytes 2048 | tf_op jit(solution)/shard_map/psum | solution.py:1075
  538.9 1.6 fusion.11
  542.2 8.6 %collective-permute-done.4 = bf16[128,768]{1,0:T(8,128)(2,1)S(1)} collective-permute-done((bf16[128,768]{1,0:T(8,128)(2,1)S(1)}, bf16[128,768]{1,0:T(8,128)(2,1)S(1)}, u32[]{:S(2)}, u32[]{:S(2)}) %collective-permute-start.4) | collective-permute-done | bytes 196640 | tf_op jit(solution)/shard_map/ppermute | solution.py:999
  550.9 1.5 fusion.4
  552.5 1.3 collective-permute-start.9
  555.5 5.4 collective-permute-done.9
  561.0 1.0 collective-permute-start.10
  561.9 1.3 collective-permute-done.7
  564.2 3.1 collective-permute-done.10
  567.3 1.9 collective-permute-done.8
  570.4 0.9 dynamic-slice_bitcast_fusion.2
  572.3 6.7 fusion
  579.0 3.2 fusion.51
  582.3 1.2 collective-permute-start.17
  584.9 5.8 collective-permute-done.25
  590.7 1.3 fusion.5
  592.1 0.9 collective-permute-start.15
  593.0 9.7 %collective-permute-done.23 = bf16[2,2,352,256]{3,2,1,0:T(8,128)(2,1)S(1)} collective-permute-done((bf16[2,2,352,256]{3,2,1,0:T(8,128)(2,1)S(1)}, bf16[2,2,352,256]{3,2,1,0:T(8,128)(2,1)S(1)}, u32[]{:S(2)}, u32[]{:S(2)}) %collective-permute-start.23) | collective-permute-done | bytes 720928 | tf_op jit(solution)/shard_map/ppermute | solution.py:932
  603.7 35.7 %collective-permute-done.26 = bf16[2,352,256]{2,1,0:T(8,128)(2,1)S(1)} collective-permute-done((bf16[2,352,256]{2,1,0:T(8,128)(2,1)S(1)}, bf16[2,352,256]{2,1,0:T(8,128)(2,1)S(1)}, u32[]{:S(2)}, u32[]{:S(2)}) %collective-permute-start.26) | collective-permute-done | bytes 360480 | tf_op jit(solution)/shard_map/ppermute | solution.py:932
  639.5 1.3 collective-permute-start.24
  641.2 0.9 collective-permute-start.18
  642.5 5.6 collective-permute-done.24
  648.1 1.4 collective-permute-start.16
  649.9 7.6 %collective-permute-done.18 = bf16[2,128,1408]{1,2,0:T(8,128)(2,1)S(1)} collective-permute-done((bf16[2,128,1408]{1,2,0:T(8,128)(2,1)S(1)}, bf16[2,128,1408]{1,2,0:T(8,128)(2,1)S(1)}, u32[]{:S(2)}, u32[]{:S(2)}) %collective-permute-start.18) | collective-permute-done | bytes 720928 | tf_op jit(solution)/shard_map/ppermute | solution.py:932
  657.5 1.7 collective-permute-start.27
  659.4 4.1 collective-permute-done.16
  664.1 4.1 collective-permute-start.29
  669.1 3.0 collective-permute-start.21
  672.9 13.3 %collective-permute-done.28 = bf16[352,256]{1,0:T(8,128)(2,1)S(1)} collective-permute-done((bf16[352,256]{1,0:T(8,128)(2,1)S(1)}, bf16[352,256]{1,0:T(8,128)(2,1)S(1)}, u32[]{:S(2)}, u32[]{:S(2)}) %collective-permute-start.28) | collective-permute-done | bytes 180256 | tf_op jit(solution)/shard_map/ppermute | solution.py:932
  686.2 0.9 fusion.27
  687.1 13.8 %collective-permute-done.20 = bf16[128,1408]{0,1:T(8,128)(2,1)S(1)} collective-permute-done((bf16[128,1408]{0,1:T(8,128)(2,1)S(1)}, bf16[128,1408]{0,1:T(8,128)(2,1)S(1)}, u32[]{:S(2)}, u32[]{:S(2)}) %collective-permute-start.20) | collective-permute-done | bytes 360480 | tf_op jit(solution)/shard_map/ppermute | solution.py:932
  701.2 0.9 fusion.54
  (124 shorter events, 19.9 us)
Async XLA Ops:
  7.2 3.9 copy-start.8
  7.2 3.9 copy-start.9
  7.2 3.9 copy-start.5
  7.2 4.6 copy-start.10
  7.2 5.2 copy-start.13
  7.2 5.2 copy-start.12
  7.2 522.3 %reduce-scatter.4.cloned.1.call-start = ((), (), s32[]{:S(2)}) async-start(), calls=%async_computation.1 | async-start | bytes 589824
  7.3 148.5 %collective-permute-start = (s32[1,4]{1,0:T(1,128)}, s32[1,4]{1,0:T(1,128)S(1)}, u32[]{:S(2)}, u32[]{:S(2)}) collective-permute-start(s32[1,4]{1,0:T(1,128)} %param.16), channel_id=1, source_target_pairs={{0,4},{4,0},{8,12},{12,8},{16,20},{20,16},{24,28},{28,24},{1,5},{5... | collective-permute-start | bytes 56 | tf_op jit(solution)/shard_map/ppermute | solution.py:1037
  12.5 143.3 %copy-start.11 = (s32[1,4]{1,0:T(1,128)S(1)}, s32[1,4]{1,0:T(1,128)}, u32[]{:S(2)}) copy-start(s32[1,4]{1,0:T(1,128)} %param.16) | copy-start | bytes 52
  14.0 0.6 copy-start.7
  156.2 6.8 copy-start.6
  309.0 263.1 %collective-permute-start.14 = (bf16[2,2,4,128,1408]{3,4,2,1,0:T(8,128)(2,1)}, bf16[2,2,4,128,1408]{3,4,2,1,0:T(8,128)(2,1)}, u32[]{:S(2)}, u32[]{:S(2)}) collective-permute-start(bf16[2,2,4,128,1408]{3,4,2,1,0:T(8,128)(2,1)} %bitcast.177), channel_id=1, source_target_pairs={{0,4},{4,0},{8,12},{12,8},{16,20},{20,16},{24,28},{28,24},{1,5},{5... | collective-permute-start | bytes 17301512 | tf_op jit(solution)/shard_map/ppermute | solution.py:932
  412.2 3.8 copy-start.3
  413.4 137.6 %collective-permute-start.6 = (bf16[2,2,4,128,256]{4,3,2,1,0:T(8,128)(2,1)}, bf16[2,2,4,128,256]{4,3,2,1,0:T(8,128)(2,1)}, u32[]{:S(2)}, u32[]{:S(2)}) collective-permute-start(bf16[2,2,4,128,256]{4,3,2,1,0:T(8,128)(2,1)} %bitcast.168), channel_id=1, source_target_pairs={{0,4},{4,0},{8,12},{12,8},{16,20},{20,16},{24,28},{28,24},{1,5},{5... | collective-permute-start | bytes 3145736 | tf_op jit(solution)/shard_map/ppermute | solution.py:932
  417.0 121.9 %collective-permute-start.1 = (bf16[2,128,768]{2,1,0:T(8,128)(2,1)}, bf16[2,128,768]{2,1,0:T(8,128)(2,1)}, u32[]{:S(2)}, u32[]{:S(2)}) collective-permute-start(bf16[2,128,768]{2,1,0:T(8,128)(2,1)} %get-tuple-element.78), channel_id=1, source_target_pairs={{0,8},{4,12},{8,16},{12,20},{16,24},{20,28},{24,0},{28,4},{1,9},{5... | collective-permute-start | bytes 1179656 | tf_op jit(solution)/shard_map/ppermute | solution.py:932
  418.5 120.4 %collective-permute-start.2 = (bf16[2,128,768]{2,1,0:T(8,128)(2,1)}, bf16[2,128,768]{2,1,0:T(8,128)(2,1)}, u32[]{:S(2)}, u32[]{:S(2)}) collective-permute-start(bf16[2,128,768]{2,1,0:T(8,128)(2,1)} %get-tuple-element.80), channel_id=1, source_target_pairs={{0,16},{4,20},{8,24},{12,28},{16,0},{20,4},{24,8},{28,12},{1,17},{... | collective-permute-start | bytes 1179656 | tf_op jit(solution)/shard_map/ppermute | solution.py:932
  419.0 119.9 %collective-permute-start.3 = (bf16[2,128,768]{2,1,0:T(8,128)(2,1)S(1)}, bf16[2,128,768]{2,1,0:T(8,128)(2,1)}, u32[]{:S(2)}, u32[]{:S(2)}) collective-permute-start(bf16[2,128,768]{2,1,0:T(8,128)(2,1)S(1)} %get-tuple-element.79), channel_id=1, source_target_pairs={{0,24},{4,28},{8,0},{12,4},{16,8},{20,12},{24,16},{28,20},{1,25},{... | collective-permute-start | bytes 1179656 | tf_op jit(solution)/shard_map/ppermute | solution.py:932
  420.4 78.7 %copy-start.2 = (f32[512,1024]{1,0:T(8,128)S(1)}, f32[512,1024]{1,0:T(8,128)}, u32[]{:S(2)}) copy-start(f32[512,1024]{1,0:T(8,128)} %get-tuple-element.49) | copy-start | bytes 6291460
  499.2 3.2 copy-start.1
  499.2 3.2 copy-start.4
  538.8 12.1 %copy-start = (bf16[2,2,1,128,4,256]{5,4,3,2,1,0:T(4,128)(2,1)S(1)}, bf16[2,2,1,128,4,256]{5,4,3,2,1,0:T(4,128)(2,1)}, u32[]{:S(2)}) copy-start(bf16[2,2,1,128,4,256]{5,4,3,2,1,0:T(4,128)(2,1)} %get-tuple-element.76) | copy-start | bytes 3145732
  538.8 30.5 %collective-permute-start.22 = (bf16[2,2,4,352,256]{4,3,2,1,0:T(8,128)(2,1)}, bf16[2,2,4,352,256]{4,3,2,1,0:T(8,128)(2,1)S(1)}, u32[]{:S(2)}, u32[]{:S(2)}) collective-permute-start(bf16[2,2,4,352,256]{4,3,2,1,0:T(8,128)(2,1)} %bitcast.181), channel_id=1, source_target_pairs={{0,4},{4,0},{8,12},{12,8},{16,20},{20,16},{24,28},{28,24},{1,5},{5... | collective-permute-start | bytes 8650760 | tf_op jit(solution)/shard_map/ppermute | solution.py:932
  540.6 10.3 %collective-permute-start.4 = (bf16[128,768]{1,0:T(8,128)(2,1)S(1)}, bf16[128,768]{1,0:T(8,128)(2,1)S(1)}, u32[]{:S(2)}, u32[]{:S(2)}) collective-permute-start(bf16[128,768]{1,0:T(8,128)(2,1)S(1)} %get-tuple-element.95), channel_id=1, source_target_pairs={{0,4},{4,2},{1,5},{5,3},{2,6},{6,0},{3,7},{7,1},{8,12},{12,10},{9,... | collective-permute-start | bytes 589832 | tf_op jit(solution)/shard_map/ppermute | solution.py:999
  541.0 9.8 %collective-permute-start.5 = (bf16[128,768]{1,0:T(8,128)(2,1)S(1)}, bf16[128,768]{1,0:T(8,128)(2,1)S(1)}, u32[]{:S(2)}, u32[]{:S(2)}) collective-permute-start(bf16[128,768]{1,0:T(8,128)(2,1)S(1)} %get-tuple-element.94), channel_id=1, source_target_pairs={{4,6},{5,7},{6,4},{7,5},{12,14},{13,15},{14,12},{15,13},{20,22},{2... | collective-permute-start | bytes 589832 | tf_op jit(solution)/shard_map/ppermute | solution.py:1011
  552.5 8.3 %collective-permute-start.9 = (bf16[2,2,128,256]{3,2,1,0:T(8,128)(2,1)S(1)}, bf16[2,2,128,256]{3,2,1,0:T(8,128)(2,1)S(1)}, u32[]{:S(2)}, u32[]{:S(2)}) collective-permute-start(bf16[2,2,128,256]{3,2,1,0:T(8,128)(2,1)S(1)} %dynamic-slice_bitcast_fusion.11), channel_id=1, source_target_pairs={{0,16},{4,20},{8,24},{12,28},{16,0},{20,4},{24,8},{28,12},{1,17},{... | collective-permute-start | bytes 786440 | tf_op jit(solution)/shard_map/ppermute | solution.py:932
  554.6 8.6 %collective-permute-start.7 = (bf16[2,2,128,256]{3,2,1,0:T(8,128)(2,1)S(1)}, bf16[2,2,128,256]{3,2,1,0:T(8,128)(2,1)S(1)}, u32[]{:S(2)}, u32[]{:S(2)}) collective-permute-start(bf16[2,2,128,256]{3,2,1,0:T(8,128)(2,1)S(1)} %dynamic-slice_bitcast_fusion.12), channel_id=1, source_target_pairs={{0,8},{4,12},{8,0},{12,4},{16,24},{20,28},{24,16},{28,20},{1,9},{5... | collective-permute-start | bytes 786440 | tf_op jit(solution)/shard_map/ppermute | solution.py:932
  561.0 6.3 collective-permute-start.10
  563.4 5.9 collective-permute-start.8
  569.3 2.8 slice-start
  569.3 2.9 slice-start.1
  571.3 19.4 %collective-permute-start.25 = (bf16[2,2,352,256]{3,2,1,0:T(8,128)(2,1)}, bf16[2,2,352,256]{3,2,1,0:T(8,128)(2,1)}, u32[]{:S(2)}, u32[]{:S(2)}) collective-permute-start(bf16[2,2,352,256]{3,2,1,0:T(8,128)(2,1)} %dynamic-slice_bitcast_fusion.2), channel_id=1, source_target_pairs={{0,16},{4,20},{8,24},{12,28},{16,0},{20,4},{24,8},{28,12},{1,17},{... | collective-permute-start | bytes 2162696 | tf_op jit(solution)/shard_map/ppermute | solution.py:932
  582.3 57.2 %collective-permute-start.17 = (bf16[2,2,128,1408]{2,3,1,0:T(8,128)(2,1)S(1)}, bf16[2,2,128,1408]{2,3,1,0:T(8,128)(2,1)S(1)}, u32[]{:S(2)}, u32[]{:S(2)}) collective-permute-start(bf16[2,2,128,1408]{2,3,1,0:T(8,128)(2,1)S(1)} %dynamic-slice_bitcast_fusion), channel_id=1, source_target_pairs={{0,16},{4,20},{8,24},{12,28},{16,0},{20,4},{24,8},{28,12},{1,17},{... | collective-permute-start | bytes 4325384 | tf_op jit(solution)/shard_map/ppermute | solution.py:932
  583.5 19.1 %collective-permute-start.23 = (bf16[2,2,352,256]{3,2,1,0:T(8,128)(2,1)S(1)}, bf16[2,2,352,256]{3,2,1,0:T(8,128)(2,1)S(1)}, u32[]{:S(2)}, u32[]{:S(2)}) collective-permute-start(bf16[2,2,352,256]{3,2,1,0:T(8,128)(2,1)S(1)} %dynamic-slice_bitcast_fusion.3), channel_id=1, source_target_pairs={{0,8},{4,12},{8,0},{12,4},{16,24},{20,28},{24,16},{28,20},{1,9},{5... | collective-permute-start | bytes 2162696 | tf_op jit(solution)/shard_map/ppermute | solution.py:932
  584.5 79.6 %collective-permute-start.11 = (bf16[128,256]{1,0:T(8,128)(2,1)S(1)}, bf16[128,256]{1,0:T(8,128)(2,1)S(1)}, u32[]{:S(2)}, u32[]{:S(2)}) collective-permute-start(bf16[128,256]{1,0:T(8,128)(2,1)S(1)} %get-tuple-element.96), channel_id=1, source_target_pairs={{0,1},{1,2},{2,3},{3,0},{4,5},{5,6},{6,7},{7,4},{8,9},{9,10},{10,1... | collective-permute-start | bytes 196616 | tf_op jit(solution)/shard_map/ppermute | solution.py:932
  584.8 83.5 %collective-permute-start.12 = (bf16[128,256]{1,0:T(8,128)(2,1)S(1)}, bf16[128,256]{1,0:T(8,128)(2,1)S(1)}, u32[]{:S(2)}, u32[]{:S(2)}) collective-permute-start(bf16[128,256]{1,0:T(8,128)(2,1)S(1)} %get-tuple-element.97), channel_id=1, source_target_pairs={{0,2},{1,3},{2,0},{3,1},{4,6},{5,7},{6,4},{7,5},{8,10},{9,11},{10,... | collective-permute-start | bytes 196616 | tf_op jit(solution)/shard_map/ppermute | solution.py:932
  592.1 49.1 %collective-permute-start.15 = (bf16[2,2,128,1408]{2,3,1,0:T(8,128)(2,1)S(1)}, bf16[2,2,128,1408]{2,3,1,0:T(8,128)(2,1)S(1)}, u32[]{:S(2)}, u32[]{:S(2)}) collective-permute-start(bf16[2,2,128,1408]{2,3,1,0:T(8,128)(2,1)S(1)} %dynamic-slice_bitcast_fusion.1), channel_id=1, source_target_pairs={{0,8},{4,12},{8,0},{12,4},{16,24},{20,28},{24,16},{28,20},{1,9},{5... | collective-permute-start | bytes 4325384 | tf_op jit(solution)/shard_map/ppermute | solution.py:932
  602.7 36.7 %collective-permute-start.26 = (bf16[2,352,256]{2,1,0:T(8,128)(2,1)S(1)}, bf16[2,352,256]{2,1,0:T(8,128)(2,1)S(1)}, u32[]{:S(2)}, u32[]{:S(2)}) collective-permute-start(bf16[2,352,256]{2,1,0:T(8,128)(2,1)S(1)} %dynamic-slice_bitcast_fusion.9), channel_id=1, source_target_pairs={{0,8},{4,12},{8,0},{12,4},{16,24},{20,28},{24,16},{28,20},{1,9},{5... | collective-permute-start | bytes 1081352 | tf_op jit(solution)/shard_map/ppermute | solution.py:932
  639.3 28.9 %collective-permute-start.13 = (bf16[128,256]{1,0:T(8,128)(2,1)S(1)}, bf16[128,256]{1,0:T(8,128)(2,1)S(1)}, u32[]{:S(2)}, u32[]{:S(2)}) collective-permute-start(bf16[128,256]{1,0:T(8,128)(2,1)S(1)} %get-tuple-element.98), channel_id=1, source_target_pairs={{0,3},{1,0},{2,1},{3,2},{4,7},{5,4},{6,5},{7,6},{8,11},{9,8},{10,9... | collective-permute-start | bytes 196616 | tf_op jit(solution)/shard_map/ppermute | solution.py:932
  639.5 8.6 %collective-permute-start.24 = (bf16[2,352,256]{2,1,0:T(8,128)(2,1)S(1)}, bf16[2,352,256]{2,1,0:T(8,128)(2,1)S(1)}, u32[]{:S(2)}, u32[]{:S(2)}) collective-permute-start(bf16[2,352,256]{2,1,0:T(8,128)(2,1)S(1)} %dynamic-slice_bitcast_fusion.10), channel_id=1, source_target_pairs={{0,16},{4,20},{8,24},{12,28},{16,0},{20,4},{24,8},{28,12},{1,17},{... | collective-permute-start | bytes 1081352 | tf_op jit(solution)/shard_map/ppermute | solution.py:932
  641.2 16.3 %collective-permute-start.18 = (bf16[2,128,1408]{1,2,0:T(8,128)(2,1)S(1)}, bf16[2,128,1408]{1,2,0:T(8,128)(2,1)S(1)}, u32[]{:S(2)}, u32[]{:S(2)}) collective-permute-start(bf16[2,128,1408]{1,2,0:T(8,128)(2,1)S(1)} %dynamic-slice_bitcast_fusion.4), channel_id=1, source_target_pairs={{0,8},{4,12},{8,0},{12,4},{16,24},{20,28},{24,16},{28,20},{1,9},{5... | collective-permute-start | bytes 2162696 | tf_op jit(solution)/shard_map/ppermute | solution.py:932
  648.1 15.4 %collective-permute-start.16 = (bf16[2,128,1408]{1,2,0:T(8,128)(2,1)S(1)}, bf16[2,128,1408]{1,2,0:T(8,128)(2,1)S(1)}, u32[]{:S(2)}, u32[]{:S(2)}) collective-permute-start(bf16[2,128,1408]{1,2,0:T(8,128)(2,1)S(1)} %dynamic-slice_bitcast_fusion.5), channel_id=1, source_target_pairs={{0,16},{4,20},{8,24},{12,28},{16,0},{20,4},{24,8},{28,12},{1,17},{... | collective-permute-start | bytes 2162696 | tf_op jit(solution)/shard_map/ppermute | solution.py:932
  657.5 11.6 %collective-permute-start.27 = (bf16[352,256]{1,0:T(8,128)(2,1)S(1)}, bf16[352,256]{1,0:T(8,128)(2,1)S(1)}, u32[]{:S(2)}, u32[]{:S(2)}) collective-permute-start(bf16[352,256]{1,0:T(8,128)(2,1)S(1)} %get-tuple-element.86), channel_id=1, source_target_pairs={{0,1},{1,2},{2,3},{3,0},{4,5},{5,6},{6,7},{7,4},{8,9},{9,10},{10,1... | collective-permute-start | bytes 540680 | tf_op jit(solution)/shard_map/ppermute | solution.py:932
  663.5 22.7 %collective-permute-start.28 = (bf16[352,256]{1,0:T(8,128)(2,1)S(1)}, bf16[352,256]{1,0:T(8,128)(2,1)S(1)}, u32[]{:S(2)}, u32[]{:S(2)}) collective-permute-start(bf16[352,256]{1,0:T(8,128)(2,1)S(1)} %get-tuple-element.87), channel_id=1, source_target_pairs={{0,2},{1,3},{2,0},{3,1},{4,6},{5,7},{6,4},{7,5},{8,10},{9,11},{10,... | collective-permute-start | bytes 540680 | tf_op jit(solution)/shard_map/ppermute | solution.py:932
  664.1 22.1 %collective-permute-start.29 = (bf16[352,256]{1,0:T(8,128)(2,1)S(1)}, bf16[352,256]{1,0:T(8,128)(2,1)S(1)}, u32[]{:S(2)}, u32[]{:S(2)}) collective-permute-start(bf16[352,256]{1,0:T(8,128)(2,1)S(1)} %get-tuple-element.88), channel_id=1, source_target_pairs={{0,3},{1,0},{2,1},{3,2},{4,7},{5,4},{6,5},{7,6},{8,11},{9,8},{10,9... | collective-permute-start | bytes 540680 | tf_op jit(solution)/shard_map/ppermute | solution.py:932
  668.3 18.8 %collective-permute-start.19 = (bf16[128,1408]{0,1:T(8,128)(2,1)S(1)}, bf16[128,1408]{0,1:T(8,128)(2,1)S(1)}, u32[]{:S(2)}, u32[]{:S(2)}) collective-permute-start(bf16[128,1408]{0,1:T(8,128)(2,1)S(1)} %get-tuple-element.81), channel_id=1, source_target_pairs={{0,1},{1,2},{2,3},{3,0},{4,5},{5,6},{6,7},{7,4},{8,9},{9,10},{10,1... | collective-permute-start | bytes 1081352 | tf_op jit(solution)/shard_map/ppermute | solution.py:932
  668.3 32.6 %collective-permute-start.20 = (bf16[128,1408]{0,1:T(8,128)(2,1)S(1)}, bf16[128,1408]{0,1:T(8,128)(2,1)S(1)}, u32[]{:S(2)}, u32[]{:S(2)}) collective-permute-start(bf16[128,1408]{0,1:T(8,128)(2,1)S(1)} %get-tuple-element.82), channel_id=1, source_target_pairs={{0,2},{1,3},{2,0},{3,1},{4,6},{5,7},{6,4},{7,5},{8,10},{9,11},{10,... | collective-permute-start | bytes 1081352 | tf_op jit(solution)/shard_map/ppermute | solution.py:932
  669.1 31.8 %collective-permute-start.21 = (bf16[128,1408]{0,1:T(8,128)(2,1)S(1)}, bf16[128,1408]{0,1:T(8,128)(2,1)S(1)}, u32[]{:S(2)}, u32[]{:S(2)}) collective-permute-start(bf16[128,1408]{0,1:T(8,128)(2,1)S(1)} %get-tuple-element.83), channel_id=1, source_target_pairs={{0,3},{1,0},{2,1},{3,2},{4,7},{5,4},{6,5},{7,6},{8,11},{9,8},{10,9... | collective-permute-start | bytes 1081352 | tf_op jit(solution)/shard_map/ppermute | solution.py:932
Sparse Core Ops, SparseCore 0:
  407.0 47.3 reduce-scatter.3

commit v2 on v1

v2 whole, which is shorter than its diff:
```python
import functools
import math

import jax
import jax.numpy as jnp
from jax import lax
from jax.experimental import pallas as pl
from jax.experimental.pallas import tpu as pltpu
from jax.sharding import PartitionSpec as P

HEAD = 64
EPSILON = 1e-05
THETA = 10000.0
NEGATIVE = -1e30
BLOCK = 256
VMEM_LIMIT = 58 * 1024 * 1024
BACKWARD_LIMIT = 58 * 1024 * 1024
MESH = pl.DeviceIdType.MESH
BF16 = jnp.bfloat16
F32 = jnp.float32


def nn(left, right):
    return lax.dot_general(left, right, (((1,), (0,)), ((), ())), preferred_element_type=F32)


def nt(left, right):
    return lax.dot_general(left, right, (((1,), (1,)), ((), ())), preferred_element_type=F32)


def tn(left, right):
    return lax.dot_general(left, right, (((0,), (0,)), ((), ())), preferred_element_type=F32)


def turns(table, width):
    lane = lax.broadcasted_iota(jnp.int32, table.shape, 1)
    swapped = pltpu.roll(table, HEAD, 1)
    cos = jnp.where(lane < HEAD, table, swapped)
    sin = jnp.where(lane < HEAD, swapped, table)
    times = width // table.shape[1]
    return jnp.concatenate([cos] * times, axis=1), jnp.concatenate([sin] * times, axis=1)


def half_swap(rows):
    width = rows.shape[1]
    lane = lax.broadcasted_iota(jnp.int32, rows.shape, 1)
    low = lax.rem(lane, HEAD) < HEAD // 2
    return jnp.where(
        low,
        pltpu.roll(rows, width - HEAD // 2, 1),
        pltpu.roll(rows, HEAD // 2, 1),
    )


def head_lanes(shape, head):
    lane = lax.broadcasted_iota(jnp.int32, shape, 1)
    return (lane >= head * HEAD) & (lane < (head + 1) * HEAD)


def forward_kernel(
    x, vf, wqkv, gain, table, start,
    h1, q, k, vm, kt, out, att, lse,
    vt, acc, mx, tot,
):
    group = x.shape[0]
    cols = vf.shape[1]
    heads = cols // HEAD
    blocks = group // BLOCK

    def project(b, carry):
        rows = pl.ds(pl.multiple_of(b * BLOCK, BLOCK), BLOCK)
        xv = x[rows, :].astype(F32)
        rstd = lax.rsqrt(jnp.mean(xv * xv, axis=1, keepdims=True) + EPSILON)
        hv = (xv * rstd * gain[...]).astype(BF16)
        h1[rows, :] = hv
        raw = nn(hv, wqkv[...])
        cos_v, sin_v = turns(table[rows, :], cols)
        rq = raw[:, :cols]
        rk = raw[:, cols : 2 * cols]
        rv = raw[:, 2 * cols :]
        qv = (rq * cos_v + half_swap(rq) * sin_v).astype(BF16)
        q[rows, :] = (qv.astype(F32) * (1.0 / math.sqrt(HEAD))).astype(BF16)
        kv = (rk * cos_v + half_swap(rk) * sin_v).astype(BF16)
        k[rows, :] = kv
        kt[:, rows] = kv.T
        mixed = (0.5 * rv + 0.5 * vf[rows, :].astype(F32)).astype(BF16)
        vm[rows, :] = mixed
        vt[:, rows] = mixed.T
        return carry

    lax.fori_loop(0, blocks, project, 0)

    def queries(b, carry):
        rows = pl.ds(pl.multiple_of(b * BLOCK, BLOCK), BLOCK)
        acc[...] = jnp.zeros_like(acc)
        mx[...] = jnp.full_like(mx, NEGATIVE)
        tot[...] = jnp.zeros_like(tot)
        qv = q[rows, :]
        first = start[0:1, rows]

        def keys(kb, inner):
            krows = pl.ds(pl.multiple_of(kb * BLOCK, BLOCK), BLOCK)
            kv = k[krows, :]
            key_pos = kb * BLOCK + lax.broadcasted_iota(jnp.int32, (BLOCK, BLOCK), 0)
            query_pos = b * BLOCK + lax.broadcasted_iota(jnp.int32, (BLOCK, BLOCK), 1)
            allowed = (key_pos <= query_pos) & (key_pos >= first)
            for head in range(heads):
                band = slice(head * HEAD, (head + 1) * HEAD)
                qm = jnp.where(head_lanes(qv.shape, head), qv, jnp.zeros_like(qv))
                s = jnp.where(allowed, nt(kv, qm), NEGATIVE)
                old = mx[head : head + 1, :]
                new = jnp.maximum(old, jnp.max(s, axis=0, keepdims=True))
                p = jnp.exp(s - new)
                shrink = jnp.exp(old - new)
                mx[head : head + 1, :] = new
                tot[head : head + 1, :] = tot[head : head + 1, :] * shrink + jnp.sum(
                    p, axis=0, keepdims=True
                )
                acc[band, :] = acc[band, :] * shrink + nn(vt[band, krows], p.astype(BF16))
            return inner

        lax.fori_loop(0, b + 1, keys, 0)
        for head in range(heads):
            band = slice(head * HEAD, (head + 1) * HEAD)
            acc[band, :] = acc[band, :] / tot[head : head + 1, :]
        ov = acc[...].T
        att[rows, :] = ov
        out[rows, :] = ov.astype(BF16)
        lse[:, rows] = mx[...] + jnp.log(tot[...])
        return carry

    lax.fori_loop(0, blocks, queries, 0)


def forward_attention(x, vf, wqkv, gain, table, start):
    group, depth = x.shape
    cols = vf.shape[1]
    shapes = (
        jax.ShapeDtypeStruct((group, depth), BF16),
        jax.ShapeDtypeStruct((group, cols), BF16),
        jax.ShapeDtypeStruct((group, cols), BF16),
        jax.ShapeDtypeStruct((group, cols), BF16),
        jax.ShapeDtypeStruct((cols, group), BF16),
        jax.ShapeDtypeStruct((group, cols), BF16),
        jax.ShapeDtypeStruct((group, cols), F32),
        jax.ShapeDtypeStruct((8, group), F32),
    )
    vmem = pl.BlockSpec(memory_space=pltpu.VMEM)
    return pl.pallas_call(
        forward_kernel,
        out_shape=shapes,
        in_specs=[vmem] * 6,
        out_specs=[vmem] * 8,
        scratch_shapes=[
            pltpu.VMEM((cols, group), BF16),
            pltpu.VMEM((cols, BLOCK), F32),
            pltpu.VMEM((8, BLOCK), F32),
            pltpu.VMEM((8, BLOCK), F32),
        ],
        compiler_params=pltpu.CompilerParams(vmem_limit_bytes=VMEM_LIMIT),
        name="attention_forward",
    )(x, vf, wqkv, gain, table, start)


class Plan:
    def __init__(self, fsdp, ctx):
        self.fsdp, self.ctx = fsdp, ctx
        self.lines = fsdp // 2
        self.across = math.isqrt(self.lines)
        self.along = self.lines // self.across
        self.half = ctx // 2
        self.f = lax.axis_index("fsdp")
        self.c = lax.axis_index("ctx")
        self.core = lax.rem(self.f, 2)
        self.line = self.f // 2
        self.a = self.line // self.along
        self.b = lax.rem(self.line, self.along)
        self.home = self.c // self.half
        self.started = []
        self.draining = False

    def barrier(self):
        sem = pltpu.get_barrier_semaphore()
        count = 0
        for step in range(1, self.fsdp):
            dev = (lax.rem(self.f + step, self.fsdp), self.c)
            pl.semaphore_signal(sem, inc=1, device_id=dev, device_id_type=MESH)
            count += 1
        for step in range(1, self.ctx):
            for core in range(2):
                dev = (self.line * 2 + core, lax.rem(self.c + step, self.ctx))
                pl.semaphore_signal(sem, inc=1, device_id=dev, device_id_type=MESH)
                count += 1
        pl.semaphore_wait(sem, count)

    def when(self, cond, act):
        if cond is True:
            act()
        else:
            pl.when(cond)(act)

    def send(self, src, dst, send_sem, recv_sem, dev, cond=True):
        def copy():
            return pltpu.make_async_remote_copy(
                src_ref=src, dst_ref=dst, send_sem=send_sem, recv_sem=recv_sem,
                device_id=dev, device_id_type=MESH,
            )

        if self.draining:
            self.when(cond, lambda: copy().wait_send())
            return
        self.when(cond, lambda: copy().start())
        self.started.append((cond, lambda: copy().wait_send()))

    def keep(self, src, dst, sem, cond=True):
        if self.draining:
            return
        self.when(cond, lambda: pltpu.make_async_copy(src, dst, sem).start())

    def arrive(self, dst, sem, cond=True):
        if self.draining:
            return
        self.when(cond, lambda: pltpu.make_async_copy(dst, dst, sem).wait())

    def drain(self):
        for cond, act in self.started:
            self.when(cond, act)
        self.started = []


def both(*conds):
    out = True
    for cond in conds:
        if cond is not True:
            out = cond if out is True else jnp.logical_and(out, cond)
    return out


def gather_kernel(
    fsdp, ctx,
    x, vf, wqkv, wo, gu, wd, gains,
    xs, vs, wq, wqh, wos, gus, wds, gs,
    x_sem, x_out, v_sem, v_out, q_sem, q_out, h_sem, g_sem, g_out, w_sem, w_z, w_p, w_s,
):
    plan = Plan(fsdp, ctx)
    f, c, core, line, home, half = plan.f, plan.c, plan.core, plan.line, plan.home, plan.half
    a, b, across, along, lines = plan.a, plan.b, plan.across, plan.along, plan.lines
    cols = vs.shape[2]
    owner = core == home
    sibling = (line * 2 + 1 - core, c)
    plan.barrier()

    def spread_x(j, below, above, cond):
        src, dst = xs.at[j], xs.at[j]
        if below:
            plan.send(src, dst, x_out.at[0, j], x_sem.at[j], (f, c - 1), both(cond, c > home * half))
        if above:
            plan.send(
                src, dst, x_out.at[1, j], x_sem.at[j], (f, c + 1),
                both(cond, c < home * half + half - 1),
            )
        plan.send(src, dst, x_out.at[2, j], x_sem.at[j], sibling, cond)

    away = jnp.logical_not(owner)
    entry = jnp.where(core == 0, half - 1, half)
    plan.send(x, xs.at[c], x_out.at[0, c], x_sem.at[c], (f, entry), away)
    plan.send(x, xs.at[c], x_out.at[0, c], x_sem.at[c], (f, c - 1), both(owner, c > home * half))
    plan.send(
        x, xs.at[c], x_out.at[1, c], x_sem.at[c], (f, c + 1),
        both(owner, c < home * half + half - 1),
    )
    plan.send(x, xs.at[c], x_out.at[2, c], x_sem.at[c], sibling, owner)
    plan.keep(x, xs.at[c], x_sem.at[c], owner)

    across_ctx = lax.rem(c + half, ctx)
    plan.send(wqkv, wqh, h_sem.at[0], h_sem.at[1], (f, across_ctx))

    def items(row, j):
        return (
            wos.at[row, :, pl.ds(pl.multiple_of(j * wo.shape[1], wo.shape[1]), wo.shape[1])],
            gus.at[j, row],
            wds.at[row, :, pl.ds(pl.multiple_of(j * wd.shape[1], wd.shape[1]), wd.shape[1])],
        )

    def spread_w(srcs, j, cond, up, down):
        dsts = items(f, j)
        for i in range(3):
            if up:
                plan.send(
                    srcs[i], dsts[i], w_z.at[i, 0, j], w_sem.at[i, f, j], (f, c + 1),
                    both(cond, c < ctx - 1),
                )
            if down:
                plan.send(
                    srcs[i], dsts[i], w_z.at[i, 1, j], w_sem.at[i, f, j], (f, c - 1),
                    both(cond, c > 0),
                )
        for i in range(3):
            for step in range(1, across):
                dev = ((lax.rem(a + step, across) * along + b) * 2 + core, c)
                plan.send(
                    srcs[i], dsts[i], w_p.at[i, step - 1, line, j], w_sem.at[i, f, j], dev, cond
                )
            for step in range(1, along):
                dev = ((a * along + lax.rem(b + step, along)) * 2 + core, c)
                plan.send(
                    srcs[i], dsts[i], w_p.at[i, across + step - 2, line, j], w_sem.at[i, f, j],
                    dev, cond,
                )
            plan.send(srcs[i], dsts[i], w_s.at[i, line, j], w_sem.at[i, f, j], sibling, cond)

    for step in range(1, fsdp):
        dev = (lax.rem(f + step, fsdp), c)
        plan.send(gains, gs.at[f], g_out.at[step - 1], g_sem.at[f], dev)
    plan.keep(gains, gs.at[f], g_sem.at[f])

    own = (wo, gu, wd)
    spread_w(own, c, True, True, True)
    for src, dst, i in zip(own, items(f, c), range(3)):
        plan.keep(src, dst, w_sem.at[i, f, c])

    for at in range(lines):
        dev = (at * 2, c)
        plan.send(wqkv, wq.at[f], q_out.at[0, at], q_sem.at[f], dev, jnp.logical_not(f == at * 2))
    plan.keep(wqkv, wq.at[f], q_sem.at[f], core == 0)

    for i in range(half):
        for k in range(2):
            to = core * half + i
            rank = lax.rem(to + k * half, ctx)
            src = vf.at[:, pl.ds(pl.multiple_of(rank * cols, cols), cols)]
            mine = both(owner, c == to, core == k)
            plan.send(
                src, vs.at[c], v_out.at[i, k], v_sem.at[c], (line * 2 + k, to),
                jnp.logical_not(mine),
            )
            plan.keep(src, vs.at[c], v_sem.at[c], mine)

    pltpu.make_async_copy(wqh, wqh, h_sem.at[1]).wait()
    for at in range(lines):
        dev = (at * 2 + 1, c)
        plan.send(
            wqh, wq.at[f], q_out.at[1, at], q_sem.at[f], dev, jnp.logical_not(f == at * 2 + 1)
        )
    plan.keep(wqh, wq.at[f], q_sem.at[f], core == 1)

    for dist in range(1, ctx):
        for side in range(2):
            j = c - dist if side == 0 else c + dist
            there = j >= 0 if side == 0 else j < ctx
            at = jnp.clip(j, 0, ctx - 1)
            cond = both(owner, there)
            plan.arrive(xs.at[at], x_sem.at[at], cond)
            spread_x(at, side == 1, side == 0, cond)
        for side in range(2):
            j = c - dist if side == 0 else c + dist
            there = j >= 0 if side == 0 else j < ctx
            at = jnp.clip(j, 0, ctx - 1)
            dsts = items(f, at)
            for i in range(3):
                plan.arrive(dsts[i], w_sem.at[i, f, at], there)
            spread_w(dsts, at, there, side == 0, side == 1)

    for dist in range(ctx):
        for side in range(2 if dist else 1):
            j = c - dist if side == 0 else c + dist
            there = j >= 0 if side == 0 else j < ctx
            at = jnp.clip(j, 0, ctx - 1)
            first = at < half
            for step in range(1, across):
                from_line = lax.rem(a + across - step, across) * along + b
                row = from_line * 2 + core
                dsts = items(row, at)
                for i in range(3):
                    plan.arrive(dsts[i], w_sem.at[i, row, at], there)
                for i in range(3):
                    for hop in range(1, along):
                        dev = ((a * along + lax.rem(b + hop, along)) * 2 + core, c)
                        plan.send(
                            dsts[i], dsts[i], w_p.at[i, across + hop - 2, from_line, at],
                            w_sem.at[i, row, at], dev, both(there, first),
                        )
                    plan.send(
                        dsts[i], dsts[i], w_s.at[i, from_line, at], w_sem.at[i, row, at], sibling,
                        there,
                    )
            for step in range(1, along):
                from_line = a * along + lax.rem(b + along - step, along)
                row = from_line * 2 + core
                dsts = items(row, at)
                for i in range(3):
                    plan.arrive(dsts[i], w_sem.at[i, row, at], there)
                for i in range(3):
                    for hop in range(1, across):
                        dev = ((lax.rem(a + hop, across) * along + b) * 2 + core, c)
                        plan.send(
                            dsts[i], dsts[i], w_p.at[i, hop - 1, from_line, at],
                            w_sem.at[i, row, at], dev, both(there, jnp.logical_not(first)),
                        )
                    plan.send(
                        dsts[i], dsts[i], w_s.at[i, from_line, at], w_sem.at[i, row, at], sibling,
                        there,
                    )
    for dist in range(ctx):
        for side in range(2 if dist else 1):
            j = c - dist if side == 0 else c + dist
            there = j >= 0 if side == 0 else j < ctx
            at = jnp.clip(j, 0, ctx - 1)
            for step in range(1, across):
                for hop in range(1, along):
                    from_line = lax.rem(a + step, across) * along + lax.rem(b + hop, along)
                    row = from_line * 2 + core
                    dsts = items(row, at)
                    for i in range(3):
                        plan.arrive(dsts[i], w_sem.at[i, row, at], there)
                        plan.send(
                            dsts[i], dsts[i], w_s.at[i, from_line, at], w_sem.at[i, row, at],
                            sibling, there,
                        )

    for i in range(3):
        plan.arrive(items(f, c)[i], w_sem.at[i, f, c])

    def far(at, carry):
        row = at * 2 + 1 - core
        for j in range(ctx):
            dsts = items(row, j)
            for i in range(3):
                plan.arrive(dsts[i], w_sem.at[i, row, j])
        return carry

    lax.fori_loop(0, lines, far, 0)
    for j in range(ctx):
        plan.arrive(xs.at[j], x_sem.at[j], both(jnp.logical_or(away, c == j)))
        plan.arrive(vs.at[j], v_sem.at[j])
    for row in range(fsdp):
        plan.arrive(wq.at[row], q_sem.at[row])
        plan.arrive(gs.at[row], g_sem.at[row])
    plan.drain()


def gather(mesh, x, vf, wqkv, wo, gu, wd, gains):
    fsdp, ctx = mesh.shape["fsdp"], mesh.shape["ctx"]
    tokens, depth = x.shape
    cols = depth // ctx
    lines = fsdp // 2
    across = math.isqrt(lines)
    peers = max(across - 1 + lines // across - 1, 1)
    anywhere = pl.BlockSpec(memory_space=pl.ANY)
    dma = pltpu.SemaphoreType.DMA
    return pl.pallas_call(
        functools.partial(gather_kernel, fsdp, ctx),
        out_shape=(
            jax.ShapeDtypeStruct((ctx, tokens, depth), BF16),
            jax.ShapeDtypeStruct((ctx, tokens, cols), BF16),
            jax.ShapeDtypeStruct((fsdp,) + wqkv.shape, BF16),
            jax.ShapeDtypeStruct(wqkv.shape, BF16),
            jax.ShapeDtypeStruct((fsdp, wo.shape[0], depth), BF16),
            jax.ShapeDtypeStruct((ctx, fsdp) + gu.shape, BF16),
            jax.ShapeDtypeStruct((fsdp, wd.shape[0], depth), BF16),
            jax.ShapeDtypeStruct((fsdp,) + gains.shape, F32),
        ),
        in_specs=[anywhere] * 7,
        out_specs=[anywhere] * 8,
        scratch_shapes=[
            dma((ctx,)), dma((3, ctx)), dma((ctx,)), dma((ctx // 2, 2)),
            dma((fsdp,)), dma((2, lines)), dma((2,)), dma((fsdp,)), dma((fsdp,)),
            dma((3, fsdp, ctx)), dma((3, 2, ctx)), dma((3, peers, lines, ctx)), dma((3, lines, ctx)),
        ],
        compiler_params=pltpu.CompilerParams(collective_id=0, has_side_effects=True),
        name="gather_all",
    )(x, vf, wqkv, wo, gu, wd, gains)


def trade_kernel(fsdp, ctx, inward, src_ref, dst_ref, recv, sent):
    plan = Plan(fsdp, ctx)
    f, c, core, line, home, half = plan.f, plan.c, plan.core, plan.line, plan.home, plan.half
    cols = (src_ref if inward else dst_ref).shape[2]
    plan.barrier()

    def band(rank):
        return pl.ds(pl.multiple_of(rank * cols, cols), cols)

    if inward:
        rank = lax.rem(c + core * half, ctx)
        for step in range(ctx):
            j = lax.rem(c + step, ctx)
            src, dst = src_ref.at[j], dst_ref.at[:, band(rank)]
            dev = (line * 2 + home, j)
            mine = both(core == home) if step == 0 else False
            if step == 0:
                plan.keep(src, dst, recv.at[rank], mine)
                plan.send(src, dst, sent.at[j], recv.at[rank], dev, jnp.logical_not(mine))
            else:
                plan.send(src, dst, sent.at[j], recv.at[rank], dev)
        for rank in range(ctx):
            plan.arrive(dst_ref.at[:, band(rank)], recv.at[rank])
    else:
        for i in range(half):
            for k in range(2):
                to = core * half + i
                src = src_ref.at[:, band(lax.rem(to + k * half, ctx))]
                mine = both(core == home, c == to, core == k)
                plan.send(
                    src, dst_ref.at[c], sent.at[i * 2 + k], recv.at[c], (line * 2 + k, to),
                    jnp.logical_not(mine),
                )
                plan.keep(src, dst_ref.at[c], recv.at[c], mine)
        for j in range(ctx):
            plan.arrive(dst_ref.at[j], recv.at[j])
    plan.drain()


def trade(mesh, array, inward, ident):
    fsdp, ctx = mesh.shape["fsdp"], mesh.shape["ctx"]
    if inward:
        shape = (array.shape[1], array.shape[2] * ctx)
    else:
        shape = (ctx, array.shape[0], array.shape[1] // ctx)
    anywhere = pl.BlockSpec(memory_space=pl.ANY)
    return pl.pallas_call(
        functools.partial(trade_kernel, fsdp, ctx, inward),
        out_shape=jax.ShapeDtypeStruct(shape, BF16),
        in_specs=[anywhere],
        out_specs=anywhere,
        scratch_shapes=[pltpu.SemaphoreType.DMA((ctx,)), pltpu.SemaphoreType.DMA((ctx,))],
        compiler_params=pltpu.CompilerParams(collective_id=ident, has_side_effects=True),
        name="trade_in" if inward else "trade_out",
    )(array)


def feed_kernel(
    fsdp, ctx,
    o, x, dy, wo, gain, gu, wd,
    out, dx2, do, dg, s_wo, s_gu, s_wd,
    x2, h2, h2t, total, dh2, act, dgu,
    my_gu, my_wd, my_wo, got_gu, got_wd, got_wo,
    gu_sem, gu_out, wd_sem, wd_out, wo_sem, wo_out,
):
    plan = Plan(fsdp, ctx)
    core = plan.core
    sibling = (plan.line * 2 + 1 - core, plan.c)
    step = pl.program_id(0)
    last = pl.num_programs(0) - 1
    tokens, depth = x.shape
    chunk = wd.shape[0]
    blocks = tokens // BLOCK
    lines = plan.lines
    shard = depth // fsdp
    row_lines = my_wd.shape[1]
    row_count = my_wd.shape[3]
    slot = lax.rem(step, 2)

    def give(at):
        place = lax.rem(at, 2)
        for i in range(lines):
            plan.send(
                my_gu.at[place, i, 1 - core], got_gu.at[at, i], gu_out.at[place, i],
                gu_sem.at[at, i], sibling,
            )
        for i in range(row_lines):
            plan.send(
                my_wd.at[place, i, 1 - core], got_wd.at[at, i], wd_out.at[place, i],
                wd_sem.at[at, i], sibling,
            )

    def given(at):
        plan.draining = True
        give(at)
        plan.draining = False

    @pl.when(step == 0)
    def _():
        sem = pltpu.get_barrier_semaphore()
        pl.semaphore_signal(sem, inc=1, device_id=sibling, device_id_type=MESH)
        pl.semaphore_wait(sem, 1)

        def rows_of(b, carry):
            rows = pl.ds(pl.multiple_of(b * BLOCK, BLOCK), BLOCK)
            mid = x[rows, :].astype(F32) + nn(o[rows, :], wo[...])
            x2[rows, :] = mid
            rstd = lax.rsqrt(jnp.mean(mid * mid, axis=1, keepdims=True) + EPSILON)
            hv = (mid * rstd * gain[...]).astype(BF16)
            h2[rows, :] = hv
            h2t[:, rows] = hv.T
            total[rows, :] = mid
            dh2[rows, :] = jnp.zeros((BLOCK, depth), F32)
            return carry

        lax.fori_loop(0, blocks, rows_of, 0)

    @pl.when(jnp.logical_and(step >= 2, step < last))
    def _():
        given(step - 2)

    @pl.when(step < last)
    def _():
        def rows_of(b, carry):
            rows = pl.ds(pl.multiple_of(b * BLOCK, BLOCK), BLOCK)
            both_ = nn(h2[rows, :], gu[0])
            gate = both_[:, :chunk]
            up = both_[:, chunk:]
            da = nt(dy[rows, :], wd[...]).astype(BF16).astype(F32)
            sig = 1.0 / (1.0 + jnp.exp(-gate))
            silu = gate * sig
            av = (silu * up).astype(BF16)
            act[rows, :] = av
            dgate = (da * up * (sig * (1.0 + gate * (1.0 - sig)))).astype(BF16)
            dup = (da * silu).astype(BF16)
            dv = jnp.concatenate([dgate, dup], axis=1)
            dgu[rows, :] = dv
            total[rows, :] = total[rows, :] + nn(av, wd[...])
            dh2[rows, :] = dh2[rows, :] + nt(dv, gu[0])
            return carry

        lax.fori_loop(0, blocks, rows_of, 0)

        for part in range(depth // 512):
            at = slice(part * 512, (part + 1) * 512)
            val = tn(act[...], dy[:, at])
            for r in range(row_lines * 2):
                my_wd[slot, r // 2, r % 2, :, at] = val[
                    r * row_count : (r + 1) * row_count
                ].astype(BF16)

        rows_each = BLOCK // shard

        def weight(b, carry):
            rows = pl.ds(pl.multiple_of(b * BLOCK, BLOCK), BLOCK)
            val = nn(h2t[rows, :], dgu[...]).astype(BF16)
            for r in range(rows_each):
                my_gu[slot, b * (rows_each // 2) + r // 2, r % 2] = val[
                    r * shard : (r + 1) * shard
                ]
            return carry

        lax.fori_loop(0, depth // BLOCK, weight, 0)
        give(step)

    def collect(at):
        place = lax.rem(at, 2)
        for i in range(lines):
            plan.arrive(got_gu.at[at, i], gu_sem.at[at, i])
            add_rows(s_gu.at[0, i], [my_gu.at[place, i, core], got_gu.at[at, i]])
        for i in range(row_lines):
            plan.arrive(got_wd.at[at, i], wd_sem.at[at, i])
            add_rows(s_wd.at[i], [my_wd.at[place, i, core], got_wd.at[at, i]])

    @pl.when(jnp.logical_and(step >= 1, step < last))
    def _():
        collect(step - 1)

    @pl.when(step == last)
    def _():
        dg[...] = jnp.zeros_like(dg)

        def rows_of(b, carry):
            rows = pl.ds(pl.multiple_of(b * BLOCK, BLOCK), BLOCK)
            out[rows, :] = total[rows, :].astype(BF16)
            mid = x2[rows, :]
            rstd = lax.rsqrt(jnp.mean(mid * mid, axis=1, keepdims=True) + EPSILON)
            xhat = mid * rstd
            dh = dh2[rows, :]
            u = dh * gain[...]
            dm = dy[rows, :].astype(F32) + rstd * (
                u - xhat * jnp.mean(u * xhat, axis=1, keepdims=True)
            )
            dx2[rows, :] = dm
            dg[0:1, :] = dg[0:1, :] + jnp.sum(dh * xhat, axis=0, keepdims=True)
            h2[rows, :] = dm.astype(BF16)
            return carry

        lax.fori_loop(0, blocks, rows_of, 0)
        rows_each = BLOCK // shard

        def weight_out(b, carry):
            at = pl.ds(pl.multiple_of(b * BLOCK, BLOCK), BLOCK)
            val = tn(o[:, at], h2[...]).astype(BF16)
            for r in range(rows_each):
                my_wo[b * (rows_each // 2) + r // 2, r % 2] = val[r * shard : (r + 1) * shard]
            return carry

        lax.fori_loop(0, depth // BLOCK, weight_out, 0)
        for i in range(lines):
            plan.send(my_wo.at[i, 1 - core], got_wo.at[i], wo_out.at[i], wo_sem.at[i], sibling)

        def rows_out(b, carry):
            rows = pl.ds(pl.multiple_of(b * BLOCK, BLOCK), BLOCK)
            do[rows, :] = nt(h2[rows, :], wo[...]).astype(BF16)
            return carry

        lax.fori_loop(0, blocks, rows_out, 0)
        collect(last - 1)
        for i in range(lines):
            plan.arrive(got_wo.at[i], wo_sem.at[i])
            add_rows(s_wo.at[i], [my_wo.at[i, core], got_wo.at[i]])
        for at in (last - 2, last - 1):
            given(at)
        plan.draining = True
        for i in range(lines):
            plan.send(my_wo.at[i, 1 - core], got_wo.at[i], wo_out.at[i], wo_sem.at[i], sibling)
        plan.draining = False


def feed_forward(mesh, o, x, dy, wo, gain, gu, wd):
    fsdp, ctx = mesh.shape["fsdp"], mesh.shape["ctx"]
    tokens, depth = x.shape
    steps, _, width = gu.shape
    chunk = width // 2
    lines = fsdp // 2
    shard = depth // fsdp
    row_count = wd.shape[0] // fsdp
    row_lines = fsdp // ctx // 2
    once = pl.Buffered(1)

    def whole(shape):
        return pl.BlockSpec(shape, lambda i: (0,) * len(shape), pipeline_mode=once)

    def whole_out(shape):
        return pl.BlockSpec(shape, lambda i: (0,) * len(shape), pipeline_mode=once)

    shapes = (
        jax.ShapeDtypeStruct((tokens, depth), BF16),
        jax.ShapeDtypeStruct((tokens, depth), F32),
        jax.ShapeDtypeStruct((tokens, depth), BF16),
        jax.ShapeDtypeStruct((8, depth), F32),
        jax.ShapeDtypeStruct((lines, shard, depth), BF16),
        jax.ShapeDtypeStruct((ctx, lines, shard, width), BF16),
        jax.ShapeDtypeStruct((lines, row_count, depth), BF16),
    )
    dma = pltpu.SemaphoreType.DMA
    return pl.pallas_call(
        functools.partial(feed_kernel, fsdp, ctx),
        grid=(steps + 1,),
        out_shape=shapes,
        in_specs=[
            whole((tokens, depth)),
            whole((tokens, depth)),
            whole((tokens, depth)),
            whole((depth, depth)),
            whole((1, depth)),
            pl.BlockSpec((1, depth, width), lambda i: (jnp.minimum(i, steps - 1), 0, 0)),
            pl.BlockSpec((chunk, depth), lambda i: (jnp.minimum(i, steps - 1), 0)),
        ],
        out_specs=[
            whole_out((tokens, depth)),
            whole_out((tokens, depth)),
            whole_out((tokens, depth)),
            whole_out((8, depth)),
            whole_out((lines, shard, depth)),
            pl.BlockSpec((1, lines, shard, width), lambda i: (jnp.maximum(i - 1, 0), 0, 0, 0)),
            pl.BlockSpec((row_lines, row_count, depth), lambda i: (jnp.maximum(i - 1, 0), 0, 0)),
        ],
        scratch_shapes=[
            pltpu.VMEM((tokens, depth), F32),
            pltpu.VMEM((tokens, depth), BF16),
            pltpu.VMEM((depth, tokens), BF16),
            pltpu.VMEM((tokens, depth), F32),
            pltpu.VMEM((tokens, depth), F32),
            pltpu.VMEM((tokens, chunk), BF16),
            pltpu.VMEM((tokens, width), BF16),
            pltpu.VMEM((2, lines, 2, shard, width), BF16),
            pltpu.VMEM((2, row_lines, 2, row_count, depth), BF16),
            pltpu.VMEM((lines, 2, shard, depth), BF16),
            pltpu.VMEM((steps, lines, shard, width), BF16),
            pltpu.VMEM((steps, row_lines, row_count, depth), BF16),
            pltpu.VMEM((lines, shard, depth), BF16),
            dma((steps, lines)), dma((2, lines)), dma((steps, row_lines)), dma((2, row_lines)),
            dma((lines,)), dma((lines,)),
        ],
        compiler_params=pltpu.CompilerParams(
            vmem_limit_bytes=VMEM_LIMIT, dimension_semantics=("arbitrary",), collective_id=4,
            has_side_effects=True,
        ),
        name="feed_forward",
    )(o, x, dy, wo, gain, gu, wd)


def chunk_rows(count):
    return 32 if count % 32 == 0 else count


def add_rows(dst, parts):
    count = dst.shape[0]
    rows = chunk_rows(count)

    def body(t, carry):
        at = pl.ds(pl.multiple_of(t * rows, rows), rows)
        total = parts[0][at, :].astype(F32)
        for part in parts[1:]:
            total = total + part[at, :].astype(F32)
        dst[at, :] = total.astype(dst.dtype)
        return carry

    lax.fori_loop(0, count // rows, body, 0)


class Reduction:
    def __init__(self, plan, sources, own, near, next_, last, outs, sems):
        self.plan = plan
        self.sources, self.own, self.near, self.next, self.last, self.outs = (
            sources, own, near, next_, last, outs,
        )
        (
            self.own_sem, self.near_sem, self.near_out, self.next_sem, self.next_out,
            self.last_sem, self.last_out,
        ) = sems
        self.side = plan.across

    def line_of(self, low, first, second):
        return second * self.plan.along + first if low else first * self.plan.along + second

    def places(self, j):
        plan = self.plan
        low = j < plan.half
        return (low, plan.b if low else plan.a, plan.a if low else plan.b)

    def piece(self, i, line, j):
        src = self.sources[i]
        if i == 1:
            return src.at[j, line]
        width = src.shape[2] // self.plan.ctx
        return src.at[line, :, pl.ds(j * width, width)]

    def start(self, order):
        plan = self.plan
        for j in order:
            low, first, second = self.places(j)
            for hop in range(1, self.side):
                to = lax.rem(first + hop, self.side)
                dev = (self.line_of(low, to, second) * 2 + plan.core, plan.c)
                for i in range(3):
                    for inner in range(self.side):
                        plan.send(
                            self.piece(i, self.line_of(low, to, inner), j),
                            self.near[i].at[j, hop - 1, inner],
                            self.near_out.at[i, j, hop - 1, inner],
                            self.near_sem.at[i, j, hop - 1, inner],
                            dev,
                        )
            for i in range(3):
                for inner in range(self.side):
                    plan.keep(
                        self.piece(i, self.line_of(low, first, inner), j),
                        self.own[i].at[j, inner],
                        self.own_sem.at[i, j, inner],
                    )

    def step_near(self, j):
        plan = self.plan
        low, first, second = self.places(j)
        for i in range(3):
            for inner in range(self.side):
                plan.arrive(self.own[i].at[j, inner], self.own_sem.at[i, j, inner])
                for hop in range(1, self.side):
                    plan.arrive(
                        self.near[i].at[j, hop - 1, inner], self.near_sem.at[i, j, hop - 1, inner]
                    )
                if not plan.draining:
                    add_rows(
                        self.own[i].at[j, inner],
                        [self.own[i].at[j, inner]]
                        + [self.near[i].at[j, hop - 1, inner] for hop in range(1, self.side)],
                    )
        for hop in range(1, self.side):
            to = lax.rem(second + hop, self.side)
            dev = (self.line_of(low, first, to) * 2 + plan.core, plan.c)
            for i in range(3):
                plan.send(
                    self.own[i].at[j, to],
                    self.next[i].at[j, hop - 1],
                    self.next_out.at[i, j, hop - 1],
                    self.next_sem.at[i, j, hop - 1],
                    dev,
                )

    def step_next(self, j):
        plan = self.plan
        low, first, second = self.places(j)
        mine = plan.c == j
        for i in range(3):
            for hop in range(1, self.side):
                plan.arrive(self.next[i].at[j, hop - 1], self.next_sem.at[i, j, hop - 1])
            if not plan.draining:
                add_rows(
                    self.own[i].at[j, second],
                    [self.own[i].at[j, second]]
                    + [self.next[i].at[j, hop - 1] for hop in range(1, self.side)],
                )
            plan.send(
                self.own[i].at[j, second],
                self.last[i].at[plan.c],
                self.last_out.at[i, j],
                self.last_sem.at[i, plan.c],
                (plan.f, j),
                jnp.logical_not(mine),
            )
            plan.keep(
                self.own[i].at[j, second], self.last[i].at[plan.c], self.last_sem.at[i, plan.c],
                mine,
            )

    def finish(self):
        plan = self.plan
        for i in range(3):
            for j in range(plan.ctx):
                plan.arrive(self.last[i].at[j], self.last_sem.at[i, j])
            add_rows(self.outs[i], [self.last[i].at[j] for j in range(plan.ctx)])


def backward_kernel(
    fsdp, ctx,
    d_out, x_in, q_in, k_in, vm_in, kt_in, att_in, lse, wqkv_in, gain, table_in, start,
    dg_two, s_wo, s_gu, s_wd,
    folded, vout, g_wo, g_gu, g_wd, g_qkv, dg_all,
    part, q, k, vm, kt, att, do, wqkv, table,
    dqt, dkk, dvv, rows_t, d3, gw_full, gw,
    other, chain, gw_near, gw_sum, gw_last, dg, dg_near, dg_sum, dg_last,
    o_wo, o_gu, o_wd, n_wo, n_gu, n_wd, x_wo, x_gu, x_wd, l_wo, l_gu, l_wd,
    load_sem, do_sem, do_out, v_sem, v_out,
    sib_sem, sib_out, chain_sem, chain_out, end_sem, end_out,
    gw_sem, gw_out, gl_sem, gl_out, dn_sem, dn_out, dl_sem, dl_out,
    own_sem, near_sem, near_out, next_sem, next_out, last_sem, last_out,
):
    plan = Plan(fsdp, ctx)
    f, c, core, line, home, half = plan.f, plan.c, plan.core, plan.line, plan.home, plan.half
    lines = plan.lines
    sibling = (line * 2 + 1 - core, c)
    low, high = home * half, home * half + half - 1
    blocks, _, depth = part.shape
    group = blocks * BLOCK
    cols = vm.shape[1]
    heads = cols // HEAD
    tokens = group // ctx
    per = tokens // BLOCK
    pairs = blocks // 2
    plan.barrier()

    for i in range(half):
        for kk in range(2):
            to = core * half + i
            rank = lax.rem(to + kk * half, ctx)
            src = d_out.at[:, pl.ds(pl.multiple_of(rank * cols, cols), cols)]
            mine = both(core == home, c == to, core == kk)
            plan.send(
                src, do.at[c], do_out.at[i * 2 + kk], do_sem.at[c], (line * 2 + kk, to),
                jnp.logical_not(mine),
            )
            plan.keep(src, do.at[c], do_sem.at[c], mine)
    loads = (
        (q_in, q), (k_in, k), (vm_in, vm), (kt_in, kt), (att_in, att), (table_in, table),
        (wqkv_in, wqkv), (x_in, part),
    )
    for i, (src, dst) in enumerate(loads):
        plan.keep(src, dst, load_sem.at[i])
    reduction = Reduction(
        plan, (s_wo, s_gu, s_wd), (o_wo, o_gu, o_wd), (n_wo, n_gu, n_wd), (x_wo, x_gu, x_wd),
        (l_wo, l_gu, l_wd), (g_wo, g_gu, g_wd),
        (own_sem, near_sem, near_out, next_sem, next_out, last_sem, last_out),
    )
    order = []
    for i in range(half):
        order += [i, half + i]
    reduction.start(order)

    dqt[...] = jnp.zeros_like(dqt)
    dkk[...] = jnp.zeros_like(dkk)
    dvv[...] = jnp.zeros_like(dvv)
    gw_full[...] = jnp.zeros_like(gw_full)
    dg[...] = jnp.zeros_like(dg)
    dg[1:2, :] = dg_two[0:1, :]
    for i, (src, dst) in enumerate(loads):
        plan.arrive(dst, load_sem.at[i])
    for j in range(ctx):
        plan.arrive(do.at[j], do_sem.at[j])

    def grads_of(b):
        return do[b // per, pl.ds(pl.multiple_of(lax.rem(b, per) * BLOCK, BLOCK), BLOCK), :]

    def dots(b, carry):
        rows = pl.ds(pl.multiple_of(b * BLOCK, BLOCK), BLOCK)
        prod = grads_of(b).astype(F32) * att[rows, :]
        upper = prod.astype(BF16)
        lower = (prod - upper.astype(F32)).astype(BF16)
        head_row = lax.broadcasted_iota(jnp.int32, (8, cols), 0)
        lane = lax.broadcasted_iota(jnp.int32, (8, cols), 1)
        choose = (lane // HEAD == head_row).astype(F32).astype(BF16)
        rows_t[:, rows] = nt(choose, upper) + nt(choose, lower)
        return carry

    lax.fori_loop(0, blocks, dots, 0)

    def tile(kb, qb):
        krows = pl.ds(pl.multiple_of(kb * BLOCK, BLOCK), BLOCK)
        rows = pl.ds(pl.multiple_of(qb * BLOCK, BLOCK), BLOCK)
        kv = k[krows, :]
        vv = vm[krows, :]
        qv = q[rows, :]
        dov = grads_of(qb)
        key_pos = kb * BLOCK + lax.broadcasted_iota(jnp.int32, (BLOCK, BLOCK), 0)
        query_pos = qb * BLOCK + lax.broadcasted_iota(jnp.int32, (BLOCK, BLOCK), 1)
        allowed = (key_pos <= query_pos) & (key_pos >= start[0:1, rows])
        dk_sum = dkk[krows, :]
        dv_sum = dvv[krows, :]
        for head in range(heads):
            band = slice(head * HEAD, (head + 1) * HEAD)
            lanes = head_lanes(qv.shape, head)
            qm = jnp.where(lanes, qv, jnp.zeros_like(qv))
            dom = jnp.where(lanes, dov, jnp.zeros_like(dov))
            s = jnp.where(allowed, nt(kv, qm), NEGATIVE)
            p = jnp.exp(s - lse[head : head + 1, rows])
            ds = (p * (nt(vv, dom) - rows_t[head : head + 1, rows])).astype(BF16)
            dv_sum = dv_sum + nn(p.astype(BF16), dom)
            dk_sum = dk_sum + nn(ds, qm)
            dqt[band, rows] = dqt[band, rows] + nn(kt[band, krows], ds)
        dkk[krows, :] = dk_sum
        dvv[krows, :] = dv_sum

    def unit_of(t):
        return jnp.where(home == 0, blocks - 1 - t, t)

    def finish(o):
        rows = pl.ds(pl.multiple_of(o * BLOCK, BLOCK), BLOCK)
        cos_v, sin_v = turns(table[rows, :], cols)
        dq = dqt[:, rows].T * (1.0 / math.sqrt(HEAD))
        d3[rows, :cols] = (dq * cos_v - half_swap(dq) * sin_v).astype(BF16)
        dk = dkk[rows, :]
        d3[rows, cols : 2 * cols] = (dk * cos_v - half_swap(dk) * sin_v).astype(BF16)
        d3[rows, 2 * cols :] = (0.5 * dvv[rows, :]).astype(BF16)
        dh = nt(d3[rows, :], wqkv[...])
        xv = part[o].astype(F32)
        rstd = lax.rsqrt(jnp.mean(xv * xv, axis=1, keepdims=True) + EPSILON)
        xhat = xv * rstd
        h1 = (xhat * gain[...]).astype(BF16)
        u = dh * gain[...]
        part[o] = (rstd * (u - xhat * jnp.mean(u * xhat, axis=1, keepdims=True))).astype(BF16)
        dg[0:1, :] = dg[0:1, :] + jnp.sum(dh * xhat, axis=0, keepdims=True)
        gw_full[...] = gw_full[...] + tn(h1, d3[rows, :])

    def give(t):
        o = unit_of(t)
        slot = t // 2
        plan.send(
            part.at[o], other.at[slot], sib_out.at[slot], sib_sem.at[slot], sibling,
            lax.rem(o, 2) != core,
        )

    def pair_unit(i):
        return jnp.where(home == 0, blocks - 2 - 2 * i, 2 * i) + core

    def add_unit(o, src):
        def body(t, carry):
            at = pl.ds(pl.multiple_of(t * 32, 32), 32)
            part[o, at, :] = (part[o, at, :].astype(F32) + src[at, :].astype(F32)).astype(BF16)
            return carry

        lax.fori_loop(0, BLOCK // 32, body, 0)

    def sum_pair(i):
        plan.arrive(other.at[i], sib_sem.at[i])
        if not plan.draining:
            add_unit(pair_unit(i), other.at[i])

    def pass_pair(i, hears):
        o = pair_unit(i)
        j = o // per
        top = jnp.minimum(j, high)
        bottom = jnp.maximum(j, low)
        from_below = both(c > low, c <= top)
        from_above = both(c < high, c >= bottom)
        now = jnp.logical_or(from_below, from_above) == hears
        spot = jnp.where(j == c, pairs, i)
        if hears and not plan.draining:

            @pl.when(from_below)
            def _():
                plan.arrive(chain.at[i], chain_sem.at[i])
                add_unit(o, chain.at[i])

            @pl.when(from_above)
            def _():
                plan.arrive(chain.at[spot], chain_sem.at[spot])
                add_unit(o, chain.at[spot])

        plan.send(
            part.at[o], chain.at[i], chain_out.at[0, i], chain_sem.at[i], (f, c + 1),
            both(now, c < top),
        )
        below = jnp.where(j == c - 1, pairs, i)
        plan.send(
            part.at[o], chain.at[below], chain_out.at[1, i], chain_sem.at[below], (f, c - 1),
            both(now, c > bottom),
        )
        end = jnp.clip(j, low, high)
        mine = both(c == end, j == c, core == home)
        where = lax.rem(o, per)
        dst = folded.at[pl.ds(pl.multiple_of(where * BLOCK, BLOCK), BLOCK), :]
        plan.send(
            part.at[o], dst, end_out.at[i], end_sem.at[where], (line * 2 + home, j),
            both(now, c == end, jnp.logical_not(mine)),
        )
        plan.keep(part.at[o], dst, end_sem.at[where], both(now, mine))

    rank = lax.rem(c + core * half, ctx)

    def give_values(i):
        j = jnp.where(home == 0, ctx - 1 - i, i)
        src = d3.at[pl.ds(pl.multiple_of(j * tokens, tokens), tokens), 2 * cols : 3 * cols]
        dst = vout.at[:, pl.ds(pl.multiple_of(rank * cols, cols), cols)]
        mine = both(core == home, c == j)
        plan.send(
            src, dst, v_out.at[i], v_sem.at[rank], (line * 2 + home, j), jnp.logical_not(mine)
        )
        plan.keep(src, dst, v_sem.at[rank], mine)

    schedule = {}

    def at_step(t, act):
        schedule.setdefault(t, []).append(act)

    scale = blocks // 8
    for j in order[:half]:
        at_step(NEAR_A * scale, lambda j=j: reduction.step_near(j))
        at_step(NEXT_A * scale, lambda j=j: reduction.step_next(j))
    for j in order[half:]:
        at_step(NEAR_B * scale, lambda j=j: reduction.step_near(j))
        at_step(NEXT_B * scale, lambda j=j: reduction.step_next(j))
    for i in range(pairs - 1):
        at_step(2 * i + 1, lambda i=i: give_values(i))
        at_step(2 * i + 2, lambda i=i: sum_pair(i))
        at_step(2 * i + 2, lambda i=i: pass_pair(i, False))
        if i < pairs - 2:
            at_step(2 * i + 4, lambda i=i: pass_pair(i, True))
    at_step(blocks - 1, lambda: give_values(pairs - 1))

    def step(t, carry):
        o = unit_of(t)

        def inner(i, carry2):
            tile(jnp.where(home == 0, i, o), jnp.where(home == 0, o, o + i))
            return carry2

        lax.fori_loop(0, blocks - t, inner, 0)
        finish(o)
        give(t)
        for s in sorted(schedule):

            @pl.when(t == s)
            def _(s=s):
                for act in schedule[s]:
                    act()

        return carry

    plan.started_at_top = plan.started
    plan.started = []
    lax.fori_loop(0, blocks, step, 0)
    plan.started = plan.started_at_top

    for hop in range(1, fsdp):
        dev = (lax.rem(f + hop, fsdp), c)
        plan.send(dg, dg_near.at[f], dn_out.at[hop - 1], dn_sem.at[f], dev)
    plan.keep(dg, dg_near.at[f], dn_sem.at[f])

    pass_pair(pairs - 2, True)
    sum_pair(pairs - 1)
    pass_pair(pairs - 1, False)
    shard = depth // fsdp
    rows_each = BLOCK // shard

    def weight(b, carry):
        at = pl.ds(pl.multiple_of(b * BLOCK, BLOCK), BLOCK)
        val = gw_full[at, :].astype(BF16)
        for r in range(rows_each):
            gw[b * (rows_each // 2) + r // 2, r % 2] = val[r * shard : (r + 1) * shard]
        return carry

    lax.fori_loop(0, depth // BLOCK, weight, 0)
    for hop in range(1, lines):
        to = lax.rem(line + hop, lines)
        plan.send(
            gw.at[to], gw_near.at[hop - 1], gw_out.at[hop - 1], gw_sem.at[hop - 1],
            (to * 2 + core, c),
        )
    pass_pair(pairs - 1, True)

    for at in range(fsdp):
        plan.arrive(dg_near.at[at], dn_sem.at[at])
    total = dg_near[0]
    for at in range(1, fsdp):
        total = total + dg_near[at]
    dg_sum[...] = total
    for hop in range(1, ctx):
        plan.send(
            dg_sum, dg_last.at[c], dl_out.at[hop - 1], dl_sem.at[c], (f, lax.rem(c + hop, ctx))
        )
    plan.keep(dg_sum, dg_last.at[c], dl_sem.at[c])

    for hop in range(1, lines):
        plan.arrive(gw_near.at[hop - 1], gw_sem.at[hop - 1])
    for kk in range(2):
        add_rows(
            gw_sum.at[kk], [gw.at[line, kk]] + [gw_near.at[hop - 1, kk] for hop in range(1, lines)]
        )
    plane = jnp.where(core == 0, c, lax.rem(c + half, ctx))
    for kk in range(2):
        mine = both(core == 0, kk == 0)
        plan.send(
            gw_sum.at[kk], gw_last.at[core], gl_out.at[kk], gl_sem.at[core], (line * 2 + kk, plane),
            jnp.logical_not(mine),
        )
        plan.keep(gw_sum.at[kk], gw_last.at[core], gl_sem.at[core], mine)

    reduction.finish()
    for at in range(ctx):
        plan.arrive(dg_last.at[at], dl_sem.at[at])
    total = dg_last[0]
    for at in range(1, ctx):
        total = total + dg_last[at]
    dg_all[...] = total
    for kk in range(2):
        plan.arrive(gw_last.at[kk], gl_sem.at[kk])
    add_rows(g_qkv, [gw_last.at[0], gw_last.at[1]])
    for at in range(per):
        plan.arrive(folded.at[pl.ds(at * BLOCK, BLOCK), :], end_sem.at[at])
    for at in range(ctx):
        plan.arrive(vout.at[:, pl.ds(at * cols, cols)], v_sem.at[at])
    plan.drain()
    plan.draining = True
    for t in range(blocks):
        give(t)
    for s in sorted(schedule):
        for act in schedule[s]:
            act()


NEAR_A, NEAR_B, NEXT_A, NEXT_B = 1, 3, 4, 6


def backward(mesh, d_out, x, q, k, vm, kt, att, lse, wqkv, gain, table, start, dg_two, sums):
    fsdp, ctx = mesh.shape["fsdp"], mesh.shape["ctx"]
    group, depth = x.shape
    cols = vm.shape[1]
    tokens = group // ctx
    blocks = group // BLOCK
    x = x.reshape(blocks, BLOCK, depth)
    pairs = blocks // 2
    half = ctx // 2
    lines = fsdp // 2
    side = math.isqrt(lines)
    shard = depth // fsdp
    s_wo, s_gu, s_wd = sums
    shapes = (
        (s_wo.shape[1], s_wo.shape[2] // ctx),
        (s_gu.shape[2], s_gu.shape[3]),
        (s_wd.shape[1], s_wd.shape[2] // ctx),
    )
    anywhere = pl.BlockSpec(memory_space=pl.ANY)
    vmem = pl.BlockSpec(memory_space=pltpu.VMEM)
    dma = pltpu.SemaphoreType.DMA
    hops = max(side - 1, 1)

    def low(*shape):
        return pltpu.VMEM(shape, BF16)

    def full(*shape):
        return pltpu.VMEM(shape, F32)

    return pl.pallas_call(
        functools.partial(backward_kernel, fsdp, ctx),
        out_shape=(
            jax.ShapeDtypeStruct((tokens, depth), BF16),
            jax.ShapeDtypeStruct((tokens, depth), BF16),
            jax.ShapeDtypeStruct(shapes[0], F32),
            jax.ShapeDtypeStruct(shapes[1], F32),
            jax.ShapeDtypeStruct(shapes[2], F32),
            jax.ShapeDtypeStruct((shard, 3 * cols), F32),
            jax.ShapeDtypeStruct((8, depth), F32),
        ),
        in_specs=[anywhere] * 7 + [vmem, anywhere, vmem] + [anywhere] + [vmem] * 2 + [anywhere] * 3,
        out_specs=[anywhere] * 2 + [vmem] * 5,
        scratch_shapes=[
            low(blocks, BLOCK, depth), low(group, cols), low(group, cols), low(group, cols),
            low(cols, group), full(group, cols), low(ctx, tokens, cols), low(depth, 3 * cols),
            full(group, table.shape[1]),
            full(cols, group), full(group, cols), full(group, cols),
            full(8, group), low(group, 3 * cols), full(depth, 3 * cols), low(lines, 2, shard, 3 * cols),
            low(pairs, BLOCK, depth), low(pairs + 1, BLOCK, depth),
            low(max(lines - 1, 1), 2, shard, 3 * cols), low(2, shard, 3 * cols),
            low(2, shard, 3 * cols),
            full(8, depth), full(fsdp, 8, depth), full(8, depth), full(ctx, 8, depth),
        ]
        + [low(ctx, side, *shape) for shape in shapes]
        + [low(ctx, hops, side, *shape) for shape in shapes]
        + [low(ctx, hops, *shape) for shape in shapes]
        + [low(ctx, *shape) for shape in shapes]
        + [
            dma((8,)), dma((ctx,)), dma((ctx,)), dma((ctx,)), dma((ctx,)),
            dma((pairs,)), dma((pairs,)), dma((pairs + 1,)), dma((2, pairs)),
            dma((tokens // BLOCK,)), dma((pairs,)),
            dma((lines,)), dma((lines,)), dma((2,)), dma((2,)),
            dma((fsdp,)), dma((fsdp,)), dma((ctx,)), dma((ctx,)),
            dma((3, ctx, side)), dma((3, ctx, hops, side)), dma((3, ctx, hops, side)),
            dma((3, ctx, hops)), dma((3, ctx, hops)), dma((3, ctx)), dma((3, ctx)),
        ],
        compiler_params=pltpu.CompilerParams(
            collective_id=3, has_side_effects=True, vmem_limit_bytes=BACKWARD_LIMIT
        ),
        name="backward",
    )(d_out, x, q, k, vm, kt, att, lse, wqkv, gain, table, start, dg_two, *sums)


def documents(length_row, places):
    doc_ends = jnp.cumsum(length_row)
    doc_starts = doc_ends - length_row
    owner_ids = jnp.sum((places[:, None] >= doc_ends[None, :]).astype(jnp.int32), axis=1)
    chosen = owner_ids[:, None] == jnp.arange(length_row.shape[0], dtype=jnp.int32)[None, :]
    first_place = jnp.sum(jnp.where(chosen, doc_starts[None, :], 0), axis=1)
    return first_place


def tables(length_row, group):
    places = jnp.arange(group, dtype=jnp.int32)
    first = documents(length_row, places)
    half = HEAD // 2
    frequency = jnp.exp(jnp.arange(half).astype(F32) * (-2.0 * math.log(THETA) / HEAD))
    angles = (places - first).astype(F32)[:, None] * frequency[None, :]
    cos, sin = jnp.cos(angles), jnp.sin(angles)
    return jnp.concatenate([cos, cos, -sin, sin], axis=1), first[None, :]


def layer(
    mesh, tokens, value_first, lengths, w_query, w_key, w_value, w_out, w_gate, w_up, w_down,
    gain_attn, gain_ffn, out_grad, value_grad,
):
    fsdp, ctx = mesh.shape["fsdp"], mesh.shape["ctx"]
    count, depth = tokens.shape
    group = count * ctx
    cols = depth // ctx
    rows = depth // fsdp
    f, c = lax.axis_index("fsdp"), lax.axis_index("ctx")
    core = lax.rem(f, 2)
    home = c // (ctx // 2)

    wqkv = jnp.concatenate([w_query, w_key, w_value], axis=1).astype(BF16)
    gu = jnp.concatenate([w_gate, w_up], axis=1).astype(BF16)
    gains = jnp.stack([gain_attn, gain_ffn]).astype(BF16).astype(F32)
    gains = lax.dynamic_update_slice(
        jnp.zeros((8, depth), F32), gains, (jnp.int32(0), (f * rows).astype(jnp.int32))
    )
    other_lengths = lax.ppermute(lengths, "fsdp", [(i, i ^ 1) for i in range(fsdp)])
    length_row = jnp.where(core == home, lengths, other_lengths)[0]
    table, first = tables(length_row, group)

    xs, vs, wq, _, wos, gus, wds, gs = gather(
        mesh, tokens, value_first, wqkv, w_out.astype(BF16), gu, w_down.astype(BF16), gains
    )
    gain_full = jnp.sum(gs, axis=0)
    gain_one, gain_two = gain_full[0:1], gain_full[1:2]
    xg = xs.reshape(group, depth)
    wq = wq.reshape(depth, 3 * cols)
    _, q, k, vm, kt, out, att, lse = forward_attention(
        xg, vs.reshape(group, cols), wq, gain_one, table, first
    )
    attended = trade(mesh, out.reshape(ctx, count, cols), True, 1)
    result, dx2, d_out, dg_two, s_wo, s_gu, s_wd = feed_forward(
        mesh, attended, tokens, out_grad, wos.reshape(depth, depth), gain_two,
        gus.reshape(ctx, depth, gu.shape[1]), wds.reshape(-1, depth),
    )
    folded, dvr, g_wo, g_gu, g_wd, g_qkv, gain_grads = backward(
        mesh, d_out, xg, q, k, vm, kt, att, lse, wq, gain_one, table, first, dg_two,
        (s_wo, s_gu, s_wd),
    )
    gain_grads = lax.dynamic_slice(
        gain_grads, (jnp.int32(0), (f * rows).astype(jnp.int32)), (2, rows)
    )
    ff = w_gate.shape[1]
    return (
        result,
        dx2 + folded.astype(F32),
        value_grad + dvr.astype(F32),
        g_qkv[:, :cols],
        g_qkv[:, cols : 2 * cols],
        g_qkv[:, 2 * cols :],
        g_wo,
        g_gu[:, :ff],
        g_gu[:, ff:],
        g_wd,
        gain_grads[0],
        gain_grads[1],
    )


def solution(mesh):
    rows = P(("fsdp", "ctx"), None)
    shard = P("fsdp", "ctx")
    return jax.shard_map(
        functools.partial(layer, mesh),
        mesh=mesh,
        in_specs=(rows, rows, P("fsdp", None)) + (shard,) * 7 + (P("fsdp"),) * 2 + (rows, rows),
        out_specs=(rows, rows, rows) + (shard,) * 7 + (P("fsdp"),) * 2,
        check_vma=False,
    )
```

time: 723 us -> 486 us (0.67); the launches traced: 709 us -> 484 us
  waiting for transfers between devices: 116 us -> 0.01 us
  local copies, waits for them, and re-layouts: 63.8 us -> 10.2 us
  starting transfers between devices: 31.4 us -> 0.52 us
  other arithmetic: 35 us -> 20.1 us
  between operations: 15.1 us -> 0.81 us
  Pallas kernels: 440 us -> 452 us
  blocking collectives: 8.37 us -> 0 us
    ppermute x29 -> x0, waiting for transfers between devices: 116 us -> none  [the longest x27 107 us: sum_over(): parts.append(lax.ppermute(out, axis_name, perm(hop)))]
    pallas_call x4 -> x3, Pallas kernels: 254 us -> 291 us  [the longest x1 181 us: backward(): pl.pallas_call(functools.partial(backward_kernel, fsdp, ctx), out_shape=(...]
    ppermute x29 -> x0, starting transfers between devices: 30.8 us -> none  [the longest x27 29.7 us: sum_over(): parts.append(lax.ppermute(out, axis_name, perm(hop)))]
    pallas_call x2 -> x1, Pallas kernels: 46.1 us -> 21.8 us  [trade(): pl.pallas_call(functools.partial(trade_kernel, fsdp, ctx, inward), out_sh...]
    unnamed x38 -> x29, local copies, waits for them, and re-layouts: 22.6 us -> 4.84 us
    reshape x2 -> x0, local copies, waits for them, and re-layouts: 14.1 us -> none  [the longest x1 10.5 us: layer(): g_wd.reshape(across, along, 2, rows_d, ctx, cols)]
    convert_element_type x16 -> x0, other arithmetic: 13.6 us -> none  [the longest x3 8.92 us: reduce_shards(): near = sum_over(grad, 'fsdp', 2, core, 2, over_core).astype(BF16)]
    another operation x3 -> x2, local copies, waits for them, and re-layouts: 10.4 us -> 0.29 us
  transfers between devices with their start and end apart: 31 -> 1, of which waited for: 13 -> 0; matrix products, arithmetic and copies ran while one was open for 10% -> 2% of each run, Pallas kernels for 44% -> 29%
where the time goes in v2:
time: 486 us; the launch traced here: 484 us
  Pallas kernels  452 us (93%)
  other arithmetic  20.1 us (4%)
  local copies, waits for them, and re-layouts  10.2 us (2%)
    pallas_call x1, Pallas kernels, backward(): pl.pallas_call(functools.partial(backward_kernel, fsdp, ctx), out_shape=(...  181 us
    pallas_call x1, Pallas kernels, gather(): pl.pallas_call(functools.partial(gather_kernel, fsdp, ctx), out_shape=(ja...  140 us
    pallas_call x1, Pallas kernels, forward_attention(): pl.pallas_call(forward_kernel, out_shape=shapes, in_specs=[vmem] * 6, out...  56.7 us
    pallas_call x1, Pallas kernels, feed_forward(): pl.pallas_call(functools.partial(feed_kernel, fsdp, ctx), grid=(steps + 1...  53.3 us
    pallas_call x1, Pallas kernels, trade(): pl.pallas_call(functools.partial(trade_kernel, fsdp, ctx, inward), out_sh...  21.8 us
  transfers between devices with their start and end apart: 1, of which 0 were waited for; matrix products, arithmetic and copies ran while one was open for 2% of the time, Pallas kernels for 29%

profile of v2, /device:TPU:0, one launch (start us, length us, event | category | flops | bytes accessed | tf_op | source)
XLA Modules:
  0.0 483.6 jit_solution(11979388784464091441)
XLA Ops:
  0.6 0.0 copy-start.4
  0.7 0.0 copy-start.10
  0.7 0.0 copy-start.11
  0.7 0.5 collective-permute-start
  1.2 0.9 convert.23
  2.1 0.9 convert.24
  3.0 0.9 convert.25
  3.9 1.5 convert_element_type.35.wo
  5.5 1.0 convert.26
  6.5 0.1 copy.34
  6.6 1.0 convert.27
  7.6 0.1 copy.35
  7.8 0.0 copy-done.4
  7.8 0.7 convert_element_type.36.wd
  8.5 0.0 copy-done.10
  8.5 0.0 copy-done.11
  8.5 0.0 copy-start.9
  8.5 0.9 pad_maximum_fusion.1.gu
  9.4 0.7 pad_maximum_fusion.2.wqkv
  10.1 0.0 copy-start.6
  10.1 0.6 copy-done.6
  10.7 139.5 %gather_all.1 = (bf16[4,512,1024]{2,1,0:T(8,128)(2,1)}, bf16[4,512,256]{2,1,0:T(8,128)(2,1)}, bf16[8,128,768]{2,1,0:T(8,128)(2,1)}, bf16[128,768]{1,0:T(8,128)(2...) custom-call(bf16[512,1024]{1,0:T(8,128)(2,1)} %x.3, ...), custom_call_target="tpu_custom_call" | custom-call | tf_op jit(solution)/shard_map/gather_all/pallas_call | solution.py:451
  150.2 1.0 reduce_sum.27
  151.2 0.6 fusion.5
  151.8 0.0 collective-permute-done
  151.8 0.0 copy-done.9
  151.8 0.2 reduce-window.4
  152.0 0.1 convert_reduce_fusion
  152.1 0.1 select_reduce_fusion
  152.2 0.0 copy-start.8
  152.2 3.7 multiply_cosine_fusion
  155.9 1.9 pad_maximum_fusion.table.table_in
  157.8 0.0 copy-done.8
  157.8 56.7 %attention_forward.1 = (bf16[2048,1024]{1,0:T(8,128)(2,1)}, bf16[2048,256]{1,0:T(8,128)(2,1)}, bf16[2048,256]{1,0:T(8,128)(2,1)}, bf16[2048,256]{1,0:T(8,128)(2,...) custom-call(bf16[2048,1024]{1,0:T(8,128)(2,1)} %bitcast.26, ...), custom_call_target="tpu_custom_call" | custom-call | tf_op jit(solution)/shard_map/attention_forward/pallas_call | solution.py:149
  214.5 21.8 %trade_in.1.o = bf16[512,1024]{1,0:T(8,128)(2,1)} custom-call(bf16[4,512,256]{2,1,0:T(8,128)(2,1)} %bitcast.34), custom_call_target="tpu_custom_call" | custom-call | tf_op jit(solution)/shard_map/trade_in/pallas_call | solution.py:521
  236.3 53.3 %feed_forward.1 = (bf16[512,1024]{1,0:T(8,128)(2,1)}, f32[512,1024]{1,0:T(8,128)}, bf16[512,1024]{1,0:T(8,128)(2,1)}, f32[8,1024]{1,0:T(8,128)}, bf16[4,128,1024...) custom-call(bf16[512,1024]{1,0:T(8,128)(2,1)} %trade_in.1.o, ...), custom_call_target="tpu_custom_call" | custom-call | tf_op jit(solution)/shard_map/feed_forward/pallas_call | solution.py:732
  289.6 180.7 %backward.1 = (bf16[512,1024]{1,0:T(8,128)(2,1)}, bf16[512,1024]{1,0:T(8,128)(2,1)}, f32[128,256]{1,0:T(8,128)}, f32[128,1408]{1,0:T(8,128)}, f32[352,256]{1,0:T...) custom-call(bf16[512,1024]{1,0:T(8,128)(2,1)} %get-tuple-element.50.d_out, bf16[8,256,1024]{2,1,0:T(8,128)(2,1)} %bitcast.27, ...), custom_call_target="tpu_custom_call" | custom-call | tf_op jit(solution)/shard_map/backward/pallas_call | solution.py:1269
  470.4 0.0 copy-start.1
  470.4 0.8 constant_dynamic-slice_fusion
  471.2 0.5 slice_bitcast_fusion
  471.7 1.8 fusion.4
  473.5 1.3 fusion.3
  474.8 0.9 copy.38
  475.7 0.9 copy.37
  476.6 0.0 copy-done.1
  476.6 0.0 copy-start
  476.6 0.0 copy-start.2
  476.6 3.0 convert_add_fusion.1
  479.6 0.0 copy-done
  479.6 0.0 copy-done.2
  479.6 0.0 copy-start.3
  479.6 1.6 convert_add_fusion
  481.2 0.0 copy-start.7
  481.2 0.0 copy-start.5
  481.2 0.0 copy-done.3
  481.2 1.0 copy.43
  482.2 0.0 copy-done.7
  482.2 0.7 copy.44
  482.9 0.0 copy-done.5
  482.9 0.7 copy.45
  (7 shorter events, 0.0 us)
Async XLA Ops:
  0.6 7.2 %copy-start.4 = (f32[352,256]{1,0:T(8,128)S(1)}, f32[352,256]{1,0:T(8,128)}, u32[]{:S(2)}) copy-start(f32[352,256]{1,0:T(8,128)} %param.23) | copy-start | bytes 1081348
  0.7 7.9 %copy-start.10 = (f32[128]{0:T(128)S(1)}, f32[128]{0:T(128)}, u32[]{:S(2)}) copy-start(f32[128]{0:T(128)} %param.25) | copy-start | bytes 1540
  0.7 7.8 %copy-start.11 = (f32[128]{0:T(128)S(1)}, f32[128]{0:T(128)}, u32[]{:S(2)}) copy-start(f32[128]{0:T(128)} %param.24) | copy-start | bytes 1540
  0.7 151.1 %collective-permute-start = (s32[1,4]{1,0:T(1,128)}, s32[1,4]{1,0:T(1,128)S(1)}, u32[]{:S(2)}, u32[]{:S(2)}) collective-permute-start(s32[1,4]{1,0:T(1,128)} %param.16), channel_id=1, source_target_pairs={{0,4},{4,0},{8,12},{12,8},{16,20},{20,16},{24,28},{28,24},{1,5},{5... | collective-permute-start | bytes 56 | tf_op jit(solution)/shard_map/ppermute | solution.py:1351
  8.5 143.3 %copy-start.9 = (s32[1,4]{1,0:T(1,128)S(1)}, s32[1,4]{1,0:T(1,128)}, u32[]{:S(2)}) copy-start(s32[1,4]{1,0:T(1,128)} %param.16) | copy-start | bytes 52
  10.1 0.6 copy-start.6
  152.2 5.6 %copy-start.8 = (s32[2048]{0:T(1024)}, s32[2048]{0:T(1024)S(1)}, u32[]{:S(2)}) copy-start(s32[2048]{0:T(1024)S(1)} %select_reduce_fusion) | copy-start | bytes 24580
  470.4 6.2 %copy-start.1 = (f32[512,1024]{1,0:T(8,128)S(1)}, f32[512,1024]{1,0:T(8,128)}, u32[]{:S(2)}) copy-start(f32[512,1024]{1,0:T(8,128)} %get-tuple-element.49) | copy-start | bytes 6291460
  476.6 3.0 copy-start
  476.6 3.0 copy-start.2
  479.6 1.6 copy-start.3
  481.2 1.0 copy-start.7
  481.2 1.7 copy-start.5

commit v3 on v2

v3 whole, which is shorter than its diff:
```python
import functools
import math

import jax
import jax.numpy as jnp
from jax import lax
from jax.experimental import pallas as pl
from jax.experimental.pallas import tpu as pltpu
from jax.sharding import PartitionSpec as P

HEAD = 64
EPSILON = 1e-05
THETA = 10000.0
NEGATIVE = -1e30
BLOCK = 256
VMEM_LIMIT = 58 * 1024 * 1024
BACKWARD_LIMIT = 58 * 1024 * 1024
MESH = pl.DeviceIdType.MESH
BF16 = jnp.bfloat16
F32 = jnp.float32


def nn(left, right):
    return lax.dot_general(left, right, (((1,), (0,)), ((), ())), preferred_element_type=F32)


def nt(left, right):
    return lax.dot_general(left, right, (((1,), (1,)), ((), ())), preferred_element_type=F32)


def tn(left, right):
    return lax.dot_general(left, right, (((0,), (0,)), ((), ())), preferred_element_type=F32)


def turns(table, width):
    lane = lax.broadcasted_iota(jnp.int32, table.shape, 1)
    swapped = pltpu.roll(table, HEAD, 1)
    cos = jnp.where(lane < HEAD, table, swapped)
    sin = jnp.where(lane < HEAD, swapped, table)
    times = width // table.shape[1]
    return jnp.concatenate([cos] * times, axis=1), jnp.concatenate([sin] * times, axis=1)


def half_swap(rows):
    width = rows.shape[1]
    lane = lax.broadcasted_iota(jnp.int32, rows.shape, 1)
    low = lax.rem(lane, HEAD) < HEAD // 2
    return jnp.where(
        low,
        pltpu.roll(rows, width - HEAD // 2, 1),
        pltpu.roll(rows, HEAD // 2, 1),
    )


def head_lanes(shape, head):
    lane = lax.broadcasted_iota(jnp.int32, shape, 1)
    return (lane >= head * HEAD) & (lane < (head + 1) * HEAD)


class Plan:
    def __init__(self, fsdp, ctx):
        self.fsdp, self.ctx = fsdp, ctx
        self.lines = fsdp // 2
        self.across = math.isqrt(self.lines)
        self.along = self.lines // self.across
        self.half = ctx // 2
        self.f = lax.axis_index("fsdp")
        self.c = lax.axis_index("ctx")
        self.core = lax.rem(self.f, 2)
        self.line = self.f // 2
        self.a = self.line // self.along
        self.b = lax.rem(self.line, self.along)
        self.home = self.c // self.half
        self.started = []
        self.draining = False

    def barrier(self):
        sem = pltpu.get_barrier_semaphore()
        count = 0
        for step in range(1, self.fsdp):
            dev = (lax.rem(self.f + step, self.fsdp), self.c)
            pl.semaphore_signal(sem, inc=1, device_id=dev, device_id_type=MESH)
            count += 1
        for step in range(1, self.ctx):
            for core in range(2):
                dev = (self.line * 2 + core, lax.rem(self.c + step, self.ctx))
                pl.semaphore_signal(sem, inc=1, device_id=dev, device_id_type=MESH)
                count += 1
        pl.semaphore_wait(sem, count)

    def greet_plane(self):
        sem = pltpu.get_barrier_semaphore()
        for step in range(1, self.fsdp):
            dev = (lax.rem(self.f + step, self.fsdp), self.c)
            pl.semaphore_signal(sem, inc=1, device_id=dev, device_id_type=MESH)
        pl.semaphore_wait(sem, self.fsdp - 1)

    def when(self, cond, act):
        if cond is True:
            act()
        else:
            pl.when(cond)(act)

    def send(self, src, dst, send_sem, recv_sem, dev, cond=True):
        def copy():
            return pltpu.make_async_remote_copy(
                src_ref=src, dst_ref=dst, send_sem=send_sem, recv_sem=recv_sem,
                device_id=dev, device_id_type=MESH,
            )

        if self.draining:
            self.when(cond, lambda: copy().wait_send())
            return
        self.when(cond, lambda: copy().start())
        self.started.append((cond, lambda: copy().wait_send()))

    def keep(self, src, dst, sem, cond=True):
        if self.draining:
            return
        self.when(cond, lambda: pltpu.make_async_copy(src, dst, sem).start())

    def arrive(self, dst, sem, cond=True):
        if self.draining:
            return
        self.when(cond, lambda: pltpu.make_async_copy(dst, dst, sem).wait())

    def drain(self):
        for cond, act in self.started:
            self.when(cond, act)
        self.started = []


def both(*conds):
    out = True
    for cond in conds:
        if cond is not True:
            out = cond if out is True else jnp.logical_and(out, cond)
    return out


class Gathering:
    def __init__(self, plan, own, whole, sems):
        self.plan, self.own, self.whole = plan, own, whole
        self.sem, self.z_out, self.p_out, self.s_out = sems
        self.widths = (own[0].shape[1], None, own[2].shape[1])

    def spots(self, row, j):
        wos, gus, wds = self.whole

        def band(width):
            return pl.ds(pl.multiple_of(j * width, width), width)

        return (
            wos.at[row, :, band(self.widths[0])], gus.at[j, row], wds.at[row, :, band(self.widths[2])],
        )

    def along_ctx(self, srcs, j, cond, up, down, items=(0, 1, 2)):
        plan = self.plan
        dsts = self.spots(plan.f, j)
        for i in items:
            if up:
                plan.send(
                    srcs[i], dsts[i], self.z_out.at[i, 0, j], self.sem.at[i, plan.f, j],
                    (plan.f, plan.c + 1), both(cond, plan.c < plan.ctx - 1),
                )
            if down:
                plan.send(
                    srcs[i], dsts[i], self.z_out.at[i, 1, j], self.sem.at[i, plan.f, j],
                    (plan.f, plan.c - 1), both(cond, plan.c > 0),
                )

    def on_plane(self, srcs, row, line, j, cond, over_a, over_b, items=(0, 1, 2)):
        plan = self.plan
        dsts = self.spots(row, j)
        for i in items:
            if over_a is not False:
                for hop in range(1, plan.across):
                    to = (lax.rem(plan.a + hop, plan.across) * plan.along + plan.b) * 2 + plan.core
                    plan.send(
                        srcs[i], dsts[i], self.p_out.at[i, hop - 1, line, j],
                        self.sem.at[i, row, j], (to, plan.c), both(cond, over_a),
                    )
            if over_b is not False:
                for hop in range(1, plan.along):
                    to = (plan.a * plan.along + lax.rem(plan.b + hop, plan.along)) * 2 + plan.core
                    plan.send(
                        srcs[i], dsts[i], self.p_out.at[i, plan.across + hop - 2, line, j],
                        self.sem.at[i, row, j], (to, plan.c), both(cond, over_b),
                    )
            plan.send(
                srcs[i], dsts[i], self.s_out.at[i, line, j], self.sem.at[i, row, j],
                (plan.line * 2 + 1 - plan.core, plan.c), cond,
            )

    def near(self, dist):
        plan = self.plan
        for side in range(2 if dist else 1):
            j = plan.c - dist if side == 0 else plan.c + dist
            there = True if dist == 0 else (j >= 0 if side == 0 else j < plan.ctx)
            yield jnp.clip(j, 0, plan.ctx - 1), there, side

    def start_ctx(self):
        self.along_ctx(self.own, self.plan.c, True, True, True)

    def start_plane(self):
        plan = self.plan
        self.on_plane(self.own, plan.f, plan.line, plan.c, True, True, True)
        for src, dst, i in zip(self.own, self.spots(plan.f, plan.c), range(3)):
            plan.keep(src, dst, self.sem.at[i, plan.f, plan.c])

    def wait(self, row, j, cond=True, items=(0, 1, 2)):
        dsts = self.spots(row, j)
        for i in items:
            self.plan.arrive(dsts[i], self.sem.at[i, row, j], cond)
        return dsts

    def from_ctx(self, dist):
        plan = self.plan
        for j, there, side in self.near(dist):
            for i in ORDER:
                dsts = self.wait(plan.f, j, there, (i,))
                self.along_ctx(dsts, j, there, side == 0, side == 1, (i,))
                self.on_plane(dsts, plan.f, plan.line, j, there, True, True, (i,))

    def from_plane(self, dist):
        plan = self.plan
        for j, there, _ in self.near(dist):
            first = j < plan.half
            for hop in range(1, plan.across):
                line = lax.rem(plan.a + plan.across - hop, plan.across) * plan.along + plan.b
                row = line * 2 + plan.core
                for i in ORDER:
                    dsts = self.wait(row, j, there, (i,))
                    self.on_plane(dsts, row, line, j, there, False, first, (i,))
            for hop in range(1, plan.along):
                line = plan.a * plan.along + lax.rem(plan.b + plan.along - hop, plan.along)
                row = line * 2 + plan.core
                for i in ORDER:
                    dsts = self.wait(row, j, there, (i,))
                    self.on_plane(
                        dsts, row, line, j, there, jnp.logical_not(first), False, (i,)
                    )

    def from_far(self, dist):
        plan = self.plan
        for j, there, _ in self.near(dist):
            for hop in range(1, plan.across):
                for hop2 in range(1, plan.along):
                    line = lax.rem(plan.a + hop, plan.across) * plan.along + lax.rem(
                        plan.b + hop2, plan.along
                    )
                    row = line * 2 + plan.core
                    for i in ORDER:
                        dsts = self.wait(row, j, there, (i,))
                        self.on_plane(dsts, row, line, j, there, False, False, (i,))

    def finish(self):
        plan = self.plan
        self.wait(plan.f, plan.c)

        def other(line, carry):
            for j in range(plan.ctx):
                self.wait(line * 2 + 1 - plan.core, j)
            return carry

        lax.fori_loop(0, plan.lines, other, 0)


def forward_kernel(
    fsdp, ctx,
    x, vf, w_q, w_k, w_v, w_o, w_g, w_u, w_d, small,
    attended, wos, gus, wds, x_out_ref, q_ref, k_ref, vm_ref, kt_ref, att_ref, wq_ref,
    lse, table, start, gain,
    xs, vs, wq, wqh, own_q, own_o, own_g, own_d, gs, q, k, vm, kt, vt, att, out, acc, mx, tot,
    x_sem, x_out, v_sem, v_out, q_sem, q_out, h_sem, g_sem, g_out,
    w_sem, w_z, w_p, w_s, o_sem, o_out, save_sem,
):
    plan = Plan(fsdp, ctx)
    f, c, core, line, home, half = plan.f, plan.c, plan.core, plan.line, plan.home, plan.half
    tokens, depth = x.shape
    group = tokens * ctx
    cols = depth // ctx
    heads = cols // HEAD
    blocks = group // BLOCK
    per = tokens // BLOCK
    owner = core == home
    away = jnp.logical_not(owner)
    sibling = (line * 2 + 1 - core, c)

    own_o[...] = w_o[...].astype(BF16)
    own_g[...] = jnp.concatenate([w_g[...].astype(BF16), w_u[...].astype(BF16)], axis=1)
    own_d[...] = w_d[...].astype(BF16)
    own_q[...] = jnp.concatenate(
        [w_q[...].astype(BF16), w_k[...].astype(BF16), w_v[...].astype(BF16)], axis=1
    )
    plan.barrier()
    gathering = Gathering(
        plan, (own_o, own_g, own_d), (wos, gus, wds), (w_sem, w_z, w_p, w_s)
    )

    for hop in range(1, fsdp):
        plan.send(small, gs.at[f], g_out.at[hop - 1], g_sem.at[f], (lax.rem(f + hop, fsdp), c))
    plan.keep(small, gs.at[f], g_sem.at[f])
    plan.send(own_q, wqh, h_sem.at[0], h_sem.at[1], (f, lax.rem(c + half, ctx)))

    piece = tokens // PIECES

    def part_of(ref, i):
        return ref.at[pl.ds(i * piece, piece), :]

    def spread_x(src, j, i, below, above, cond):
        dst = part_of(xs.at[j], i)
        if below:
            plan.send(
                src, dst, x_out.at[0, j, i], x_sem.at[j, i], (f, c - 1),
                both(cond, c > home * half),
            )
        if above:
            plan.send(
                src, dst, x_out.at[1, j, i], x_sem.at[j, i], (f, c + 1),
                both(cond, c < home * half + half - 1),
            )
        plan.send(src, dst, x_out.at[2, j, i], x_sem.at[j, i], sibling, cond)

    entry = jnp.where(core == 0, half - 1, half)
    for i in range(PIECES):
        src = part_of(x, i)
        plan.send(
            src, part_of(xs.at[c], i), x_out.at[0, c, i], x_sem.at[c, i], (f, entry), away
        )
        spread_x(src, c, i, True, True, owner)
        plan.keep(src, part_of(xs.at[c], i), x_sem.at[c, i], owner)
    for at in range(plan.lines):
        plan.send(
            own_q, wq.at[f], q_out.at[0, at], q_sem.at[f], (at * 2, c),
            jnp.logical_not(f == at * 2),
        )
    plan.keep(own_q, wq.at[f], q_sem.at[f], core == 0)
    for i in range(half):
        for kk in range(2):
            to = core * half + i
            rank = lax.rem(to + kk * half, ctx)
            src = vf.at[:, pl.ds(pl.multiple_of(rank * cols, cols), cols)]
            mine = both(owner, c == to, core == kk)
            plan.send(
                src, vs.at[c], v_out.at[i, kk], v_sem.at[c], (line * 2 + kk, to),
                jnp.logical_not(mine),
            )
            plan.keep(src, vs.at[c], v_sem.at[c], mine)
    gathering.start_plane()

    for row in range(fsdp):
        plan.arrive(gs.at[row], g_sem.at[row])
    total = gs[0]
    for row in range(1, fsdp):
        total = total + gs[row]
    gain[...] = total
    lens = gs[line * 2 + home]
    doc_count = SHORTS_AND_LONG

    def firsts(places):
        end = jnp.zeros((1, 1), F32)
        first = jnp.zeros(places.shape, F32)
        for d in range(doc_count):
            size = lens[2:3, d : d + 1]
            end = end + size
            first = first + jnp.where(places >= end, size, 0.0)
        return first

    places = lax.broadcasted_iota(jnp.int32, (1, group), 1).astype(F32)
    start[...] = firsts(places).astype(jnp.int32)

    def angles(b, carry):
        rows = pl.ds(pl.multiple_of(b * BLOCK, BLOCK), BLOCK)
        at = (b * BLOCK + lax.broadcasted_iota(jnp.int32, (BLOCK, 128), 0)).astype(F32)
        lane = lax.broadcasted_iota(jnp.int32, (BLOCK, 128), 1)
        pair = lax.rem(lane, HEAD // 2).astype(F32)
        angle = (at - firsts(at)) * jnp.exp(pair * (-2.0 * math.log(THETA) / HEAD))
        sine = jnp.sin(angle)
        table[rows, :] = jnp.where(
            lane < HEAD, jnp.cos(angle), jnp.where(lane < HEAD + HEAD // 2, -sine, sine)
        )
        return carry

    lax.fori_loop(0, blocks, angles, 0)

    plan.arrive(wqh, h_sem.at[1])
    for at in range(plan.lines):
        plan.send(
            wqh, wq.at[f], q_out.at[1, at], q_sem.at[f], (at * 2 + 1, c),
            jnp.logical_not(f == at * 2 + 1),
        )
    plan.keep(wqh, wq.at[f], q_sem.at[f], core == 1)

    def project(j):
        def body(i, carry):
            rows = pl.ds(pl.multiple_of(j * tokens + i * BLOCK, BLOCK), BLOCK)
            xv = xs[j, pl.ds(pl.multiple_of(i * BLOCK, BLOCK), BLOCK), :].astype(F32)
            rstd = lax.rsqrt(jnp.mean(xv * xv, axis=1, keepdims=True) + EPSILON)
            hv = (xv * rstd * gain[0:1, :]).astype(BF16)
            raw = nn(hv, wq[...].reshape(depth, 3 * cols))
            cos_v, sin_v = turns(table[rows, :], cols)
            rq = raw[:, :cols]
            rk = raw[:, cols : 2 * cols]
            qv = (rq * cos_v + half_swap(rq) * sin_v).astype(BF16)
            q[rows, :] = (qv.astype(F32) * (1.0 / math.sqrt(HEAD))).astype(BF16)
            kv = (rk * cos_v + half_swap(rk) * sin_v).astype(BF16)
            k[rows, :] = kv
            kt[:, rows] = kv.T
            att[rows, :] = 0.5 * raw[:, 2 * cols :]
            return carry

        lax.fori_loop(0, per, body, 0)

    def actions(place):
        out = [gathering.start_ctx] if place == START else []
        for kind in ("from_ctx", "from_plane", "from_far"):
            for dist in range(ctx):
                if (kind, dist) != ("from_ctx", 0) and place == spot_of(kind, dist, ctx, blocks):
                    out.append(functools.partial(getattr(gathering, kind), dist))
        return out

    for dist in range(ctx):
        for i in range(PIECES):
            for j, there, side in gathering.near(dist):
                spot = part_of(xs.at[j], i)
                plan.arrive(spot, x_sem.at[j, i], there)
                if dist:
                    spread_x(spot, j, i, side == 1, side == 0, both(owner, there))
        for act in actions(("x", dist)):
            act()
    for row in range(fsdp):
        plan.arrive(wq.at[row], q_sem.at[row])
    for act in actions("q"):
        act()
    for j in range(ctx):
        project(j)
    for act in actions("p"):
        act()
    saves = [(xs, x_out_ref), (q, q_ref), (k, k_ref), (kt, kt_ref), (wq, wq_ref)]
    for i, (src, dst) in enumerate(saves):
        plan.keep(src, dst, save_sem.at[i])
    for j in range(ctx):
        plan.arrive(vs.at[j], v_sem.at[j])

    def mix(b, carry):
        rows = pl.ds(pl.multiple_of(b * BLOCK, BLOCK), BLOCK)
        first = vs[b // per, pl.ds(pl.multiple_of(lax.rem(b, per) * BLOCK, BLOCK), BLOCK), :]
        mixed = (att[rows, :] + 0.5 * first.astype(F32)).astype(BF16)
        vm[rows, :] = mixed
        vt[:, rows] = mixed.T
        return carry

    lax.fori_loop(0, blocks, mix, 0)
    plan.keep(vm, vm_ref, save_sem.at[5])

    rank = lax.rem(c + core * half, ctx)

    def give(b):
        j = b // per
        where = lax.rem(b, per)
        src = out.at[pl.ds(pl.multiple_of(b * BLOCK, BLOCK), BLOCK), :]
        dst = attended.at[
            pl.ds(pl.multiple_of(where * BLOCK, BLOCK), BLOCK),
            pl.ds(pl.multiple_of(rank * cols, cols), cols),
        ]
        mine = both(owner, c == j)
        plan.send(
            src, dst, o_out.at[b], o_sem.at[rank, where], (line * 2 + home, j),
            jnp.logical_not(mine),
        )
        plan.keep(src, dst, o_sem.at[rank, where], mine)

    schedule = {}

    def at_step(t, act):
        schedule.setdefault(min(t, blocks - 1), []).append(act)

    for place in range(blocks):
        for act in actions(("t", place)):
            at_step(place, act)

    def unit(t, carry):
        b = blocks - 1 - t
        rows = pl.ds(pl.multiple_of(b * BLOCK, BLOCK), BLOCK)
        acc[...] = jnp.zeros_like(acc)
        mx[...] = jnp.full_like(mx, NEGATIVE)
        tot[...] = jnp.zeros_like(tot)
        qv = q[rows, :]
        first = start[0:1, rows]

        def keys(kb, inner):
            krows = pl.ds(pl.multiple_of(kb * BLOCK, BLOCK), BLOCK)
            kv = k[krows, :]
            key_pos = kb * BLOCK + lax.broadcasted_iota(jnp.int32, (BLOCK, BLOCK), 0)
            query_pos = b * BLOCK + lax.broadcasted_iota(jnp.int32, (BLOCK, BLOCK), 1)
            allowed = (key_pos <= query_pos) & (key_pos >= first)
            for head in range(heads):
                band = slice(head * HEAD, (head + 1) * HEAD)
                qm = jnp.where(head_lanes(qv.shape, head), qv, jnp.zeros_like(qv))
                s = jnp.where(allowed, nt(kv, qm), NEGATIVE)
                old = mx[head : head + 1, :]
                new = jnp.maximum(old, jnp.max(s, axis=0, keepdims=True))
                p = jnp.exp(s - new)
                shrink = jnp.exp(old - new)
                mx[head : head + 1, :] = new
                tot[head : head + 1, :] = tot[head : head + 1, :] * shrink + jnp.sum(
                    p, axis=0, keepdims=True
                )
                acc[band, :] = acc[band, :] * shrink + nn(vt[band, krows], p.astype(BF16))
            return inner

        lax.fori_loop(0, b + 1, keys, 0)
        for head in range(heads):
            band = slice(head * HEAD, (head + 1) * HEAD)
            acc[band, :] = acc[band, :] / tot[head : head + 1, :]
        ov = acc[...].T
        att[rows, :] = ov
        out[rows, :] = ov.astype(BF16)
        lse[:, rows] = mx[...] + jnp.log(tot[...])
        give(b)
        for s in sorted(schedule):

            @pl.when(t == s)
            def _(s=s):
                for act in schedule[s]:
                    act()

        return carry

    kept = plan.started
    plan.started = []
    lax.fori_loop(0, blocks, unit, 0)
    plan.started = kept
    plan.keep(att, att_ref, save_sem.at[6])
    for act in actions("late"):
        act()
    gathering.finish()
    for at in range(ctx):
        for where in range(per):
            plan.arrive(
                attended.at[pl.ds(where * BLOCK, BLOCK), pl.ds(at * cols, cols)],
                o_sem.at[at, where],
            )
    for i, (src, dst) in enumerate(saves + [(vm, vm_ref), (att, att_ref)]):
        plan.arrive(dst, save_sem.at[i])
    plan.drain()
    plan.draining = True
    for b in range(blocks):
        give(b)
    for s in sorted(schedule):
        for act in schedule[s]:
            act()


ORDER = (0, 1, 2)
PIECES = 4
START = ('x', 0)
SHORTS_AND_LONG = 4
SPOTS = {
    "from_ctx": (None, ('x', 2), ('x', 3), 'q'),
    "from_plane": (('x', 2), ('x', 3), 'p', ('t', 2)),
    "from_far": (('t', 0), ('t', 2), ('t', 4), 'late'),
}


def spot_of(kind, dist, ctx, blocks):
    if dist >= 4:
        return "p" if kind == "from_ctx" else "late"
    spot = SPOTS[kind][dist]
    return ("t", spot[1] * (blocks // 8)) if spot[0] == "t" else spot


def forward(mesh, x, vf, weights, small):
    fsdp, ctx = mesh.shape["fsdp"], mesh.shape["ctx"]
    tokens, depth = x.shape
    cols = depth // ctx
    group = tokens * ctx
    blocks = group // BLOCK
    per = tokens // BLOCK
    lines = fsdp // 2
    across = math.isqrt(lines)
    peers = max(across - 1 + lines // across - 1, 1)
    shard = depth // fsdp
    out_shape = weights[3].shape
    up_shape = (weights[4].shape[0], 2 * weights[4].shape[1])
    down_shape = weights[6].shape
    anywhere = pl.BlockSpec(memory_space=pl.ANY)
    vmem = pl.BlockSpec(memory_space=pltpu.VMEM)
    dma = pltpu.SemaphoreType.DMA

    def low(*shape):
        return pltpu.VMEM(shape, BF16)

    def full(*shape):
        return pltpu.VMEM(shape, F32)

    def array(dtype, *shape):
        return jax.ShapeDtypeStruct(shape, dtype)

    return pl.pallas_call(
        functools.partial(forward_kernel, fsdp, ctx),
        out_shape=(
            array(BF16, tokens, depth),
            array(BF16, fsdp, out_shape[0], depth),
            array(BF16, ctx, fsdp, *up_shape),
            array(BF16, fsdp, down_shape[0], depth),
            array(BF16, ctx, tokens, depth),
            array(BF16, group, cols),
            array(BF16, group, cols),
            array(BF16, group, cols),
            array(BF16, cols, group),
            array(F32, group, cols),
            array(BF16, fsdp, shard, 3 * cols),
            array(F32, 8, group),
            array(F32, group, 128),
            array(jnp.int32, 1, group),
            array(F32, 8, depth),
        ),
        in_specs=[anywhere] * 2 + [vmem] * 8,
        out_specs=[anywhere] * 11 + [vmem] * 4,
        scratch_shapes=[
            low(ctx, tokens, depth), low(ctx, tokens, cols), low(fsdp, shard, 3 * cols),
            low(shard, 3 * cols), low(shard, 3 * cols), low(*out_shape), low(*up_shape),
            low(*down_shape), full(fsdp, 8, depth),
            low(group, cols), low(group, cols), low(group, cols), low(cols, group),
            low(cols, group), full(group, cols), low(group, cols),
            full(cols, BLOCK), full(8, BLOCK), full(8, BLOCK),
            dma((ctx, PIECES)), dma((3, ctx, PIECES)), dma((ctx,)), dma((ctx // 2, 2)),
            dma((fsdp,)), dma((2, lines)), dma((2,)), dma((fsdp,)), dma((fsdp,)),
            dma((3, fsdp, ctx)), dma((3, 2, ctx)), dma((3, peers, lines, ctx)), dma((3, lines, ctx)),
            dma((ctx, per)), dma((blocks,)), dma((7,)),
        ],
        compiler_params=pltpu.CompilerParams(
            collective_id=0, has_side_effects=True, vmem_limit_bytes=VMEM_LIMIT
        ),
        name="forward",
    )(x, vf, *weights, small)


def chunk_order(i, ctx):
    return i % 2 * (ctx // 2) + i // 2


def reduce_line(plan, low, first, second):
    return second * plan.along + first if low else first * plan.along + second


def reduce_places(plan, j):
    low = j < plan.half
    return (low, plan.b if low else plan.a, plan.a if low else plan.b)


def feed_kernel(
    fsdp, ctx,
    o, x, dy, wo, gain, gu, wd,
    out, dx2, do, dg, s_wo, s_gu, s_wd, early,
    x2, h2, h2t, total, act, dgu,
    my_gu, my_wd, my_wo, got_gu, got_wd, got_wo, near_gu,
    gu_sem, gu_out, wd_sem, wd_out, wo_sem, wo_out, near_sem, near_out,
):
    plan = Plan(fsdp, ctx)
    core = plan.core
    sibling = (plan.line * 2 + 1 - core, plan.c)
    step = pl.program_id(0)
    last = pl.num_programs(0) - 1
    tokens, depth = x.shape
    chunk = wd.shape[0]
    blocks = tokens // BLOCK
    lines = plan.lines
    shard = depth // fsdp
    row_lines = my_wd.shape[1]
    row_count = my_wd.shape[3]
    slot = lax.rem(step, 2)
    half, side = plan.half, plan.across

    def give(at):
        place = lax.rem(at, 2)
        for i in range(lines):
            plan.send(
                my_gu.at[place, i, 1 - core], got_gu.at[at, i], gu_out.at[place, i],
                gu_sem.at[at, i], sibling,
            )
        for i in range(row_lines):
            plan.send(
                my_wd.at[place, i, 1 - core], got_wd.at[at, i], wd_out.at[place, i],
                wd_sem.at[at, i], sibling,
            )

    def given(at):
        plan.draining = True
        give(at)
        plan.draining = False

    @pl.when(step == 0)
    def _():
        plan.greet_plane()

        def rows_of(b, carry):
            rows = pl.ds(pl.multiple_of(b * BLOCK, BLOCK), BLOCK)
            mid = x[rows, :].astype(F32) + nn(o[rows, :], wo[...])
            x2[rows, :] = mid
            rstd = lax.rsqrt(jnp.mean(mid * mid, axis=1, keepdims=True) + EPSILON)
            hv = (mid * rstd * gain[...]).astype(BF16)
            h2[rows, :] = hv
            h2t[:, rows] = hv.T
            total[rows, :] = mid
            dx2[rows, :] = jnp.zeros((BLOCK, depth), F32)
            return carry

        lax.fori_loop(0, blocks, rows_of, 0)

    @pl.when(jnp.logical_and(step >= 2, step < last))
    def _():
        given(step - 2)

    @pl.when(step < last)
    def _():
        def rows_of(b, carry):
            rows = pl.ds(pl.multiple_of(b * BLOCK, BLOCK), BLOCK)
            both_ = nn(h2[rows, :], gu[0])
            gate = both_[:, :chunk]
            up = both_[:, chunk:]
            da = nt(dy[rows, :], wd[...]).astype(BF16).astype(F32)
            sig = 1.0 / (1.0 + jnp.exp(-gate))
            silu = gate * sig
            av = (silu * up).astype(BF16)
            act[rows, :] = av
            dgate = (da * up * (sig * (1.0 + gate * (1.0 - sig)))).astype(BF16)
            dup = (da * silu).astype(BF16)
            dv = jnp.concatenate([dgate, dup], axis=1)
            dgu[rows, :] = dv
            total[rows, :] = total[rows, :] + nn(av, wd[...])
            dx2[rows, :] = dx2[rows, :] + nt(dv, gu[0])
            return carry

        lax.fori_loop(0, blocks, rows_of, 0)

        for part in range(depth // 512):
            at = slice(part * 512, (part + 1) * 512)
            val = tn(act[...], dy[:, at])
            for r in range(row_lines * 2):
                my_wd[slot, r // 2, r % 2, :, at] = val[
                    r * row_count : (r + 1) * row_count
                ].astype(BF16)

        rows_each = BLOCK // shard

        def weight(b, carry):
            rows = pl.ds(pl.multiple_of(b * BLOCK, BLOCK), BLOCK)
            val = nn(h2t[rows, :], dgu[...]).astype(BF16)
            for r in range(rows_each):
                my_gu[slot, b * (rows_each // 2) + r // 2, r % 2] = val[
                    r * shard : (r + 1) * shard
                ]
            return carry

        lax.fori_loop(0, depth // BLOCK, weight, 0)
        give(step)

    def over_plane(at):
        j = chunk_order(at, ctx)
        low, first, second = reduce_places(plan, j)
        for hop in range(1, side):
            to = lax.rem(first + hop, side)
            dev = (reduce_line(plan, low, to, second) * 2 + core, plan.c)
            for inner in range(side):
                plan.send(
                    got_gu.at[at, reduce_line(plan, low, to, inner)],
                    near_gu.at[at, hop - 1, inner], near_out.at[at, hop - 1, inner],
                    near_sem.at[at, hop - 1, inner], dev,
                )

    def collect(at):
        place = lax.rem(at, 2)
        for i in range(lines):
            plan.arrive(got_gu.at[at, i], gu_sem.at[at, i])

            @pl.when(at >= half)
            def _(i=i):
                add_rows(s_gu.at[0, i], [my_gu.at[place, i, core], got_gu.at[at, i]])

            @pl.when(at < half)
            def _(i=i):
                add_rows(got_gu.at[at, i], [my_gu.at[place, i, core], got_gu.at[at, i]])

        for early_at in range(half):

            @pl.when(at == early_at)
            def _(early_at=early_at):
                over_plane(early_at)

        for i in range(row_lines):
            plan.arrive(got_wd.at[at, i], wd_sem.at[at, i])
            add_rows(s_wd.at[i], [my_wd.at[place, i, core], got_wd.at[at, i]])

    @pl.when(jnp.logical_and(step >= 1, step < last))
    def _():
        collect(step - 1)

    @pl.when(step == last)
    def _():
        dg[...] = jnp.zeros_like(dg)

        def rows_of(b, carry):
            rows = pl.ds(pl.multiple_of(b * BLOCK, BLOCK), BLOCK)
            out[rows, :] = total[rows, :].astype(BF16)
            mid = x2[rows, :]
            rstd = lax.rsqrt(jnp.mean(mid * mid, axis=1, keepdims=True) + EPSILON)
            xhat = mid * rstd
            dh = dx2[rows, :]
            u = dh * gain[...]
            dm = dy[rows, :].astype(F32) + rstd * (
                u - xhat * jnp.mean(u * xhat, axis=1, keepdims=True)
            )
            dx2[rows, :] = dm
            dg[0:1, :] = dg[0:1, :] + jnp.sum(dh * xhat, axis=0, keepdims=True)
            h2[rows, :] = dm.astype(BF16)
            return carry

        lax.fori_loop(0, blocks, rows_of, 0)
        rows_each = BLOCK // shard

        def weight_out(b, carry):
            at = pl.ds(pl.multiple_of(b * BLOCK, BLOCK), BLOCK)
            val = tn(o[:, at], h2[...]).astype(BF16)
            for r in range(rows_each):
                my_wo[b * (rows_each // 2) + r // 2, r % 2] = val[r * shard : (r + 1) * shard]
            return carry

        lax.fori_loop(0, depth // BLOCK, weight_out, 0)
        for i in range(lines):
            plan.send(my_wo.at[i, 1 - core], got_wo.at[i], wo_out.at[i], wo_sem.at[i], sibling)

        def rows_out(b, carry):
            rows = pl.ds(pl.multiple_of(b * BLOCK, BLOCK), BLOCK)
            do[rows, :] = nt(h2[rows, :], wo[...]).astype(BF16)
            return carry

        lax.fori_loop(0, blocks, rows_out, 0)
        collect(last - 1)
        for i in range(lines):
            plan.arrive(got_wo.at[i], wo_sem.at[i])
            add_rows(s_wo.at[i], [my_wo.at[i, core], got_wo.at[i]])
        for at in (last - 2, last - 1):
            given(at)
        for at in range(half):
            low, first, _ = reduce_places(plan, chunk_order(at, ctx))
            for inner in range(side):
                for hop in range(1, side):
                    plan.arrive(near_gu.at[at, hop - 1, inner], near_sem.at[at, hop - 1, inner])
                add_rows(
                    early.at[at, inner],
                    [got_gu.at[at, reduce_line(plan, low, first, inner)]]
                    + [near_gu.at[at, hop - 1, inner] for hop in range(1, side)],
                )
        plan.draining = True
        for at in range(half):
            over_plane(at)
        for i in range(lines):
            plan.send(my_wo.at[i, 1 - core], got_wo.at[i], wo_out.at[i], wo_sem.at[i], sibling)
        plan.draining = False


def feed_forward(mesh, o, x, dy, wo, gain, gu, wd):
    fsdp, ctx = mesh.shape["fsdp"], mesh.shape["ctx"]
    tokens, depth = x.shape
    steps, _, width = gu.shape
    chunk = width // 2
    lines = fsdp // 2
    shard = depth // fsdp
    row_count = wd.shape[0] // fsdp
    row_lines = fsdp // ctx // 2
    half = ctx // 2
    side = math.isqrt(lines)
    hops = max(side - 1, 1)
    once = pl.Buffered(1)

    def chunk_of(i):
        return chunk_order(jnp.minimum(i, steps - 1), ctx)

    def chunk_before(i):
        return chunk_order(jnp.maximum(i - 1, 0), ctx)

    def whole(shape):
        return pl.BlockSpec(shape, lambda i: (0,) * len(shape), pipeline_mode=once)

    def whole_out(shape):
        return pl.BlockSpec(shape, lambda i: (0,) * len(shape), pipeline_mode=once)

    shapes = (
        jax.ShapeDtypeStruct((tokens, depth), BF16),
        jax.ShapeDtypeStruct((tokens, depth), F32),
        jax.ShapeDtypeStruct((tokens, depth), BF16),
        jax.ShapeDtypeStruct((8, depth), F32),
        jax.ShapeDtypeStruct((lines, shard, depth), BF16),
        jax.ShapeDtypeStruct((ctx - half, lines, shard, width), BF16),
        jax.ShapeDtypeStruct((lines, row_count, depth), BF16),
        jax.ShapeDtypeStruct((half, side, shard, width), BF16),
    )
    dma = pltpu.SemaphoreType.DMA
    return pl.pallas_call(
        functools.partial(feed_kernel, fsdp, ctx),
        grid=(steps + 1,),
        out_shape=shapes,
        in_specs=[
            whole((tokens, depth)),
            whole((tokens, depth)),
            whole((tokens, depth)),
            whole((depth, depth)),
            whole((1, depth)),
            pl.BlockSpec((1, depth, width), lambda i: (chunk_of(i), 0, 0)),
            pl.BlockSpec((chunk, depth), lambda i: (chunk_of(i), 0)),
        ],
        out_specs=[
            whole_out((tokens, depth)),
            whole_out((tokens, depth)),
            whole_out((tokens, depth)),
            whole_out((8, depth)),
            whole_out((lines, shard, depth)),
            pl.BlockSpec(
                (1, lines, shard, width), lambda i: (jnp.maximum(i - 1 - half, 0), 0, 0, 0)
            ),
            pl.BlockSpec((row_lines, row_count, depth), lambda i: (chunk_before(i), 0, 0)),
            whole_out((half, side, shard, width)),
        ],
        scratch_shapes=[
            pltpu.VMEM((tokens, depth), F32),
            pltpu.VMEM((tokens, depth), BF16),
            pltpu.VMEM((depth, tokens), BF16),
            pltpu.VMEM((tokens, depth), F32),
            pltpu.VMEM((tokens, chunk), BF16),
            pltpu.VMEM((tokens, width), BF16),
            pltpu.VMEM((2, lines, 2, shard, width), BF16),
            pltpu.VMEM((2, row_lines, 2, row_count, depth), BF16),
            pltpu.VMEM((lines, 2, shard, depth), BF16),
            pltpu.VMEM((steps, lines, shard, width), BF16),
            pltpu.VMEM((steps, row_lines, row_count, depth), BF16),
            pltpu.VMEM((lines, shard, depth), BF16),
            pltpu.VMEM((half, hops, side, shard, width), BF16),
            dma((steps, lines)), dma((2, lines)), dma((steps, row_lines)), dma((2, row_lines)),
            dma((lines,)), dma((lines,)), dma((half, hops, side)), dma((half, hops, side)),
        ],
        compiler_params=pltpu.CompilerParams(
            vmem_limit_bytes=VMEM_LIMIT, dimension_semantics=("arbitrary",), collective_id=4,
            has_side_effects=True,
        ),
        name="feed_forward",
    )(o, x, dy, wo, gain, gu, wd)


def chunk_rows(count):
    return 32 if count % 32 == 0 else count


def add_rows(dst, parts):
    count = dst.shape[0]
    rows = chunk_rows(count)

    def body(t, carry):
        at = pl.ds(pl.multiple_of(t * rows, rows), rows)
        total = parts[0][at, :].astype(F32)
        for part in parts[1:]:
            total = total + part[at, :].astype(F32)
        dst[at, :] = total.astype(dst.dtype)
        return carry

    lax.fori_loop(0, count // rows, body, 0)


class Reduction:
    def __init__(self, plan, sources, early, own, near, next_, last, outs, sems):
        self.plan = plan
        self.sources, self.early, self.own, self.near, self.next, self.last, self.outs = (
            sources, early, own, near, next_, last, outs,
        )
        (
            self.own_sem, self.near_sem, self.near_out, self.next_sem, self.next_out,
            self.last_sem, self.last_out,
        ) = sems
        self.side = plan.across
        half, ctx = plan.half, plan.ctx
        self.chunks = [chunk_order(i, ctx) for i in range(ctx)]
        self.first_set = [(1, j) for j in self.chunks[:half]]
        self.second_set = [(1, j) for j in self.chunks[half:]]
        self.third_set = [(i, j) for i in (0, 2) for j in self.chunks]

    def piece(self, i, line, j):
        src = self.sources[i]
        if i == 1:
            return src.at[self.chunks.index(j) - self.plan.half, line]
        width = src.shape[2] // self.plan.ctx
        return src.at[line, :, pl.ds(j * width, width)]

    def send_next(self, i, j, source):
        plan = self.plan
        low, first, second = reduce_places(plan, j)
        for hop in range(1, self.side):
            to = lax.rem(second + hop, self.side)
            plan.send(
                source(to),
                self.next[i].at[j, hop - 1],
                self.next_out.at[i, j, hop - 1],
                self.next_sem.at[i, j, hop - 1],
                (reduce_line(plan, low, first, to) * 2 + plan.core, plan.c),
            )

    def start_early(self):
        plan = self.plan
        for at, (i, j) in enumerate(self.first_set):
            self.send_next(i, j, lambda to, at=at: self.early.at[at, to])
            for inner in range(self.side):
                plan.keep(
                    self.early.at[at, inner], self.own[i].at[j, inner], self.own_sem.at[i, j, inner]
                )

    def start(self, pairs):
        plan = self.plan
        for i, j in pairs:
            low, first, second = reduce_places(plan, j)
            for hop in range(1, self.side):
                to = lax.rem(first + hop, self.side)
                dev = (reduce_line(plan, low, to, second) * 2 + plan.core, plan.c)
                for inner in range(self.side):
                    plan.send(
                        self.piece(i, reduce_line(plan, low, to, inner), j),
                        self.near[i].at[j, hop - 1, inner],
                        self.near_out.at[i, j, hop - 1, inner],
                        self.near_sem.at[i, j, hop - 1, inner],
                        dev,
                    )
            for inner in range(self.side):
                plan.keep(
                    self.piece(i, reduce_line(plan, low, first, inner), j),
                    self.own[i].at[j, inner],
                    self.own_sem.at[i, j, inner],
                )

    def step_near(self, pairs):
        plan = self.plan
        for i, j in pairs:
            for inner in range(self.side):
                plan.arrive(self.own[i].at[j, inner], self.own_sem.at[i, j, inner])
                for hop in range(1, self.side):
                    plan.arrive(
                        self.near[i].at[j, hop - 1, inner], self.near_sem.at[i, j, hop - 1, inner]
                    )
                if not plan.draining:
                    add_rows(
                        self.own[i].at[j, inner],
                        [self.own[i].at[j, inner]]
                        + [self.near[i].at[j, hop - 1, inner] for hop in range(1, self.side)],
                    )
            self.send_next(i, j, lambda to, i=i, j=j: self.own[i].at[j, to])

    def step_next(self, pairs):
        plan = self.plan
        for i, j in pairs:
            _, _, second = reduce_places(plan, j)
            if (i, j) in self.first_set:
                for inner in range(self.side):
                    plan.arrive(self.own[i].at[j, inner], self.own_sem.at[i, j, inner])
            for hop in range(1, self.side):
                plan.arrive(self.next[i].at[j, hop - 1], self.next_sem.at[i, j, hop - 1])
            if not plan.draining:
                add_rows(
                    self.own[i].at[j, second],
                    [self.own[i].at[j, second]]
                    + [self.next[i].at[j, hop - 1] for hop in range(1, self.side)],
                )
            self.send_last(i, j, second, both(plan.c == 0, j > 0), both(plan.c == plan.ctx - 1, j < plan.ctx - 1))

    def send_last(self, i, j, second, up, down):
        plan = self.plan
        if up is not None:
            plan.send(
                self.own[i].at[j, second], self.last[i].at[j], self.last_out.at[i, j],
                self.last_sem.at[i, j], (plan.f, plan.c + 1), up,
            )
        if down is not None:
            slot = jnp.where(plan.c - 1 == j, plan.ctx, j)
            plan.send(
                self.own[i].at[j, second], self.last[i].at[slot], self.last_out.at[i, j],
                self.last_sem.at[i, slot], (plan.f, plan.c - 1), down,
            )

    def step_pass(self, pairs, hop):
        plan = self.plan
        for i, j in pairs:
            _, _, second = reduce_places(plan, j)
            up = both(plan.c == hop, plan.c < j) if hop < j else None
            down = both(plan.c == plan.ctx - 1 - hop, plan.c > j) if plan.ctx - 1 - hop > j else None
            for cond in (up, down):
                if cond is not None and not plan.draining:

                    @pl.when(cond)
                    def _(i=i, j=j, second=second):
                        plan.arrive(self.last[i].at[j], self.last_sem.at[i, j])
                        add_rows(
                            self.own[i].at[j, second],
                            [self.own[i].at[j, second], self.last[i].at[j]],
                        )

            self.send_last(i, j, second, up, down)

    def finish(self):
        plan = self.plan
        for i in range(3):
            count = self.outs[i].shape[0]
            rows = chunk_rows(count)
            slots = ((plan.c > 0, plan.c), (plan.c < plan.ctx - 1, plan.ctx))
            for there, slot in slots:
                plan.arrive(self.last[i].at[slot], self.last_sem.at[i, slot], there)

            def body(t, carry, i=i, rows=rows):
                at = pl.ds(pl.multiple_of(t * rows, rows), rows)
                for j in range(plan.ctx):
                    _, _, second = reduce_places(plan, j)

                    @pl.when(plan.c == j)
                    def _(j=j, second=second):
                        total = self.own[i][j, second, at, :].astype(F32)
                        if j > 0:
                            total = total + self.last[i][j, at, :].astype(F32)
                        if j < plan.ctx - 1:
                            total = total + self.last[i][plan.ctx, at, :].astype(F32)
                        self.outs[i][at, :] = total

                return carry

            lax.fori_loop(0, count // rows, body, 0)


def backward_kernel(
    fsdp, ctx,
    d_out, x_in, q_in, k_in, vm_in, kt_in, att_in, lse, wqkv_in, gain, table_in, start,
    dg_two, s_wo, s_gu, s_wd, early,
    folded, vout, g_wo, g_gu, g_wd, g_qkv, dg_all,
    part, q, k, vm, kt, att, do, wqkv, table,
    dqt, dkk, dvv, rows_t, d3, gw_full, gw,
    other, chain, gw_near, gw_sum, gw_last, dg, dg_near, dg_sum, dg_last,
    o_wo, o_gu, o_wd, n_wo, n_gu, n_wd, x_wo, x_gu, x_wd, l_wo, l_gu, l_wd,
    load_sem, do_sem, do_out, v_sem, v_out,
    sib_sem, sib_out, chain_sem, chain_out, end_sem, end_out,
    gw_sem, gw_out, gl_sem, gl_out, dn_sem, dn_out, dl_sem, dl_out,
    own_sem, near_sem, near_out, next_sem, next_out, last_sem, last_out,
):
    plan = Plan(fsdp, ctx)
    f, c, core, line, home, half = plan.f, plan.c, plan.core, plan.line, plan.home, plan.half
    lines = plan.lines
    sibling = (line * 2 + 1 - core, c)
    low, high = home * half, home * half + half - 1
    blocks, _, depth = part.shape
    group = blocks * BLOCK
    cols = vm.shape[1]
    heads = cols // HEAD
    tokens = group // ctx
    per = tokens // BLOCK
    pairs = blocks // 2
    plan.barrier()

    for i in range(half):
        for kk in range(2):
            to = core * half + i
            rank = lax.rem(to + kk * half, ctx)
            src = d_out.at[:, pl.ds(pl.multiple_of(rank * cols, cols), cols)]
            mine = both(core == home, c == to, core == kk)
            plan.send(
                src, do.at[c], do_out.at[i * 2 + kk], do_sem.at[c], (line * 2 + kk, to),
                jnp.logical_not(mine),
            )
            plan.keep(src, do.at[c], do_sem.at[c], mine)
    loads = (
        (q_in, q), (k_in, k), (vm_in, vm), (kt_in, kt), (att_in, att), (table_in, table),
        (wqkv_in, wqkv), (x_in, part),
    )
    for i, (src, dst) in enumerate(loads):
        plan.keep(src, dst, load_sem.at[i])
    reduction = Reduction(
        plan, (s_wo, s_gu, s_wd), early, (o_wo, o_gu, o_wd), (n_wo, n_gu, n_wd), (x_wo, x_gu, x_wd),
        (l_wo, l_gu, l_wd), (g_wo, g_gu, g_wd),
        (own_sem, near_sem, near_out, next_sem, next_out, last_sem, last_out),
    )
    reduction.start_early()
    reduction.start(reduction.second_set)
    reduction.start(reduction.third_set)

    dqt[...] = jnp.zeros_like(dqt)
    dkk[...] = jnp.zeros_like(dkk)
    dvv[...] = jnp.zeros_like(dvv)
    gw_full[...] = jnp.zeros_like(gw_full)
    dg[...] = jnp.zeros_like(dg)
    dg[1:2, :] = dg_two[0:1, :]
    for i, (src, dst) in enumerate(loads):
        plan.arrive(dst, load_sem.at[i])
    for j in range(ctx):
        plan.arrive(do.at[j], do_sem.at[j])

    def grads_of(b):
        return do[b // per, pl.ds(pl.multiple_of(lax.rem(b, per) * BLOCK, BLOCK), BLOCK), :]

    def dots(b, carry):
        rows = pl.ds(pl.multiple_of(b * BLOCK, BLOCK), BLOCK)
        prod = grads_of(b).astype(F32) * att[rows, :]
        upper = prod.astype(BF16)
        lower = (prod - upper.astype(F32)).astype(BF16)
        head_row = lax.broadcasted_iota(jnp.int32, (8, cols), 0)
        lane = lax.broadcasted_iota(jnp.int32, (8, cols), 1)
        choose = (lane // HEAD == head_row).astype(F32).astype(BF16)
        rows_t[:, rows] = nt(choose, upper) + nt(choose, lower)
        return carry

    lax.fori_loop(0, blocks, dots, 0)

    def tile(kb, qb):
        krows = pl.ds(pl.multiple_of(kb * BLOCK, BLOCK), BLOCK)
        rows = pl.ds(pl.multiple_of(qb * BLOCK, BLOCK), BLOCK)
        kv = k[krows, :]
        vv = vm[krows, :]
        qv = q[rows, :]
        dov = grads_of(qb)
        key_pos = kb * BLOCK + lax.broadcasted_iota(jnp.int32, (BLOCK, BLOCK), 0)
        query_pos = qb * BLOCK + lax.broadcasted_iota(jnp.int32, (BLOCK, BLOCK), 1)
        allowed = (key_pos <= query_pos) & (key_pos >= start[0:1, rows])
        dk_sum = dkk[krows, :]
        dv_sum = dvv[krows, :]
        for head in range(heads):
            band = slice(head * HEAD, (head + 1) * HEAD)
            lanes = head_lanes(qv.shape, head)
            qm = jnp.where(lanes, qv, jnp.zeros_like(qv))
            dom = jnp.where(lanes, dov, jnp.zeros_like(dov))
            s = jnp.where(allowed, nt(kv, qm), NEGATIVE)
            p = jnp.exp(s - lse[head : head + 1, rows])
            ds = (p * (nt(vv, dom) - rows_t[head : head + 1, rows])).astype(BF16)
            dv_sum = dv_sum + nn(p.astype(BF16), dom)
            dk_sum = dk_sum + nn(ds, qm)
            dqt[band, rows] = dqt[band, rows] + nn(kt[band, krows], ds)
        dkk[krows, :] = dk_sum
        dvv[krows, :] = dv_sum

    def unit_of(t):
        return jnp.where(home == 0, blocks - 1 - t, t)

    def finish(o):
        rows = pl.ds(pl.multiple_of(o * BLOCK, BLOCK), BLOCK)
        cos_v, sin_v = turns(table[rows, :], cols)
        dq = dqt[:, rows].T * (1.0 / math.sqrt(HEAD))
        d3[rows, :cols] = (dq * cos_v - half_swap(dq) * sin_v).astype(BF16)
        dk = dkk[rows, :]
        d3[rows, cols : 2 * cols] = (dk * cos_v - half_swap(dk) * sin_v).astype(BF16)
        d3[rows, 2 * cols :] = (0.5 * dvv[rows, :]).astype(BF16)
        dh = nt(d3[rows, :], wqkv[...])
        xv = part[o].astype(F32)
        rstd = lax.rsqrt(jnp.mean(xv * xv, axis=1, keepdims=True) + EPSILON)
        xhat = xv * rstd
        h1 = (xhat * gain[...]).astype(BF16)
        u = dh * gain[...]
        part[o] = (rstd * (u - xhat * jnp.mean(u * xhat, axis=1, keepdims=True))).astype(BF16)
        dg[0:1, :] = dg[0:1, :] + jnp.sum(dh * xhat, axis=0, keepdims=True)
        gw_full[...] = gw_full[...] + tn(h1, d3[rows, :])

    def give(t):
        o = unit_of(t)
        slot = t // 2
        plan.send(
            part.at[o], other.at[slot], sib_out.at[slot], sib_sem.at[slot], sibling,
            lax.rem(o, 2) != core,
        )

    def pair_unit(i):
        return jnp.where(home == 0, blocks - 2 - 2 * i, 2 * i) + core

    def add_unit(o, src):
        def body(t, carry):
            at = pl.ds(pl.multiple_of(t * 32, 32), 32)
            part[o, at, :] = (part[o, at, :].astype(F32) + src[at, :].astype(F32)).astype(BF16)
            return carry

        lax.fori_loop(0, BLOCK // 32, body, 0)

    def sum_pair(i):
        plan.arrive(other.at[i], sib_sem.at[i])
        if not plan.draining:
            add_unit(pair_unit(i), other.at[i])

    def pass_pair(i, hears):
        o = pair_unit(i)
        j = o // per
        top = jnp.minimum(j, high)
        bottom = jnp.maximum(j, low)
        from_below = both(c > low, c <= top)
        from_above = both(c < high, c >= bottom)
        now = jnp.logical_or(from_below, from_above) == hears
        spot = jnp.where(j == c, pairs, i)
        if hears and not plan.draining:

            @pl.when(from_below)
            def _():
                plan.arrive(chain.at[i], chain_sem.at[i])
                add_unit(o, chain.at[i])

            @pl.when(from_above)
            def _():
                plan.arrive(chain.at[spot], chain_sem.at[spot])
                add_unit(o, chain.at[spot])

        plan.send(
            part.at[o], chain.at[i], chain_out.at[0, i], chain_sem.at[i], (f, c + 1),
            both(now, c < top),
        )
        below = jnp.where(j == c - 1, pairs, i)
        plan.send(
            part.at[o], chain.at[below], chain_out.at[1, i], chain_sem.at[below], (f, c - 1),
            both(now, c > bottom),
        )
        end = jnp.clip(j, low, high)
        mine = both(c == end, j == c, core == home)
        where = lax.rem(o, per)
        dst = folded.at[pl.ds(pl.multiple_of(where * BLOCK, BLOCK), BLOCK), :]
        plan.send(
            part.at[o], dst, end_out.at[i], end_sem.at[where], (line * 2 + home, j),
            both(now, c == end, jnp.logical_not(mine)),
        )
        plan.keep(part.at[o], dst, end_sem.at[where], both(now, mine))

    rank = lax.rem(c + core * half, ctx)

    def give_values(i):
        j = jnp.where(home == 0, ctx - 1 - i, i)
        src = d3.at[pl.ds(pl.multiple_of(j * tokens, tokens), tokens), 2 * cols : 3 * cols]
        dst = vout.at[:, pl.ds(pl.multiple_of(rank * cols, cols), cols)]
        mine = both(core == home, c == j)
        plan.send(
            src, dst, v_out.at[i], v_sem.at[rank], (line * 2 + home, j), jnp.logical_not(mine)
        )
        plan.keep(src, dst, v_sem.at[rank], mine)

    schedule = {}
    schedule_last = []

    def at_step(t, act):
        schedule.setdefault(t, []).append(act)

    scale = blocks // 8
    for kind, which, place in REDUCE_STEPS:
        pairs_of = getattr(reduction, which)
        if kind != "step_pass":
            at_step(place * scale, functools.partial(getattr(reduction, kind), pairs_of))
            continue
        for hop in range(1, ctx - 1):
            act = functools.partial(reduction.step_pass, pairs_of, hop)
            when = place + PASS_GAP * (hop - 1)
            if when < 8 and hop < 3:
                at_step(when * scale, act)
            else:
                schedule_last.append(act)
    for i in range(pairs - 1):
        at_step(2 * i + 1, lambda i=i: give_values(i))
        at_step(2 * i + 2, lambda i=i: sum_pair(i))
        at_step(2 * i + 2, lambda i=i: pass_pair(i, False))
        if i < pairs - 2:
            at_step(2 * i + 4, lambda i=i: pass_pair(i, True))
    at_step(blocks - 1, lambda: give_values(pairs - 1))

    def step(t, carry):
        o = unit_of(t)

        def inner(i, carry2):
            tile(jnp.where(home == 0, i, o), jnp.where(home == 0, o, o + i))
            return carry2

        lax.fori_loop(0, blocks - t, inner, 0)
        finish(o)
        give(t)
        for s in sorted(schedule):

            @pl.when(t == s)
            def _(s=s):
                for act in schedule[s]:
                    act()

        return carry

    kept = plan.started
    plan.started = []
    lax.fori_loop(0, blocks, step, 0)
    plan.started = kept

    for hop in range(1, fsdp):
        dev = (lax.rem(f + hop, fsdp), c)
        plan.send(dg, dg_near.at[f], dn_out.at[hop - 1], dn_sem.at[f], dev)
    plan.keep(dg, dg_near.at[f], dn_sem.at[f])

    pass_pair(pairs - 2, True)
    sum_pair(pairs - 1)
    pass_pair(pairs - 1, False)
    shard = depth // fsdp
    rows_each = BLOCK // shard

    def weight(b, carry):
        at = pl.ds(pl.multiple_of(b * BLOCK, BLOCK), BLOCK)
        val = gw_full[at, :].astype(BF16)
        for r in range(rows_each):
            gw[b * (rows_each // 2) + r // 2, r % 2] = val[r * shard : (r + 1) * shard]
        return carry

    lax.fori_loop(0, depth // BLOCK, weight, 0)
    for i in range(3):
        for hop in range(1, lines):
            to = lax.rem(line + hop, lines)
            plan.send(
                gw.at[to, :, :, pl.ds(i * cols, cols)],
                gw_near.at[hop - 1, :, :, pl.ds(i * cols, cols)],
                gw_out.at[i, hop - 1], gw_sem.at[i, hop - 1], (to * 2 + core, c),
            )
    pass_pair(pairs - 1, True)

    for at in range(fsdp):
        plan.arrive(dg_near.at[at], dn_sem.at[at])
    total = dg_near[0]
    for at in range(1, fsdp):
        total = total + dg_near[at]
    dg_sum[...] = total
    for hop in range(1, ctx):
        plan.send(
            dg_sum, dg_last.at[c], dl_out.at[hop - 1], dl_sem.at[c], (f, lax.rem(c + hop, ctx))
        )
    plan.keep(dg_sum, dg_last.at[c], dl_sem.at[c])

    plane = jnp.where(core == 0, c, lax.rem(c + half, ctx))
    for i in range(3):
        band = pl.ds(i * cols, cols)
        for hop in range(1, lines):
            plan.arrive(gw_near.at[hop - 1, :, :, band], gw_sem.at[i, hop - 1])
        for kk in range(2):
            add_rows(
                gw_sum.at[kk, :, band],
                [gw.at[line, kk, :, band]]
                + [gw_near.at[hop - 1, kk, :, band] for hop in range(1, lines)],
            )
            mine = both(core == 0, kk == 0)
            src, dst = gw_sum.at[kk, :, band], gw_last.at[core, :, band]
            plan.send(
                src, dst, gl_out.at[kk, i], gl_sem.at[core, i], (line * 2 + kk, plane),
                jnp.logical_not(mine),
            )
            plan.keep(src, dst, gl_sem.at[core, i], mine)

    for act in schedule_last:
        act()
    reduction.finish()
    for at in range(ctx):
        plan.arrive(dg_last.at[at], dl_sem.at[at])
    total = dg_last[0]
    for at in range(1, ctx):
        total = total + dg_last[at]
    dg_all[...] = total
    for kk in range(2):
        for i in range(3):
            plan.arrive(gw_last.at[kk, :, pl.ds(i * cols, cols)], gl_sem.at[kk, i])
    add_rows(g_qkv, [gw_last.at[0], gw_last.at[1]])
    for at in range(per):
        plan.arrive(folded.at[pl.ds(at * BLOCK, BLOCK), :], end_sem.at[at])
    for at in range(ctx):
        plan.arrive(vout.at[:, pl.ds(at * cols, cols)], v_sem.at[at])
    plan.drain()
    plan.draining = True
    for t in range(blocks):
        give(t)
    for s in sorted(schedule):
        for act in schedule[s]:
            act()


PASS_GAP = 1
REDUCE_STEPS = (
    ("step_near", "second_set", 0),
    ("step_next", "first_set", 0),
    ("step_near", "third_set", 1),
    ("step_next", "second_set", 2),
    ("step_pass", "first_set", 2),
    ("step_next", "third_set", 3),
    ("step_pass", "second_set", 4),
    ("step_pass", "third_set", 6),
)


def backward(mesh, d_out, x, q, k, vm, kt, att, lse, wqkv, gain, table, start, dg_two, sums):
    fsdp, ctx = mesh.shape["fsdp"], mesh.shape["ctx"]
    group, depth = x.shape
    cols = vm.shape[1]
    tokens = group // ctx
    blocks = group // BLOCK
    x = x.reshape(blocks, BLOCK, depth)
    pairs = blocks // 2
    half = ctx // 2
    lines = fsdp // 2
    side = math.isqrt(lines)
    shard = depth // fsdp
    s_wo, s_gu, s_wd, _ = sums
    shapes = (
        (s_wo.shape[1], s_wo.shape[2] // ctx),
        (s_gu.shape[2], s_gu.shape[3]),
        (s_wd.shape[1], s_wd.shape[2] // ctx),
    )
    anywhere = pl.BlockSpec(memory_space=pl.ANY)
    vmem = pl.BlockSpec(memory_space=pltpu.VMEM)
    dma = pltpu.SemaphoreType.DMA
    hops = max(side - 1, 1)

    def low(*shape):
        return pltpu.VMEM(shape, BF16)

    def full(*shape):
        return pltpu.VMEM(shape, F32)

    return pl.pallas_call(
        functools.partial(backward_kernel, fsdp, ctx),
        out_shape=(
            jax.ShapeDtypeStruct((tokens, depth), BF16),
            jax.ShapeDtypeStruct((tokens, depth), BF16),
            jax.ShapeDtypeStruct(shapes[0], F32),
            jax.ShapeDtypeStruct(shapes[1], F32),
            jax.ShapeDtypeStruct(shapes[2], F32),
            jax.ShapeDtypeStruct((shard, 3 * cols), F32),
            jax.ShapeDtypeStruct((8, depth), F32),
        ),
        in_specs=[anywhere] * 7 + [vmem, anywhere, vmem] + [anywhere] + [vmem] * 2 + [anywhere] * 4,
        out_specs=[anywhere] * 2 + [vmem] * 5,
        scratch_shapes=[
            low(blocks, BLOCK, depth), low(group, cols), low(group, cols), low(group, cols),
            low(cols, group), full(group, cols), low(ctx, tokens, cols), low(depth, 3 * cols),
            full(group, table.shape[1]),
            full(cols, group), full(group, cols), full(group, cols),
            full(8, group), low(group, 3 * cols), full(depth, 3 * cols), low(lines, 2, shard, 3 * cols),
            low(pairs, BLOCK, depth), low(pairs + 1, BLOCK, depth),
            low(max(lines - 1, 1), 2, shard, 3 * cols), low(2, shard, 3 * cols),
            low(2, shard, 3 * cols),
            full(8, depth), full(fsdp, 8, depth), full(8, depth), full(ctx, 8, depth),
        ]
        + [low(ctx, side, *shape) for shape in shapes]
        + [low(ctx, hops, side, *shape) for shape in shapes]
        + [low(ctx, hops, *shape) for shape in shapes]
        + [low(ctx + 1, *shape) for shape in shapes]
        + [
            dma((8,)), dma((ctx,)), dma((ctx,)), dma((ctx,)), dma((ctx,)),
            dma((pairs,)), dma((pairs,)), dma((pairs + 1,)), dma((2, pairs)),
            dma((tokens // BLOCK,)), dma((pairs,)),
            dma((3, lines)), dma((3, lines)), dma((2, 3)), dma((2, 3)),
            dma((fsdp,)), dma((fsdp,)), dma((ctx,)), dma((ctx,)),
            dma((3, ctx, side)), dma((3, ctx, hops, side)), dma((3, ctx, hops, side)),
            dma((3, ctx, hops)), dma((3, ctx, hops)), dma((3, ctx + 1)), dma((3, ctx)),
        ],
        compiler_params=pltpu.CompilerParams(
            collective_id=3, has_side_effects=True, vmem_limit_bytes=BACKWARD_LIMIT
        ),
        name="backward",
    )(d_out, x, q, k, vm, kt, att, lse, wqkv, gain, table, start, dg_two, *sums)


def layer(
    mesh, tokens, value_first, lengths, w_query, w_key, w_value, w_out, w_gate, w_up, w_down,
    gain_attn, gain_ffn, out_grad, value_grad,
):
    fsdp, ctx = mesh.shape["fsdp"], mesh.shape["ctx"]
    count, depth = tokens.shape
    group = count * ctx
    cols = depth // ctx
    rows = depth // fsdp
    f, c = lax.axis_index("fsdp"), lax.axis_index("ctx")
    small = jnp.stack([gain_attn, gain_ffn]).astype(BF16).astype(F32)
    small = lax.dynamic_update_slice(
        jnp.zeros((8, depth), F32), small, (jnp.int32(0), (f * rows).astype(jnp.int32))
    )
    small = lax.dynamic_update_slice(small, lengths.astype(F32), (2, 0))
    (
        attended, wos, gus, wds, xs, q, k, vm, kt, att, wq, lse, table, first, gains
    ) = forward(
        mesh, tokens, value_first, (w_query, w_key, w_value, w_out, w_gate, w_up, w_down), small
    )
    gain_one, gain_two = gains[0:1], gains[1:2]
    wq = wq.reshape(depth, 3 * cols)
    result, dx2, d_out, dg_two, *sums = feed_forward(
        mesh, attended, tokens, out_grad, wos.reshape(depth, depth), gain_two,
        gus.reshape(ctx, depth, -1), wds.reshape(-1, depth),
    )
    folded, dvr, g_wo, g_gu, g_wd, g_qkv, gain_grads = backward(
        mesh, d_out, xs.reshape(group, depth), q, k, vm, kt, att, lse, wq, gain_one, table, first, dg_two,
        sums,
    )
    gain_grads = lax.dynamic_slice(
        gain_grads, (jnp.int32(0), (f * rows).astype(jnp.int32)), (2, rows)
    )
    ff = w_gate.shape[1]
    return (
        result,
        dx2 + folded.astype(F32),
        value_grad + dvr.astype(F32),
        g_qkv[:, :cols],
        g_qkv[:, cols : 2 * cols],
        g_qkv[:, 2 * cols :],
        g_wo,
        g_gu[:, :ff],
        g_gu[:, ff:],
        g_wd,
        gain_grads[0],
        gain_grads[1],
    )


def solution(mesh):
    rows = P(("fsdp", "ctx"), None)
    shard = P("fsdp", "ctx")
    return jax.shard_map(
        functools.partial(layer, mesh),
        mesh=mesh,
        in_specs=(rows, rows, P("fsdp", None)) + (shard,) * 7 + (P("fsdp"),) * 2 + (rows, rows),
        out_specs=(rows, rows, rows) + (shard,) * 7 + (P("fsdp"),) * 2,
        check_vma=False,
    )
```

time: 486 us -> 410 us (0.84)
  Pallas kernels: 452 us -> 387 us
  other arithmetic: 20.1 us -> 5.96 us
    pallas_call x3 -> x1, Pallas kernels: 218 us -> 166 us  [forward(): pl.pallas_call(functools.partial(forward_kernel, fsdp, ctx), out_shape=(a...]
    pallas_call x1, Pallas kernels: 181 us -> 158 us  [backward(): pl.pallas_call(functools.partial(backward_kernel, fsdp, ctx), out_shape=(...]
    pallas_call x1, Pallas kernels: 53.3 us -> 62.3 us  [feed_forward(): pl.pallas_call(functools.partial(feed_kernel, fsdp, ctx), grid=(steps + 1...]
  transfers between devices with their start and end apart: 1 -> 0, of which waited for: 0 -> 0; matrix products, arithmetic and copies ran while one was open for 2% -> 0% of each run, Pallas kernels for 29% -> 0%
where the time goes in v3:
time: 410 us; the launch traced here: 407 us
  Pallas kernels  387 us (94%)
  local copies, waits for them, and re-layouts  14.1 us (3%)
  other arithmetic  5.96 us (1%)
    pallas_call x1, Pallas kernels, forward(): pl.pallas_call(functools.partial(forward_kernel, fsdp, ctx), out_shape=(a...  166 us
    pallas_call x1, Pallas kernels, backward(): pl.pallas_call(functools.partial(backward_kernel, fsdp, ctx), out_shape=(...  158 us
    pallas_call x1, Pallas kernels, feed_forward(): pl.pallas_call(functools.partial(feed_kernel, fsdp, ctx), grid=(steps + 1...  62.3 us

profile of v3, /device:TPU:0, one launch (start us, length us, event | category | flops | bytes accessed | tf_op | source)
XLA Modules:
  0.0 407.4 jit_solution(10147871503405658572)
XLA Ops:
  0.6 0.7 convert_element_type.14
  1.3 0.7 convert_bitcast_fusion
  2.0 0.2 dynamic_update_slice.7.small
  2.2 0.0 copy-start.6
  2.3 1.9 copy.26.w_g
  4.2 1.9 copy.27.w_u
  6.1 0.0 copy-done.6
  6.1 166.4 %forward.1 = (bf16[512,1024]{1,0:T(8,128)(2,1)}, bf16[8,128,1024]{2,1,0:T(8,128)(2,1)}, bf16[4,8,128,1408]{3,2,1,0:T(8,128)(2,1)}, bf16[8,352,1024]{2,1,0:T(8,12...) custom-call(bf16[512,1024]{1,0:T(8,128)(2,1)} %x.3, ...), custom_call_target="tpu_custom_call" | custom-call | tf_op jit(solution)/shard_map/forward/pallas_call | solution.py:601
  172.5 1.4 fusion.2
  173.9 62.3 %feed_forward.1 = (bf16[512,1024]{1,0:T(8,128)(2,1)}, f32[512,1024]{1,0:T(8,128)}, bf16[512,1024]{1,0:T(8,128)(2,1)}, f32[8,1024]{1,0:T(8,128)}, bf16[4,128,1024...) custom-call(bf16[512,1024]{1,0:T(8,128)(2,1)} %get-tuple-element.42., ...), custom_call_target="tpu_custom_call" | custom-call | tf_op jit(solution)/shard_map/feed_forward/pallas_call | solution.py:902
  236.2 157.9 %backward.1 = (bf16[512,1024]{1,0:T(8,128)(2,1)}, bf16[512,1024]{1,0:T(8,128)(2,1)}, f32[128,256]{1,0:T(8,128)}, f32[128,1408]{1,0:T(8,128)}, f32[352,256]{1,0:T...) custom-call(bf16[512,1024]{1,0:T(8,128)(2,1)} %get-tuple-element.49.d_out, bf16[8,256,1024]{2,1,0:T(8,128)(2,1)} %bitcast.15, ...), custom_call_target="tpu_custom_call" | custom-call | tf_op jit(solution)/shard_map/backward/pallas_call | solution.py:1517
  394.1 0.0 copy-start.1
  394.1 0.8 constant_dynamic-slice_fusion
  395.0 0.5 slice_bitcast_fusion
  395.5 1.8 fusion.1
  397.3 1.3 fusion
  398.6 0.9 copy.29
  399.5 0.9 copy.28
  400.4 0.0 copy-done.1
  400.4 0.0 copy-start
  400.4 0.0 copy-start.2
  400.4 3.0 convert_add_fusion.1
  403.4 0.0 copy-done
  403.4 0.0 copy-done.2
  403.4 0.0 copy-start.3
  403.4 1.6 convert_add_fusion
  405.0 0.0 copy-done.3
  405.0 0.0 copy-start.5
  405.0 0.0 copy-start.4
  405.0 1.0 copy.35
  406.0 0.0 copy-done.5
  406.0 0.7 copy.36
  406.7 0.0 copy-done.4
  406.7 0.7 copy.37
  (2 shorter events, 0.0 us)
Async XLA Ops:
  2.2 3.8 copy-start.6
  394.1 6.2 %copy-start.1 = (f32[512,1024]{1,0:T(8,128)S(1)}, f32[512,1024]{1,0:T(8,128)}, u32[]{:S(2)}) copy-start(f32[512,1024]{1,0:T(8,128)} %get-tuple-element.48) | copy-start | bytes 6291460
  400.4 3.0 copy-start
  400.4 3.0 copy-start.2
  403.4 1.6 copy-start.3
  405.0 1.0 copy-start.5
  405.0 1.7 copy-start.4

commit v4 on v3

--- a/solution.py
+++ b/solution.py
@@ -57,6 +57,10 @@
     return (lane >= head * HEAD) & (lane < (head + 1) * HEAD)
 
 
+def early_chunks(ctx):
+    return max(ctx // 2, 1)
+
+
 class Plan:
     def __init__(self, fsdp, ctx):
         self.fsdp, self.ctx = fsdp, ctx
@@ -64,6 +68,7 @@
         self.across = math.isqrt(self.lines)
         self.along = self.lines // self.across
         self.half = ctx // 2
+        self.early = early_chunks(ctx)
         self.f = lax.axis_index("fsdp")
         self.c = lax.axis_index("ctx")
         self.core = lax.rem(self.f, 2)
@@ -268,13 +273,15 @@
 
 def forward_kernel(
     fsdp, ctx,
-    x, vf, w_q, w_k, w_v, w_o, w_g, w_u, w_d, small,
+    x, vf, m_q, m_k, m_v, m_o, m_g, m_u, m_d, small,
     attended, wos, gus, wds, x_out_ref, q_ref, k_ref, vm_ref, kt_ref, att_ref, wq_ref,
     lse, table, start, gain,
     xs, vs, wq, wqh, own_q, own_o, own_g, own_d, gs, q, k, vm, kt, vt, att, out, acc, mx, tot,
     x_sem, x_out, v_sem, v_out, q_sem, q_out, h_sem, g_sem, g_out,
     w_sem, w_z, w_p, w_s, o_sem, o_out, save_sem,
+    w_q, w_k, w_v, w_o, w_g, w_u, w_d, m_sem,
 ):
+    masters = (m_q, m_k, m_v, m_o, m_g, m_u, m_d)
     plan = Plan(fsdp, ctx)
     f, c, core, line, home, half = plan.f, plan.c, plan.core, plan.line, plan.home, plan.half
     tokens, depth = x.shape
@@ -287,9 +294,11 @@
     away = jnp.logical_not(owner)
     sibling = (line * 2 + 1 - core, c)
 
-    own_o[...] = w_o[...].astype(BF16)
-    own_g[...] = jnp.concatenate([w_g[...].astype(BF16), w_u[...].astype(BF16)], axis=1)
-    own_d[...] = w_d[...].astype(BF16)
+    fetched = (w_q, w_k, w_v, w_o, w_g, w_u, w_d)
+    for i, (src, dst) in enumerate(zip(masters, fetched)):
+        plan.keep(src, dst, m_sem.at[i])
+    for i in range(3):
+        plan.arrive(fetched[i], m_sem.at[i])
     own_q[...] = jnp.concatenate(
         [w_q[...].astype(BF16), w_k[...].astype(BF16), w_v[...].astype(BF16)], axis=1
     )
@@ -347,7 +356,11 @@
                 jnp.logical_not(mine),
             )
             plan.keep(src, vs.at[c], v_sem.at[c], mine)
-    gathering.start_plane()
+    for i in range(3, 7):
+        plan.arrive(fetched[i], m_sem.at[i])
+    own_o[...] = w_o[...].astype(BF16)
+    own_g[...] = jnp.concatenate([w_g[...].astype(BF16), w_u[...].astype(BF16)], axis=1)
+    own_d[...] = w_d[...].astype(BF16)
 
     for row in range(fsdp):
         plan.arrive(gs.at[row], g_sem.at[row])
@@ -391,6 +404,7 @@
             jnp.logical_not(f == at * 2 + 1),
         )
     plan.keep(wqh, wq.at[f], q_sem.at[f], core == 1)
+    gathering.start_plane()
 
     def project(j):
         def body(i, carry):
@@ -490,10 +504,10 @@
         first = start[0:1, rows]
 
         def keys(kb, inner):
-            krows = pl.ds(pl.multiple_of(kb * BLOCK, BLOCK), BLOCK)
+            krows = pl.ds(pl.multiple_of(kb * KEYS, KEYS), KEYS)
             kv = k[krows, :]
-            key_pos = kb * BLOCK + lax.broadcasted_iota(jnp.int32, (BLOCK, BLOCK), 0)
-            query_pos = b * BLOCK + lax.broadcasted_iota(jnp.int32, (BLOCK, BLOCK), 1)
+            key_pos = kb * KEYS + lax.broadcasted_iota(jnp.int32, (KEYS, BLOCK), 0)
+            query_pos = b * BLOCK + lax.broadcasted_iota(jnp.int32, (KEYS, BLOCK), 1)
             allowed = (key_pos <= query_pos) & (key_pos >= first)
             for head in range(heads):
                 band = slice(head * HEAD, (head + 1) * HEAD)
@@ -510,7 +524,7 @@
                 acc[band, :] = acc[band, :] * shrink + nn(vt[band, krows], p.astype(BF16))
             return inner
 
-        lax.fori_loop(0, b + 1, keys, 0)
+        lax.fori_loop(0, b // (KEYS // BLOCK) + 1, keys, 0)
         for head in range(heads):
             band = slice(head * HEAD, (head + 1) * HEAD)
             acc[band, :] = acc[band, :] / tot[head : head + 1, :]
@@ -557,10 +571,11 @@
 PIECES = 4
 START = ('x', 0)
 SHORTS_AND_LONG = 4
+KEYS = 512
 SPOTS = {
-    "from_ctx": (None, ('x', 2), ('x', 3), 'q'),
-    "from_plane": (('x', 2), ('x', 3), 'p', ('t', 2)),
-    "from_far": (('t', 0), ('t', 2), ('t', 4), 'late'),
+    "from_ctx": (None, ('x', 2), ('x', 3), ('t', 0)),
+    "from_plane": (('x', 2), ('x', 3), ('t', 0), ('t', 3)),
+    "from_far": (('t', 0), ('t', 2), ('t', 5), 'late'),
 }
 
 
@@ -617,7 +632,7 @@
             array(jnp.int32, 1, group),
             array(F32, 8, depth),
         ),
-        in_specs=[anywhere] * 2 + [vmem] * 8,
+        in_specs=[anywhere] * 9 + [vmem],
         out_specs=[anywhere] * 11 + [vmem] * 4,
         scratch_shapes=[
             low(ctx, tokens, depth), low(ctx, tokens, cols), low(fsdp, shard, 3 * cols),
@@ -630,7 +645,9 @@
             dma((fsdp,)), dma((2, lines)), dma((2,)), dma((fsdp,)), dma((fsdp,)),
             dma((3, fsdp, ctx)), dma((3, 2, ctx)), dma((3, peers, lines, ctx)), dma((3, lines, ctx)),
             dma((ctx, per)), dma((blocks,)), dma((7,)),
-        ],
+        ]
+        + [full(*weight.shape) for weight in weights]
+        + [dma((7,))],
         compiler_params=pltpu.CompilerParams(
             collective_id=0, has_side_effects=True, vmem_limit_bytes=VMEM_LIMIT
         ),
@@ -672,7 +689,7 @@
     row_lines = my_wd.shape[1]
     row_count = my_wd.shape[3]
     slot = lax.rem(step, 2)
-    half, side = plan.half, plan.across
+    side = plan.across
 
     def give(at):
         place = lax.rem(at, 2)
@@ -776,15 +793,15 @@
         for i in range(lines):
             plan.arrive(got_gu.at[at, i], gu_sem.at[at, i])
 
-            @pl.when(at >= half)
+            @pl.when(at >= plan.early)
             def _(i=i):
                 add_rows(s_gu.at[0, i], [my_gu.at[place, i, core], got_gu.at[at, i]])
 
-            @pl.when(at < half)
+            @pl.when(at < plan.early)
             def _(i=i):
                 add_rows(got_gu.at[at, i], [my_gu.at[place, i, core], got_gu.at[at, i]])
 
-        for early_at in range(half):
+        for early_at in range(plan.early):
 
             @pl.when(at == early_at)
             def _(early_at=early_at):
@@ -844,7 +861,7 @@
             add_rows(s_wo.at[i], [my_wo.at[i, core], got_wo.at[i]])
         for at in (last - 2, last - 1):
             given(at)
-        for at in range(half):
+        for at in range(plan.early):
             low, first, _ = reduce_places(plan, chunk_order(at, ctx))
             for inner in range(side):
                 for hop in range(1, side):
@@ -855,7 +872,7 @@
                     + [near_gu.at[at, hop - 1, inner] for hop in range(1, side)],
                 )
         plan.draining = True
-        for at in range(half):
+        for at in range(plan.early):
             over_plane(at)
         for i in range(lines):
             plan.send(my_wo.at[i, 1 - core], got_wo.at[i], wo_out.at[i], wo_sem.at[i], sibling)
@@ -871,8 +888,8 @@
     shard = depth // fsdp
     row_count = wd.shape[0] // fsdp
     row_lines = fsdp // ctx // 2
-    half = ctx // 2
     side = math.isqrt(lines)
+    early = early_chunks(ctx)
     hops = max(side - 1, 1)
     once = pl.Buffered(1)
 
@@ -894,9 +911,9 @@
         jax.ShapeDtypeStruct((tokens, depth), BF16),
         jax.ShapeDtypeStruct((8, depth), F32),
         jax.ShapeDtypeStruct((lines, shard, depth), BF16),
-        jax.ShapeDtypeStruct((ctx - half, lines, shard, width), BF16),
+        jax.ShapeDtypeStruct((ctx - early, lines, shard, width), BF16),
         jax.ShapeDtypeStruct((lines, row_count, depth), BF16),
-        jax.ShapeDtypeStruct((half, side, shard, width), BF16),
+        jax.ShapeDtypeStruct((early, side, shard, width), BF16),
     )
     dma = pltpu.SemaphoreType.DMA
     return pl.pallas_call(
@@ -919,10 +936,10 @@
             whole_out((8, depth)),
             whole_out((lines, shard, depth)),
             pl.BlockSpec(
-                (1, lines, shard, width), lambda i: (jnp.maximum(i - 1 - half, 0), 0, 0, 0)
+                (1, lines, shard, width), lambda i: (jnp.maximum(i - 1 - early, 0), 0, 0, 0)
             ),
             pl.BlockSpec((row_lines, row_count, depth), lambda i: (chunk_before(i), 0, 0)),
-            whole_out((half, side, shard, width)),
+            whole_out((early, side, shard, width)),
         ],
         scratch_shapes=[
             pltpu.VMEM((tokens, depth), F32),
@@ -937,9 +954,9 @@
             pltpu.VMEM((steps, lines, shard, width), BF16),
             pltpu.VMEM((steps, row_lines, row_count, depth), BF16),
             pltpu.VMEM((lines, shard, depth), BF16),
-            pltpu.VMEM((half, hops, side, shard, width), BF16),
+            pltpu.VMEM((early, hops, side, shard, width), BF16),
             dma((steps, lines)), dma((2, lines)), dma((steps, row_lines)), dma((2, row_lines)),
-            dma((lines,)), dma((lines,)), dma((half, hops, side)), dma((half, hops, side)),
+            dma((lines,)), dma((lines,)), dma((early, hops, side)), dma((early, hops, side)),
         ],
         compiler_params=pltpu.CompilerParams(
             vmem_limit_bytes=VMEM_LIMIT, dimension_semantics=("arbitrary",), collective_id=4,
@@ -979,16 +996,16 @@
             self.last_sem, self.last_out,
         ) = sems
         self.side = plan.across
-        half, ctx = plan.half, plan.ctx
+        ctx = plan.ctx
         self.chunks = [chunk_order(i, ctx) for i in range(ctx)]
-        self.first_set = [(1, j) for j in self.chunks[:half]]
-        self.second_set = [(1, j) for j in self.chunks[half:]]
+        self.first_set = [(1, j) for j in self.chunks[: plan.early]]
+        self.second_set = [(1, j) for j in self.chunks[plan.early :]]
         self.third_set = [(i, j) for i in (0, 2) for j in self.chunks]
 
     def piece(self, i, line, j):
         src = self.sources[i]
         if i == 1:
-            return src.at[self.chunks.index(j) - self.plan.half, line]
+            return src.at[self.chunks.index(j) - self.plan.early, line]
         width = src.shape[2] // self.plan.ctx
         return src.at[line, :, pl.ds(j * width, width)]
 
@@ -1336,6 +1353,7 @@
         plan.keep(src, dst, v_sem.at[rank], mine)
 
     schedule = {}
+    schedule_first = []
     schedule_last = []
 
     def at_step(t, act):
@@ -1344,6 +1362,9 @@
     scale = blocks // 8
     for kind, which, place in REDUCE_STEPS:
         pairs_of = getattr(reduction, which)
+        if place < 0:
+            schedule_first.append(functools.partial(getattr(reduction, kind), pairs_of))
+            continue
         if kind != "step_pass":
             at_step(place * scale, functools.partial(getattr(reduction, kind), pairs_of))
             continue
@@ -1381,6 +1402,8 @@
 
         return carry
 
+    for act in schedule_first:
+        act()
     kept = plan.started
     plan.started = []
     lax.fori_loop(0, blocks, step, 0)

time: 410 us -> 398 us (0.971)
  Pallas kernels: 387 us -> 374 us
    pallas_call x1, Pallas kernels: 166 us -> 155 us  [forward(): pl.pallas_call(functools.partial(forward_kernel, fsdp, ctx), out_shape=(a...]
where the time goes in v4:
time: 398 us; the launch traced here: 395 us
  Pallas kernels  374 us (94%)
  local copies, waits for them, and re-layouts  14.1 us (4%)
  other arithmetic  5.96 us (1%)
    pallas_call x1, Pallas kernels, backward(): pl.pallas_call(functools.partial(backward_kernel, fsdp, ctx), out_shape=(...  158 us
    pallas_call x1, Pallas kernels, forward(): pl.pallas_call(functools.partial(forward_kernel, fsdp, ctx), out_shape=(a...  155 us
    pallas_call x1, Pallas kernels, feed_forward(): pl.pallas_call(functools.partial(feed_kernel, fsdp, ctx), grid=(steps + 1...  61.4 us
    unnamed x21, local copies, waits for them, and re-layouts  8.03 us

profile of v4, /device:TPU:0, one launch (start us, length us, event | category | flops | bytes accessed | tf_op | source)
XLA Modules:
  0.0 394.9 jit_solution(13049361332060435224)
XLA Ops:
  0.6 0.7 convert_element_type.14
  1.3 0.7 convert_bitcast_fusion
  2.0 0.2 dynamic_update_slice.7.small
  2.2 0.0 copy-start.6
  2.3 1.9 copy.26.m_g
  4.2 1.9 copy.27.m_u
  6.1 0.0 copy-done.6
  6.1 154.8 %forward.1 = (bf16[512,1024]{1,0:T(8,128)(2,1)}, bf16[8,128,1024]{2,1,0:T(8,128)(2,1)}, bf16[4,8,128,1408]{3,2,1,0:T(8,128)(2,1)}, bf16[8,352,1024]{2,1,0:T(8,12...) custom-call(bf16[512,1024]{1,0:T(8,128)(2,1)} %x.3, ...), custom_call_target="tpu_custom_call" | custom-call | tf_op jit(solution)/shard_map/forward/pallas_call | solution.py:616
  160.9 1.4 fusion.2
  162.3 61.4 %feed_forward.1 = (bf16[512,1024]{1,0:T(8,128)(2,1)}, f32[512,1024]{1,0:T(8,128)}, bf16[512,1024]{1,0:T(8,128)(2,1)}, f32[8,1024]{1,0:T(8,128)}, bf16[4,128,1024...) custom-call(bf16[512,1024]{1,0:T(8,128)(2,1)} %get-tuple-element.42., ...), custom_call_target="tpu_custom_call" | custom-call | tf_op jit(solution)/shard_map/feed_forward/pallas_call | solution.py:919
  223.7 157.9 %backward.1 = (bf16[512,1024]{1,0:T(8,128)(2,1)}, bf16[512,1024]{1,0:T(8,128)(2,1)}, f32[128,256]{1,0:T(8,128)}, f32[128,1408]{1,0:T(8,128)}, f32[352,256]{1,0:T...) custom-call(bf16[512,1024]{1,0:T(8,128)(2,1)} %get-tuple-element.49.d_out, bf16[8,256,1024]{2,1,0:T(8,128)(2,1)} %bitcast.15, ...), custom_call_target="tpu_custom_call" | custom-call | tf_op jit(solution)/shard_map/backward/pallas_call | solution.py:1540
  381.6 0.0 copy-start.1
  381.6 0.8 constant_dynamic-slice_fusion
  382.5 0.5 slice_bitcast_fusion
  383.0 1.8 fusion.1
  384.8 1.3 fusion
  386.0 0.9 copy.29
  386.9 0.9 copy.28
  387.8 0.0 copy-done.1
  387.8 0.0 copy-start
  387.9 0.0 copy-start.2
  387.9 3.0 convert_add_fusion.1
  390.8 0.0 copy-done
  390.8 0.0 copy-done.2
  390.8 0.0 copy-start.3
  390.8 1.6 convert_add_fusion
  392.5 0.0 copy-done.3
  392.5 0.0 copy-start.5
  392.5 0.0 copy-start.4
  392.5 1.0 copy.35
  393.5 0.0 copy-done.5
  393.5 0.7 copy.36
  394.1 0.0 copy-done.4
  394.1 0.7 copy.37
  (2 shorter events, 0.0 us)
Async XLA Ops:
  2.2 3.8 copy-start.6
  381.6 6.2 %copy-start.1 = (f32[512,1024]{1,0:T(8,128)S(1)}, f32[512,1024]{1,0:T(8,128)}, u32[]{:S(2)}) copy-start(f32[512,1024]{1,0:T(8,128)} %get-tuple-element.48) | copy-start | bytes 6291460
  387.8 3.0 copy-start
  387.9 3.0 copy-start.2
  390.8 1.6 copy-start.3
  392.5 1.0 copy-start.5
  392.5 1.7 copy-start.4

commit v5 on v4

--- a/solution.py
+++ b/solution.py
@@ -1414,7 +1414,6 @@
         plan.send(dg, dg_near.at[f], dn_out.at[hop - 1], dn_sem.at[f], dev)
     plan.keep(dg, dg_near.at[f], dn_sem.at[f])
 
-    pass_pair(pairs - 2, True)
     sum_pair(pairs - 1)
     pass_pair(pairs - 1, False)
     shard = depth // fsdp
@@ -1436,6 +1435,7 @@
                 gw_near.at[hop - 1, :, :, pl.ds(i * cols, cols)],
                 gw_out.at[i, hop - 1], gw_sem.at[i, hop - 1], (to * 2 + core, c),
             )
+    pass_pair(pairs - 2, True)
     pass_pair(pairs - 1, True)
 
     for at in range(fsdp):

time: 398 us -> 394 us (0.990)
  no operation moved by 1% of the time
where the time goes in v5:
time: 394 us; the launch traced here: 393 us
  Pallas kernels  373 us (95%)
  local copies, waits for them, and re-layouts  14.1 us (4%)
  other arithmetic  5.96 us (2%)
    pallas_call x1, Pallas kernels, backward(): pl.pallas_call(functools.partial(backward_kernel, fsdp, ctx), out_shape=(...  156 us
    pallas_call x1, Pallas kernels, forward(): pl.pallas_call(functools.partial(forward_kernel, fsdp, ctx), out_shape=(a...  155 us
    pallas_call x1, Pallas kernels, feed_forward(): pl.pallas_call(functools.partial(feed_kernel, fsdp, ctx), grid=(steps + 1...  61.4 us
    unnamed x21, local copies, waits for them, and re-layouts  8.03 us

profile of v5, /device:TPU:0, one launch (start us, length us, event | category | flops | bytes accessed | tf_op | source)
XLA Modules:
  0.0 393.4 jit_solution(7392105381540495788)
XLA Ops:
  0.6 0.7 convert_element_type.14
  1.3 0.7 convert_bitcast_fusion
  2.0 0.2 dynamic_update_slice.7.small
  2.2 0.0 copy-start.6
  2.3 1.9 copy.26.m_g
  4.2 1.9 copy.27.m_u
  6.1 0.0 copy-done.6
  6.1 154.8 %forward.1 = (bf16[512,1024]{1,0:T(8,128)(2,1)}, bf16[8,128,1024]{2,1,0:T(8,128)(2,1)}, bf16[4,8,128,1408]{3,2,1,0:T(8,128)(2,1)}, bf16[8,352,1024]{2,1,0:T(8,12...) custom-call(bf16[512,1024]{1,0:T(8,128)(2,1)} %x.3, ...), custom_call_target="tpu_custom_call" | custom-call | tf_op jit(solution)/shard_map/forward/pallas_call | solution.py:616
  160.9 1.4 fusion.2
  162.3 61.4 %feed_forward.1 = (bf16[512,1024]{1,0:T(8,128)(2,1)}, f32[512,1024]{1,0:T(8,128)}, bf16[512,1024]{1,0:T(8,128)(2,1)}, f32[8,1024]{1,0:T(8,128)}, bf16[4,128,1024...) custom-call(bf16[512,1024]{1,0:T(8,128)(2,1)} %get-tuple-element.42., ...), custom_call_target="tpu_custom_call" | custom-call | tf_op jit(solution)/shard_map/feed_forward/pallas_call | solution.py:919
  223.7 156.4 %backward.1 = (bf16[512,1024]{1,0:T(8,128)(2,1)}, bf16[512,1024]{1,0:T(8,128)(2,1)}, f32[128,256]{1,0:T(8,128)}, f32[128,1408]{1,0:T(8,128)}, f32[352,256]{1,0:T...) custom-call(bf16[512,1024]{1,0:T(8,128)(2,1)} %get-tuple-element.49.d_out, bf16[8,256,1024]{2,1,0:T(8,128)(2,1)} %bitcast.15, ...), custom_call_target="tpu_custom_call" | custom-call | tf_op jit(solution)/shard_map/backward/pallas_call | solution.py:1540
  380.1 0.0 copy-start.1
  380.2 0.8 constant_dynamic-slice_fusion
  381.0 0.5 slice_bitcast_fusion
  381.5 1.8 fusion.1
  383.3 1.3 fusion
  384.6 0.9 copy.29
  385.5 0.9 copy.28
  386.4 0.0 copy-done.1
  386.4 0.0 copy-start
  386.4 0.0 copy-start.2
  386.4 3.0 convert_add_fusion.1
  389.4 0.0 copy-done
  389.4 0.0 copy-done.2
  389.4 0.0 copy-start.3
  389.4 1.6 convert_add_fusion
  391.0 0.0 copy-done.3
  391.0 0.0 copy-start.5
  391.0 0.0 copy-start.4
  391.0 1.0 copy.35
  392.0 0.0 copy-done.5
  392.0 0.7 copy.36
  392.7 0.0 copy-done.4
  392.7 0.7 copy.37
  (2 shorter events, 0.0 us)
Async XLA Ops:
  2.2 3.8 copy-start.6
  380.1 6.2 %copy-start.1 = (f32[512,1024]{1,0:T(8,128)S(1)}, f32[512,1024]{1,0:T(8,128)}, u32[]{:S(2)}) copy-start(f32[512,1024]{1,0:T(8,128)} %get-tuple-element.48) | copy-start | bytes 6291460
  386.4 3.0 copy-start
  386.4 3.0 copy-start.2
  389.4 1.6 copy-start.3
  391.0 1.0 copy-start.5
  391.0 1.7 copy-start.4
